TPU v7x, 128 devices: a whole 4x4x4 slice. The times are simulated.
128 devices in a mesh: row: 32 (over z, y_hi, x), ch: 4 (over y_lo, core).
Axes of the slice: x: 4, y: 4 (y_hi: 2, y_lo: 2; y = y_hi * 2 + y_lo), z: 4, core: 2. Of those that a mesh axis runs over, the one named last changes fastest.
Arguments:
- features: bfloat16 [4, 64, 384, 128], P(None, 'row', 'ch'), may hold values from -4 to 4
- gain_in: bfloat16 [384], P('ch'), may hold values from 0.25 to 1.75
- w_conv: bfloat16 [27, 384, 384], P(None, 'ch'), may hold values from -0.0625 to 0.0625
- gain_attn: bfloat16 [384], P('ch'), may hold values from 0.25 to 1.75
- w_qkv: bfloat16 [384, 1152], replicated, may hold values from -8 to 8
- w_out: bfloat16 [384, 384], replicated, may hold values from -0.4375 to 0.4375
- cotangent: bfloat16 [4, 64, 384, 128], P(None, 'row', 'ch'), may hold values from -4 to 4
Outputs:
- grad_features: bfloat16 [4, 64, 384, 128], P(None, 'row', 'ch')
- grad_weights: float32 [27, 384, 384], P(None, 'ch')
All inputs are finite; a program needn't handle non-finite values.
Results may differ from a plain program's by a relative error of at most 0.015.
Values may be sent and summed in bfloat16 or wider, within the bound.
A program may use at most 192 MiB of HBM per device.

v0:
```python
import math

import jax
import jax.numpy as jnp
from jax import lax
from jax.sharding import PartitionSpec as P

EPSILON = 1e-06


def padded_2(block, sides, width):
    for axis, dim in sides:
        count = lax.axis_size(axis)
        forward = [(i, i + 1) for i in range(count - 1)]
        backward = [(target, source) for source, target in forward]
        low = lax.ppermute(
            lax.slice_in_dim(block, block.shape[dim] - width, None, axis=dim), axis, forward
        )
        high = lax.ppermute(lax.slice_in_dim(block, 0, width, axis=dim), axis, backward)
        block = jnp.concatenate([low, block, high], axis=dim)
    return block


def silu_slope(before):
    sig_value = jax.nn.sigmoid(before)
    return sig_value * (1.0 + before * (1.0 - sig_value))


def channel_total(values):
    return lax.psum(values, "ch")


def rim_rows(values):
    return padded_2(values, (("row", 1),), 1)


def tap_slab(padded, t_off, h_off, frames, row_count, col_count):
    return jnp.concatenate(
        [
            padded[t_off : t_off + frames, h_off : h_off + row_count, :, w_off : w_off + col_count]
            for w_off in range(3)
        ],
        axis=2,
    )


def conv_forward(padded, weights, frames, row_count, col_count):
    running = jnp.zeros((frames, row_count, weights.shape[1], col_count), jnp.float32)
    for t_off in range(3):
        for h_off in range(3):
            slab = tap_slab(padded, t_off, h_off, frames, row_count, col_count)
            kernel = jnp.concatenate(
                [weights[9 * t_off + 3 * h_off + w_off] for w_off in range(3)], axis=1
            )
            running = running + jnp.einsum(
                "ok,fhkw->fhow", kernel, slab, preferred_element_type=jnp.float32
            )
    return running


def conv_input_grad(padded, weights, frames, row_count, col_count):
    running = jnp.zeros((frames, row_count, weights.shape[2], col_count), jnp.float32)
    for t_off in range(3):
        for h_off in range(3):
            slab = tap_slab(padded, t_off, h_off, frames, row_count, col_count)
            kernel = jnp.concatenate(
                [weights[9 * (2 - t_off) + 3 * (2 - h_off) + (2 - w_off)].T for w_off in range(3)],
                axis=1,
            )
            running = running + jnp.einsum(
                "ik,fhkw->fhiw", kernel, slab, preferred_element_type=jnp.float32
            )
    return running


def conv_weight_grad(padded, grad_out, frames, row_count, col_count):
    pieces = []
    for t_off in range(3):
        for h_off in range(3):
            slab = tap_slab(padded, t_off, h_off, frames, row_count, col_count)
            block = jnp.einsum("fhow,fhkw->ok", grad_out, slab, preferred_element_type=jnp.float32)
            pieces.append(block.reshape(block.shape[0], 3, -1).transpose(1, 0, 2))
    return jnp.concatenate(pieces, axis=0)


def on_device(features, gain_in, w_conv, gain_attn, w_qkv, w_out, cotangent):
    frames, row_count, part_ch, col_count = features.shape
    channels = part_ch * lax.axis_size("ch")
    feat_f32 = features.astype(jnp.float32)
    gain_in_col = gain_in.astype(jnp.float32)[:, None]
    gain_attn_col = gain_attn.astype(jnp.float32)[:, None]
    inv_in = lax.rsqrt(
        channel_total(jnp.sum(feat_f32 * feat_f32, 2, keepdims=True)) / channels + EPSILON
    )
    before = feat_f32 * inv_in * gain_in_col
    activated = jax.nn.silu(before).astype(jnp.bfloat16)
    full_act = rim_rows(lax.all_gather(activated, "ch", axis=2, tiled=True))
    padded_act = jnp.pad(full_act, ((2, 0), (0, 0), (0, 0), (1, 1)))
    conv_out = conv_forward(padded_act, w_conv, frames, row_count, col_count)
    residual = (feat_f32 + conv_out).astype(jnp.bfloat16)
    res_f32 = lax.optimization_barrier(residual).astype(jnp.float32)
    inv_attn = lax.rsqrt(
        channel_total(jnp.sum(res_f32 * res_f32, 2, keepdims=True)) / channels + EPSILON
    )
    normed = (res_f32 * inv_attn * gain_attn_col).astype(jnp.bfloat16)
    normed_frame, grad_frame = (
        lax.all_to_all(normed, "ch", split_axis=0, concat_axis=2, tiled=True),
        lax.all_to_all(cotangent, "ch", split_axis=0, concat_axis=2, tiled=True),
    )
    own_frames = normed_frame.shape[0]
    normed_tok = normed_frame.transpose(0, 1, 3, 2)
    cot_tok = grad_frame.transpose(0, 1, 3, 2)
    projected = jnp.dot(normed_tok, w_qkv, preferred_element_type=jnp.float32).astype(jnp.bfloat16)
    queries = projected[..., :channels]
    keys_own = projected[..., channels : 2 * channels]
    values_own = projected[..., 2 * channels :]
    grad_o = jnp.dot(cot_tok, w_out.T, preferred_element_type=jnp.float32).astype(jnp.bfloat16)
    keys_all, values_all = (
        lax.all_gather(keys_own, "row", axis=1, tiled=True),
        lax.all_gather(values_own, "row", axis=1, tiled=True),
    )
    score_scale = 1.0 / math.sqrt(channels)
    q_flat = queries.reshape(own_frames, -1, channels)
    k_flat = keys_all.reshape(own_frames, -1, channels)
    v_flat = values_all.reshape(own_frames, -1, channels)
    g_flat = grad_o.reshape(own_frames, -1, channels)
    scores = (
        jnp.einsum("fqc,fkc->fqk", q_flat, k_flat, preferred_element_type=jnp.float32) * score_scale
    )
    row_max = jnp.max(scores, -1, keepdims=True)
    exp_scores = jnp.exp(scores - row_max)
    totals = jnp.sum(exp_scores, -1, keepdims=True)
    prob_f32 = exp_scores / totals
    prob_bf16 = prob_f32.astype(jnp.bfloat16)
    attended = jnp.einsum(
        "fqk,fkc->fqc", prob_bf16, v_flat, preferred_element_type=jnp.float32
    ).astype(jnp.bfloat16)
    row_delta = jnp.sum(
        g_flat.astype(jnp.float32) * lax.optimization_barrier(attended).astype(jnp.float32),
        -1,
        keepdims=True,
    )
    grad_p = jnp.einsum("fqc,fkc->fqk", g_flat, v_flat, preferred_element_type=jnp.float32)
    grad_s = (prob_f32 * (grad_p - row_delta) * score_scale).astype(jnp.bfloat16)
    grad_q = jnp.einsum("fqk,fkc->fqc", grad_s, k_flat, preferred_element_type=jnp.float32).astype(
        jnp.bfloat16
    )
    cell_shape = (own_frames, row_count, col_count, channels)
    key_term = jnp.concatenate(
        [
            jnp.einsum("fqk,fqc->fkc", grad_s, q_flat, preferred_element_type=jnp.float32),
            jnp.einsum("fqk,fqc->fkc", prob_bf16, g_flat, preferred_element_type=jnp.float32),
        ],
        -1,
    )
    summed = lax.psum_scatter(
        key_term.reshape(own_frames, -1, col_count, 2 * channels),
        "row",
        scatter_dimension=1,
        tiled=True,
    )
    grad_k = summed[..., :channels]
    grad_v = summed[..., channels:]
    grad_qkv = jnp.concatenate(
        [grad_q.reshape(cell_shape), grad_k.astype(jnp.bfloat16), grad_v.astype(jnp.bfloat16)], -1
    )
    grad_normed = (
        jnp.dot(grad_qkv, w_qkv.T, preferred_element_type=jnp.float32)
        .astype(jnp.bfloat16)
        .transpose(0, 1, 3, 2)
    )
    grad_norm_ch = lax.all_to_all(grad_normed, "ch", split_axis=2, concat_axis=0, tiled=True)
    scaled = grad_norm_ch.astype(jnp.float32) * gain_attn_col
    inner = channel_total(jnp.sum(res_f32 * scaled, 2, keepdims=True)) / channels
    grad_res = (
        cotangent.astype(jnp.float32)
        + inv_attn * scaled
        - res_f32 * inv_attn * inv_attn * inv_attn * inner
    )
    grad_conv_out = grad_res.astype(jnp.bfloat16)
    padded_grad = jnp.pad(rim_rows(grad_conv_out), ((0, 2), (0, 0), (0, 0), (1, 1)))
    partial_in = conv_input_grad(padded_grad, w_conv, frames, row_count, col_count)
    grad_act = lax.psum_scatter(partial_in, "ch", scatter_dimension=2, tiled=True)
    scaled_in = grad_act * silu_slope(before) * gain_in_col
    inner_in = channel_total(jnp.sum(feat_f32 * scaled_in, 2, keepdims=True)) / channels
    grad_features = grad_res + inv_in * scaled_in - feat_f32 * inv_in * inv_in * inv_in * inner_in
    weight_part = conv_weight_grad(padded_act, grad_conv_out, frames, row_count, col_count)
    cell_scale = 1.0 / math.sqrt(frames * row_count * lax.axis_size("row") * col_count)
    grad_weights = lax.psum(weight_part, "row") * cell_scale
    return (grad_features.astype(jnp.bfloat16), grad_weights)


def solution(mesh):
    return jax.shard_map(
        on_device,
        mesh=mesh,
        in_specs=(
            P(None, "row", "ch", None),
            P("ch"),
            P(None, "ch", None),
            P("ch"),
            P(),
            P(),
            P(None, "row", "ch", None),
        ),
        out_specs=(P(None, "row", "ch", None), P(None, "ch", None)),
        check_vma=False,
    )
```

profile of v0, /device:TPU:8, one launch (start us, length us, event | category | flops | bytes accessed | tf_op | source)
XLA Modules:
  0.0 1122.4 jit_solution(14515780004736910460)
XLA Ops:
  8.9 5.8 psum.35
  16.5 8.8 all_gather.9
  32.1 5.4 collective-permute-done
  47.6 5.1 fusion.253
  65.9 5.8 psum.36
  71.8 6.8 all_to_all.45
  80.9 8.2 all_to_all.46
  89.6 90.0 %all-gather.3.cloned.1.call-done = bf16[1,64,128,384]{3,2,0,1:T(8,128)(2,1)} async-done(((bf16[1,2,128,384]{3,2,0,1:T(8,128)(2,1)}), bf16[1,64,128,384]{3,2,0,1:T(8,128)(2,1)}) %all-gather.3.cloned.1.call-update) | async-done | bytes 6291472 | tf_op jit(solution)/shard_map/all_gather | solution.py:119
  179.5 5.2 fusion.259
  191.0 82.0 %all-gather.5.cloned.1.call-done = bf16[1,64,128,384]{3,2,0,1:T(8,128)(2,1)} async-done(((bf16[1,2,128,384]{3,2,0,1:T(8,128)(2,1)}), bf16[1,64,128,384]{3,2,0,1:T(8,128)(2,1)}) %all-gather.5.cloned.1.call-update) | async-done | bytes 6291472 | tf_op jit(solution)/shard_map/all_gather | solution.py:120
  273.0 7.6 fusion.45
  280.6 6.4 copy.106
  287.1 9.8 fusion.2
  296.9 6.5 copy.105
  303.5 4.7 convolution_bitcast_fusion.1
  310.5 8.7 pad_maximum_fusion
  319.3 6.4 convolution_convert_fusion.1
  325.7 295.0 %reduce-scatter.3.cloned.1.call-done = f32[1,2,128,768]{3,2,1,0:T(8,128)} async-done(((f32[1,64,128,768]{3,2,1,0:T(8,128)}), f32[1,2,128,768]{3,2,1,0:T(8,128)}) %reduce-scatter.3.cloned.1.call-update) | async-done | bytes 786448 | tf_op jit(solution)/shard_map/reduce_scatter | solution.py:156
  622.6 7.5 all_to_all.47
  630.3 6.7 psum.37
  699.1 37.4 %concatenate.189 = f32[27,96,384]{2,0,1:T(8,128)} concatenate(f32[3,96,384]{2,0,1:T(4,128)} %bitcast.399, f32[3,96,384]{2,0,1:T(4,128)} %bitcast.400, f32[3,96,384]{2,0,1:T(4,128)} %bitcast.401, f32[3,96,384]{2,0,1:T(4,128)} %bitcast.402, f32[3,96,384]{2,0,1:T(4,128)} %bitcast.403, f32[3,96,384]{2,0,1:T(4,128)} %bitcast.404, f32[3,96,384]{2,0,1:T(4,128)} %bitcast.398, ...), dimensions={0} | concatenate | bytes 7962624 | tf_op jit(solution)/shard_map/concatenate | solution.py:83
  738.5 5.7 psum.38
  746.3 362.2 %all-reduce.4.cloned.1.call-done = f32[27,96,384]{2,0,1:T(8,128)} async-done(((f32[27,96,384]{2,0,1:T(8,128)}), f32[27,96,384]{2,0,1:T(8,128)}) %all-reduce.4.cloned.1.call-update) | async-done | bytes 3981328 | tf_op jit(solution)/shard_map/psum | solution.py:189
  1111.4 4.2 copy.68
  (238 shorter events, 115.6 us)
Async XLA Ops:
  7.2 71.6 %copy-start = (bf16[384,1152]{1,0:T(8,128)(2,1)S(1)}, bf16[384,1152]{1,0:T(8,128)(2,1)}, u32[]{:S(2)}) copy-start(bf16[384,1152]{1,0:T(8,128)(2,1)} %param.11) | copy-start | bytes 2654212
  7.2 22.8 %copy-start.71 = (bf16[96]{0:T(256)(128)(2,1)S(1)}, bf16[96]{0:T(256)(128)(2,1)}, u32[]{:S(2)}) copy-start(bf16[96]{0:T(256)(128)(2,1)} %param.10) | copy-start | bytes 580
  7.2 172.3 %all-gather.3.cloned.1.call-start = ((), (), s32[]{:S(2)}) async-start(), calls=%async_computation.5 | async-start | bytes 6488064 | tf_op jit(solution)/shard_map/all_gather | solution.py:119
  8.0 6.8 copy-start.69
  14.7 15.3 %copy-start.3 = (bf16[27,96,384]{2,1,0:T(8,128)(2,1)S(1)}, bf16[27,96,384]{2,1,0:T(8,128)(2,1)}, u32[]{:S(2)}) copy-start(bf16[27,96,384]{2,1,0:T(8,128)(2,1)} %param.9) | copy-start | bytes 5971972
  25.3 12.3 %collective-permute-start = (bf16[4,1,384,128]{3,2,1,0:T(8,128)(2,1)S(1)}, bf16[4,1,384,128]{3,2,1,0:T(8,128)(2,1)S(1)}, u32[]{:S(2)}, u32[]{:S(2)}) collective-permute-start(bf16[4,1,384,128]{3,2,1,0:T(8,128)(2,1)S(1)} %get-tuple-element.108), channel_id=1, source_target_pairs={{0,4},{4,8},{8,12},{12,16},{16,20},{20,24},{24,28},{28,32},{32,36}... | collective-permute-start | bytes 1179656 | tf_op jit(solution)/shard_map/ppermute | solution.py:16
  28.7 13.0 %collective-permute-start.1 = (bf16[4,1,384,128]{3,2,1,0:T(8,128)(2,1)S(1)}, bf16[4,1,384,128]{3,2,1,0:T(8,128)(2,1)S(1)}, u32[]{:S(2)}, u32[]{:S(2)}) collective-permute-start(bf16[4,1,384,128]{3,2,1,0:T(8,128)(2,1)S(1)} %get-tuple-element.109), channel_id=1, source_target_pairs={{4,0},{8,4},{12,8},{16,12},{20,16},{24,20},{28,24},{32,28},{36,32}... | collective-permute-start | bytes 1179656 | tf_op jit(solution)/shard_map/ppermute | solution.py:19
  37.5 25.5 %copy-start.31 = (bf16[4,1,384,128]{3,2,1,0:T(8,128)(2,1)}, bf16[4,1,384,128]{3,2,1,0:T(8,128)(2,1)S(1)}, u32[]{:S(2)}) copy-start(bf16[4,1,384,128]{3,2,1,0:T(8,128)(2,1)S(1)} %collective-permute-done) | copy-start | bytes 1179652
  41.7 19.9 %copy-start.32 = (bf16[4,1,384,128]{3,2,1,0:T(8,128)(2,1)}, bf16[4,1,384,128]{3,2,1,0:T(8,128)(2,1)S(1)}, u32[]{:S(2)}) copy-start(bf16[4,1,384,128]{3,2,1,0:T(8,128)(2,1)S(1)} %collective-permute-done.1) | copy-start | bytes 1179652
  47.6 12.9 %copy-start.14 = (bf16[4,2,384,128]{3,2,1,0:T(8,128)(2,1)}, bf16[4,2,384,128]{3,2,1,0:T(8,128)(2,1)S(1)}, u32[]{:S(2)}) copy-start(bf16[4,2,384,128]{3,2,1,0:T(8,128)(2,1)S(1)} %get-tuple-element.26) | copy-start | bytes 2359300
  47.6 12.9 %copy-start.16 = (bf16[4,2,384,128]{3,2,1,0:T(8,128)(2,1)}, bf16[4,2,384,128]{3,2,1,0:T(8,128)(2,1)S(1)}, u32[]{:S(2)}) copy-start(bf16[4,2,384,128]{3,2,1,0:T(8,128)(2,1)S(1)} %get-tuple-element.27) | copy-start | bytes 2359300
  47.6 16.9 %copy-start.20 = (bf16[4,2,384,128]{3,2,1,0:T(8,128)(2,1)}, bf16[4,2,384,128]{3,2,1,0:T(8,128)(2,1)S(1)}, u32[]{:S(2)}) copy-start(bf16[4,2,384,128]{3,2,1,0:T(8,128)(2,1)S(1)} %get-tuple-element.25) | copy-start | bytes 2359300
  47.6 16.9 %copy-start.21 = (bf16[4,2,384,128]{3,2,1,0:T(8,128)(2,1)}, bf16[4,2,384,128]{3,2,1,0:T(8,128)(2,1)S(1)}, u32[]{:S(2)}) copy-start(bf16[4,2,384,128]{3,2,1,0:T(8,128)(2,1)S(1)} %get-tuple-element.28) | copy-start | bytes 2359300
  71.7 9.2 copy-start.6
  78.6 10.7 copy-start.34
  80.1 192.8 %all-gather.5.cloned.1.call-start = ((), (), s32[]{:S(2)}) async-start(), calls=%async_computation.6 | async-start | bytes 6488064 | tf_op jit(solution)/shard_map/all_gather | solution.py:120
  80.9 539.9 %reduce-scatter.3.cloned.1.call-start = ((), (), s32[]{:S(2)}) async-start(), calls=%async_computation.7 | async-start | bytes 25952256 | tf_op jit(solution)/shard_map/reduce_scatter | solution.py:156
  319.3 417.3 %reduce-scatter.5.cloned.1.call-start = ((), (), s32[]{:S(2)}) async-start(), calls=%async_computation.8 | async-start | bytes 1966080 | tf_op jit(solution)/shard_map/reduce_scatter | solution.py:183
  637.2 5.3 collective-permute-start.2
  639.4 6.5 collective-permute-start.3
  655.1 453.4 %all-reduce.4.cloned.1.call-start = ((), (), s32[]{:S(2)}) async-start(), calls=%async_computation.9 | async-start | bytes 9437184 | tf_op jit(solution)/shard_map/psum | solution.py:189
  669.8 5.3 copy-start.15
  683.5 5.3 copy-start.11
  693.9 5.3 copy-start.5
  (57 other events, 115.2 us)
Sparse Core Ops, SparseCore 0:
  80.2 99.2 all-gather.2
  183.1 89.8 all-gather.4
  319.4 301.3 reduce-scatter.2
  655.2 27.7 reduce-scatter.4
  736.7 371.7 all-reduce.3
where the time goes:
time: 1130 us; the launch traced here: 1120 us
  waiting for transfers between devices  843 us (75%)
  local copies, waits for them, and re-layouts  92.5 us (8%)
  matrix products  79.8 us (7%)
  blocking collectives  55.1 us (5%)
  other arithmetic  28.2 us (2%)
  between operations  15 us (1%)
    psum x1, waiting for transfers between devices, on_device(): grad_weights = lax.psum(weight_part, 'row') * cell_scale  362 us
    reduce_scatter x1, waiting for transfers between devices, on_device(): lax.psum_scatter(key_term.reshape(own_frames, -1, col_count, 2 * channels...  295 us
    all_gather x1, waiting for transfers between devices, on_device(): lax.all_gather(keys_own, 'row', axis=1, tiled=True)  90 us
    all_gather x1, waiting for transfers between devices, on_device(): lax.all_gather(values_own, 'row', axis=1, tiled=True)  82 us
    concatenate x1, local copies, waits for them, and re-layouts, conv_weight_grad(): return jnp.concatenate(pieces, axis=0)  37.4 us
    dot_general x9, matrix products, conv_weight_grad(): jnp.einsum('fhow,fhkw->ok', grad_out, slab, preferred_element_type=jnp.fl...  27.5 us
    psum x4, blocking collectives, channel_total(): return lax.psum(values, 'ch')  23.9 us
  transfers between devices with their start and end apart: 9, of which 7 were waited for; matrix products, arithmetic and copies ran while one was open for 9% of the time, Pallas kernels for 0%

commit v1 on v0

v1 whole, which is shorter than its diff:
```python
import functools
import math

import jax
import jax.numpy as jnp
from jax import lax
from jax.experimental import pallas as pl
from jax.experimental.pallas import tpu as pltpu
from jax.sharding import PartitionSpec as P

EPSILON = 1e-06
MESH = pl.DeviceIdType.MESH
F32 = jnp.float32
BF16 = jnp.bfloat16
ROWS = 32
CH = 4
VMEM_BYTES = 56 * 1024 * 1024


def coords():
    return lax.axis_index("row"), lax.axis_index("ch")


def exchange(cid, ins, outs, plan, count):
    def body(*refs):
        srcs, dsts = refs[: len(ins)], refs[len(ins) : len(ins) + len(outs)]
        send, recv, own = refs[len(ins) + len(outs) :]
        remote, local, peers = plan(srcs, dsts)
        barrier = pltpu.get_barrier_semaphore()
        for peer in peers:
            pl.semaphore_signal(barrier, inc=1, device_id=peer, device_id_type=MESH)
        here = [pltpu.make_async_copy(s, d, own.at[k]) for k, (s, d) in enumerate(local)]
        for copy in here:
            copy.start()
        pl.semaphore_wait(barrier, len(peers))
        there = [
            pltpu.make_async_remote_copy(
                src_ref=s,
                dst_ref=d,
                send_sem=send.at[k],
                recv_sem=recv.at[k],
                device_id=peer,
                device_id_type=MESH,
            )
            for k, (s, d, peer) in enumerate(remote)
        ]
        for copy in there:
            copy.start()
        for copy in here:
            copy.wait()
        for copy in there:
            copy.wait()

    return pl.pallas_call(
        body,
        out_shape=[jax.ShapeDtypeStruct(s, t) for s, t in outs],
        in_specs=[pl.BlockSpec(memory_space=pl.ANY)] * len(ins),
        out_specs=[pl.BlockSpec(memory_space=pl.ANY)] * len(outs),
        scratch_shapes=[
            pltpu.SemaphoreType.DMA((count[0],)),
            pltpu.SemaphoreType.DMA((count[0],)),
            pltpu.SemaphoreType.DMA((max(count[1], 1),)),
        ],
        compiler_params=pltpu.CompilerParams(collective_id=cid, has_side_effects=True),
        name="exchange_%d" % cid,
    )(*ins)


def compute(body, outs, *ins, scratch=(), name):
    return pl.pallas_call(
        body,
        out_shape=[jax.ShapeDtypeStruct(s, t) for s, t in outs],
        in_specs=[pl.BlockSpec(memory_space=pltpu.VMEM)] * len(ins),
        out_specs=[pl.BlockSpec(memory_space=pltpu.VMEM)] * len(outs),
        scratch_shapes=list(scratch),
        compiler_params=pltpu.CompilerParams(vmem_limit_bytes=VMEM_BYTES),
        name=name,
    )(*ins)


def dot(a, b):
    return lax.dot_general(a, b, (((1,), (0,)), ((), ())), preferred_element_type=F32)


def dot_t(a, b):
    return lax.dot_general(a, b, (((1,), (1,)), ((), ())), preferred_element_type=F32)


def move(block, by):
    lanes = block.shape[1]
    at = lax.broadcasted_iota(jnp.int32, block.shape, 1)
    if by > 0:
        return jnp.where(at == 0, 0.0, pltpu.roll(block, 1, axis=1))
    return jnp.where(at == lanes - 1, 0.0, pltpu.roll(block, lanes - 1, axis=1))


def ch_peers(r, c):
    return [(r, lax.rem(c + d, CH)) for d in range(1, CH)]


def near_rows(r):
    return lax.rem(r + ROWS - 1, ROWS), lax.rem(r + 1, ROWS)


def start_plan(srcs, dsts):
    feat, cot, gain = srcs
    all_feat, prev_feat, next_feat, cot_frame, all_gain = dsts
    r, c = coords()
    low, high = near_rows(r)
    remote, peers = [], []
    for row, c_to in ch_peers(r, c):
        remote.append((feat, all_feat.at[c], (row, c_to)))
        remote.append((cot.at[c_to], cot_frame.at[c], (row, c_to)))
        remote.append((gain, all_gain.at[c], (row, c_to)))
        peers.append((row, c_to))
    for d in range(CH):
        c_to = lax.rem(c + d, CH)
        remote.append((feat.at[:, 1], prev_feat.at[c], (high, c_to)))
        remote.append((feat.at[:, 0], next_feat.at[c], (low, c_to)))
        peers += [(high, c_to), (low, c_to)]
    local = [(feat, all_feat.at[c]), (cot.at[c], cot_frame.at[c]), (gain, all_gain.at[c])]
    return remote, local, peers


def frame_plan(srcs, dsts):
    (res,), (res_frame,) = srcs, dsts
    r, c = coords()
    peers = ch_peers(r, c)
    remote = [(res.at[to[1]], res_frame.at[c], to) for to in peers]
    return remote, [(res.at[c], res_frame.at[c])], peers


def key_peers(r, c):
    z, yx = r // 8, lax.rem(r, 8)
    return [(lax.rem(z + d, 4) * 8 + yx, c) for d in range(1, 4)]


def query_peers(r, c):
    z, y, x = r // 8, lax.rem(r // 4, 2), lax.rem(r, 4)
    found = []
    for dy in range(2):
        for dx in range(4):
            if dy or dx:
                found.append((z * 8 + lax.rem(y + dy, 2) * 4 + lax.rem(x + dx, 4), c))
    return found


def gather_plan(srcs, dsts):
    q, g, k, v = srcs
    all_q, all_g, all_k, all_v = dsts
    r, c = coords()
    z, yx = r // 8, lax.rem(r, 8)
    remote, peers = [], []
    for to in query_peers(r, c):
        remote += [(q, all_q.at[yx], to), (g, all_g.at[yx], to)]
        peers.append(to)
    for to in key_peers(r, c):
        remote += [(k, all_k.at[z], to), (v, all_v.at[z], to)]
        peers.append(to)
    local = [(q, all_q.at[yx]), (g, all_g.at[yx]), (k, all_k.at[z]), (v, all_v.at[z])]
    return remote, local, peers


def stats_plan(srcs, dsts):
    (own,), (every,) = srcs, dsts
    r, c = coords()
    yx = lax.rem(r, 8)
    peers = query_peers(r, c)
    return [(own, every.at[yx], to) for to in peers], [(own, every.at[yx])], peers


def back_plan(srcs, dsts):
    dq, dk, dv = srcs
    all_q, all_k, all_v = dsts
    r, c = coords()
    z, yx = r // 8, lax.rem(r, 8)
    remote, peers = [], []
    for to in query_peers(r, c):
        remote.append((dq.at[lax.rem(to[0], 8)], all_q.at[yx], to))
        peers.append(to)
    for to in key_peers(r, c):
        at = to[0] // 8
        remote += [(dk.at[at], all_k.at[z], to), (dv.at[at], all_v.at[z], to)]
        peers.append(to)
    local = [(dq.at[yx], all_q.at[yx]), (dk.at[z], all_k.at[z]), (dv.at[z], all_v.at[z])]
    return remote, local, peers


def grad_plan(srcs, dsts):
    (g,), (own, prev_g, next_g) = srcs, dsts
    r, c = coords()
    low, high = near_rows(r)
    remote, peers = [], []
    for to in ch_peers(r, c):
        remote.append((g.at[to[1]], own.at[c], to))
        peers.append(to)
    for d in range(CH):
        c_to = lax.rem(c + d, CH)
        remote.append((g.at[c_to, 1], prev_g.at[c], (high, c_to)))
        remote.append((g.at[c_to, 0], next_g.at[c], (low, c_to)))
        peers += [(high, c_to), (low, c_to)]
    return remote, [(g.at[c], own.at[c])], peers


def row_peers(r, c):
    return [(lax.rem(r + d, ROWS), c) for d in range(1, ROWS)]


def scatter_plan(srcs, dsts):
    weight, part, inner = srcs
    all_weight, all_part, all_inner = dsts
    r, c = coords()
    remote, peers = [], []
    for to in ch_peers(r, c):
        remote += [(part.at[to[1]], all_part.at[c], to), (inner, all_inner.at[c], to)]
        peers.append(to)
    for to in row_peers(r, c):
        remote.append((weight.at[to[0]], all_weight.at[r], to))
        peers.append(to)
    local = [
        (part.at[c], all_part.at[c]),
        (inner, all_inner.at[c]),
        (weight.at[r], all_weight.at[r]),
    ]
    return remote, local, peers


def spread_plan(srcs, dsts):
    (own,), (every,) = srcs, dsts
    r, c = coords()
    peers = row_peers(r, c)
    return [(own, every.at[r], to) for to in peers], [(own, every.at[r])], peers


def sigmoid(v):
    return 1.0 / (1.0 + jnp.exp(-v))


def conv_kernel(feat, all_feat, prev_feat, next_feat, gains, w, cot, w_out, res, act, inv_in, grad_o, full):
    r = lax.axis_index("row")
    gain = jnp.concatenate([gains[b, 0] for b in range(CH)], 0).astype(F32)
    for f in range(4):
        for h in range(4):
            blocks = [
                prev_feat[b, f] if h == 0 else next_feat[b, f] if h == 3 else all_feat[b, f, h - 1]
                for b in range(CH)
            ]
            x = jnp.concatenate(blocks, 0).astype(F32)
            inv = lax.rsqrt(jnp.mean(x * x, 0, keepdims=True) + EPSILON)
            before = x * inv * gain
            a = before * sigmoid(before)
            if h == 0:
                a = jnp.where(r == 0, 0.0, a)
            elif h == 3:
                a = jnp.where(r == ROWS - 1, 0.0, a)
            else:
                inv_in[2 * f + h - 1, :] = inv[0]
            act[:, pl.ds((4 * f + h) * 128, 128)] = a.astype(BF16)
    for f in range(4):
        acc = jnp.zeros((288, 256), F32)
        for t in range(3):
            source = f + t - 2
            if source < 0:
                continue
            for h in range(3):
                acc += dot(w[3 * t + h], act[:, pl.ds((4 * source + h) * 128, 256)])
        for h in range(2):
            y = acc[:, 128 * h : 128 * h + 128]
            out = move(y[:96], 1) + y[96:192] + move(y[192:], -1)
            res[f, h] = (feat[f, h].astype(F32) + out).astype(BF16)
    for b in range(CH):
        for h in range(2):
            full[pl.ds(96 * b, 96), pl.ds(128 * h, 128)] = cot[b, h]
    grad_o[...] = dot(w_out[...], full[...]).astype(BF16)


def attn_norm(res_frame, full):
    for b in range(CH):
        for h in range(2):
            full[pl.ds(96 * b, 96), pl.ds(128 * h, 128)] = res_frame[b, h]
    x = full[...].astype(F32)
    return x, lax.rsqrt(jnp.mean(x * x, 0, keepdims=True) + EPSILON)


def project_kernel(res_frame, gains, w_qkv, q, k, v, full):
    gain = jnp.concatenate([gains[b, 1] for b in range(CH)], 0).astype(F32)
    gain = jnp.concatenate([gain, gain], 1)
    x, inv = attn_norm(res_frame, full)
    normed = (x * inv * gain).astype(BF16).astype(F32)
    out = dot(normed.T.astype(BF16), w_qkv[...])
    q[...] = out[:, :384].T.astype(BF16)
    k[...] = out[:, 384:768].astype(BF16)
    v[...] = out[:, 768:].astype(BF16)


def stats_kernel(scale, q, g, k, v, stats):
    keys, values = k[...].reshape(1024, 384), v[...].reshape(1024, 384)

    def step(b, carry):
        s = dot(keys, q[b]) * scale
        m = jnp.max(s, 0, keepdims=True)
        e = jnp.exp(s - m)
        stats[b, 0:1, :] = m
        stats[b, 1:2, :] = jnp.sum(e, 0, keepdims=True)
        stats[b, 2:3, :] = jnp.sum(e * dot(values, g[b]), 0, keepdims=True)
        stats[b, 3:8, :] = jnp.zeros((5, 256), F32)
        return carry

    lax.fori_loop(0, 8, step, 0)


def attn_kernel(scale, q, g, k, v, stats, dq, dk, dv, acc_k, acc_v):
    keys, values = k[...].reshape(1024, 384), v[...].reshape(1024, 384)
    keys_t = keys.T
    acc_k[...] = jnp.zeros_like(acc_k)
    acc_v[...] = jnp.zeros_like(acc_v)

    def step(b, carry):
        part = [stats[i, b] for i in range(8)]
        top = functools.reduce(jnp.maximum, [p[0:1] for p in part])
        shift = [jnp.exp(p[0:1] - top) for p in part]
        total = sum(p[1:2] * w for p, w in zip(part, shift))
        delta = sum(p[2:3] * w for p, w in zip(part, shift)) / total
        offset = top + jnp.log(total)
        prob = jnp.exp(dot(keys, q[b]) * scale - offset)
        grad_s = (prob * (dot(values, g[b]) - delta)).astype(BF16)
        acc_v[...] += dot_t(prob.astype(BF16), g[b])
        acc_k[...] += dot_t(grad_s, q[b])
        dq[b] = (dot(keys_t, grad_s) * scale).astype(BF16)
        return carry

    lax.fori_loop(0, 8, step, 0)
    dk[...] = (acc_k[...] * scale).astype(BF16).reshape(4, 256, 384)
    dv[...] = acc_v[...].astype(BF16).reshape(4, 256, 384)


def total_of(ref, count):
    total = ref[0].astype(F32)
    for i in range(1, count):
        total += ref[i].astype(F32)
    return total


def residual_kernel(dq, dk, dv, res_frame, cot, gains, w_qkv, grad, full, cot_full):
    gain = jnp.concatenate([gains[b, 1] for b in range(CH)], 0).astype(F32)
    gain = jnp.concatenate([gain, gain], 1)
    x, inv = attn_norm(res_frame, full)
    for b in range(CH):
        for h in range(2):
            cot_full[pl.ds(96 * b, 96), pl.ds(128 * h, 128)] = cot[b, h]
    w = w_qkv[...]
    normed = (
        dot(w[:, :384], total_of(dq, 8).astype(BF16))
        + dot_t(w[:, 384:768], total_of(dk, 4).astype(BF16))
        + dot_t(w[:, 768:], total_of(dv, 4).astype(BF16))
    )
    scaled = normed.astype(BF16).astype(F32) * gain
    inner = jnp.mean(x * scaled, 0, keepdims=True)
    out = cot_full[...].astype(F32) + inv * scaled - x * (inv * inv * inv * inner)
    for b in range(CH):
        for h in range(2):
            grad[b, h] = out[96 * b : 96 * b + 96, 128 * h : 128 * h + 128].astype(BF16)


def grad_kernel(own, prev_g, next_g, act, w_t, all_feat, inv_in, gains, weight, part, inner, rows, lines):
    r = lax.axis_index("row")
    for f in range(4):
        rows[f, 0] = jnp.where(r == 0, 0.0, prev_g[f].astype(F32)).astype(BF16)
        rows[f, 1] = own[f, 0]
        rows[f, 2] = own[f, 1]
        rows[f, 3] = jnp.where(r == ROWS - 1, 0.0, next_g[f].astype(F32)).astype(BF16)
    moved = []
    for f in range(4):
        both = []
        for h in range(2):
            y = own[f, h].astype(F32)
            both.append(jnp.concatenate([move(y, -1), y, move(y, 1)], 0).astype(BF16))
        moved.append(jnp.concatenate(both, 1))
    for t in range(3):
        for h in range(3):
            acc = jnp.zeros((288, 384), F32)
            for f in range(4):
                source = f + t - 2
                if source < 0:
                    continue
                acc += dot_t(moved[f], act[:, pl.ds((4 * source + h) * 128, 256)])
            for lane in range(3):
                at = (3 * (3 * t + h) + lane) * 288
                weight[pl.ds(at, 288), :] = acc[:, 128 * lane : 128 * lane + 128].astype(BF16)
    weight[pl.ds(27 * 288, 416), :] = jnp.zeros((416, 128), BF16)
    for f in range(4):
        for h in range(3):
            for k in range(2):
                lines[f, pl.ds(96 * h, 96), pl.ds(128 * k, 128)] = rows[f, 2 - h + k]
    gain = jnp.concatenate([gains[b, 0] for b in range(CH)], 0).astype(F32)
    for f in range(4):
        acc = jnp.zeros((1152, 256), F32)
        for t in range(3):
            source = f + 2 - t
            if source > 3:
                continue
            acc += dot(w_t[t], lines[source])
        for h in range(2):
            y = acc[:, 128 * h : 128 * h + 128]
            out = move(y[:384], -1) + y[384:768] + move(y[768:], 1)
            x = jnp.concatenate([all_feat[b, f, h] for b in range(CH)], 0).astype(F32)
            before = x * inv_in[2 * f + h : 2 * f + h + 1, :] * gain
            sig = sigmoid(before)
            slope = sig * (1.0 + before * (1.0 - sig))
            inner[2 * f + h : 2 * f + h + 1, :] = jnp.sum(x * slope * gain * out, 0, keepdims=True)
            for b in range(CH):
                part[b, f, h] = out[96 * b : 96 * b + 96].astype(BF16)


def finish_kernel(feat, own, part, inner, inv_in, gain_own, weights, out, weight):
    total = total_of(weights, ROWS)
    weight[...] = total.astype(BF16)
    mean = (inner[0] + inner[1] + inner[2] + inner[3]) / 384.0
    gain = gain_own[0].astype(F32)
    for f in range(4):
        for h in range(2):
            x = feat[f, h].astype(F32)
            inv = inv_in[2 * f + h : 2 * f + h + 1, :]
            act = part[0, f, h].astype(F32)
            for b in range(1, CH):
                act += part[b, f, h].astype(F32)
            before = x * inv * gain
            sig = sigmoid(before)
            scaled = act * (sig * (1.0 + before * (1.0 - sig))) * gain
            cube = inv * inv * inv * mean[2 * f + h : 2 * f + h + 1, :]
            out[f, h] = (own[f, h].astype(F32) + inv * scaled - x * cube).astype(BF16)


def widen_kernel(scale, flat, out):
    for k in range(9):
        for lane in range(3):
            piece = flat[pl.ds((3 * k + lane) * 288, 288), :].astype(F32) * scale
            out[pl.ds(288 * k, 288), pl.ds(128 * lane, 128)] = piece


def on_device(features, gain_in, w_conv, gain_attn, w_qkv, w_out, cotangent):
    scale = 1.0 / math.sqrt(384)
    gain_own = jnp.broadcast_to(jnp.stack([gain_in, gain_attn])[:, :, None], (2, 96, 128))
    w_rows = w_conv.reshape(9, 288, 384)
    w_t = w_conv.reshape(3, 3, 3, 96, 384).transpose(0, 2, 4, 1, 3).reshape(3, 1152, 288)
    all_feat, prev_feat, next_feat, cot_frame, gains = exchange(
        0,
        (features, cotangent, gain_own),
        [
            ((4, 4, 2, 96, 128), BF16),
            ((4, 4, 96, 128), BF16),
            ((4, 4, 96, 128), BF16),
            ((4, 2, 96, 128), BF16),
            ((4, 2, 96, 128), BF16),
        ],
        start_plan,
        (17, 3),
    )
    res, act, inv_in, grad_o = compute(
        conv_kernel,
        [((4, 2, 96, 128), BF16), ((384, 2048), BF16), ((8, 128), F32), ((384, 256), BF16)],
        features,
        all_feat,
        prev_feat,
        next_feat,
        gains,
        w_rows,
        cot_frame,
        w_out,
        scratch=[pltpu.VMEM((384, 256), BF16)],
        name="conv",
    )
    (res_frame,) = exchange(1, (res,), [((4, 2, 96, 128), BF16)], frame_plan, (3, 1))
    q, k, v = compute(
        project_kernel,
        [((384, 256), BF16), ((256, 384), BF16), ((256, 384), BF16)],
        res_frame,
        gains,
        w_qkv,
        scratch=[pltpu.VMEM((384, 256), BF16)],
        name="project",
    )
    all_q, all_g, all_k, all_v = exchange(
        2,
        (q, grad_o, k, v),
        [((8, 384, 256), BF16)] * 2 + [((4, 256, 384), BF16)] * 2,
        gather_plan,
        (20, 4),
    )
    (stats,) = compute(
        functools.partial(stats_kernel, scale),
        [((8, 8, 256), F32)],
        all_q,
        all_g,
        all_k,
        all_v,
        name="stats",
    )
    (all_stats,) = exchange(3, (stats,), [((8, 8, 8, 256), F32)], stats_plan, (7, 1))
    dq, dk, dv = compute(
        functools.partial(attn_kernel, scale),
        [((8, 384, 256), BF16)] + [((4, 256, 384), BF16)] * 2,
        all_q,
        all_g,
        all_k,
        all_v,
        all_stats,
        scratch=[pltpu.VMEM((1024, 384), F32)] * 2,
        name="attn",
    )
    all_dq, all_dk, all_dv = exchange(
        4,
        (dq, dk, dv),
        [((8, 384, 256), BF16)] + [((4, 256, 384), BF16)] * 2,
        back_plan,
        (13, 3),
    )
    (grad,) = compute(
        residual_kernel,
        [((4, 2, 96, 128), BF16)],
        all_dq,
        all_dk,
        all_dv,
        res_frame,
        cot_frame,
        gains,
        w_qkv,
        scratch=[pltpu.VMEM((384, 256), BF16)] * 2,
        name="residual",
    )
    own, prev_g, next_g = exchange(
        5,
        (grad,),
        [((4, 2, 96, 128), BF16), ((4, 96, 128), BF16), ((4, 96, 128), BF16)],
        grad_plan,
        (11, 1),
    )
    weight, part, inner = compute(
        grad_kernel,
        [((8192, 128), BF16), ((4, 4, 2, 96, 128), BF16), ((8, 128), F32)],
        own,
        prev_g,
        next_g,
        act,
        w_t,
        all_feat,
        inv_in,
        gains,
        scratch=[pltpu.VMEM((4, 4, 96, 128), BF16), pltpu.VMEM((4, 288, 256), BF16)],
        name="grad",
    )
    weights, parts, inners = exchange(
        6,
        (weight.reshape(ROWS, 256, 128), part, inner),
        [((ROWS, 256, 128), BF16), ((4, 4, 2, 96, 128), BF16), ((4, 8, 128), F32)],
        scatter_plan,
        (37, 3),
    )
    out, weight_sum = compute(
        finish_kernel,
        [((4, 2, 96, 128), BF16), ((256, 128), BF16)],
        features,
        own,
        parts,
        inners,
        inv_in,
        gain_own,
        weights,
        name="finish",
    )
    (flat,) = exchange(7, (weight_sum,), [((ROWS, 256, 128), BF16)], spread_plan, (31, 1))
    cell_scale = 1.0 / math.sqrt(32768)
    (grad_weights,) = compute(
        functools.partial(widen_kernel, cell_scale),
        [((2592, 384), F32)],
        flat.reshape(8192, 128),
        name="widen",
    )
    return out, grad_weights.reshape(27, 96, 384)


def solution(mesh):
    return jax.shard_map(
        on_device,
        mesh=mesh,
        in_specs=(
            P(None, "row", "ch", None),
            P("ch"),
            P(None, "ch", None),
            P("ch"),
            P(),
            P(),
            P(None, "row", "ch", None),
        ),
        out_specs=(P(None, "row", "ch", None), P(None, "ch", None)),
        check_vma=False,
    )
```

time: 1130 us -> 290 us (0.26)
  waiting for transfers between devices: 843 us -> 0 us
  Pallas kernels: 0 us -> 277 us
  local copies, waits for them, and re-layouts: 92.5 us -> 11.2 us
  matrix products: 79.8 us -> 0 us
  blocking collectives: 55.1 us -> 0 us
  other arithmetic: 28.2 us -> 0.68 us
  between operations: 15 us -> 0.7 us
    psum x1 -> x0, waiting for transfers between devices: 362 us -> none  [on_device(): grad_weights = lax.psum(weight_part, 'row') * cell_scale]
    reduce_scatter x2 -> x0, waiting for transfers between devices: 295 us -> none  [the longest x1 295 us: on_device(): lax.psum_scatter(key_term.reshape(own_frames, -1, col_count, 2 * channels...]
    pallas_call x0 -> x16, Pallas kernels: none -> 277 us  [the longest x8 220 us: exchange(): pl.pallas_call(body, out_shape=[jax.ShapeDtypeStruct(s, t) for s, t in ou...]
    all_gather x2 -> x0, waiting for transfers between devices: 172 us -> none  [the longest x1 90 us: on_device(): lax.all_gather(keys_own, 'row', axis=1, tiled=True)]
    dot_general x36 -> x0, matrix products: 79.8 us -> none  [the longest x9 27.5 us: conv_weight_grad(): jnp.einsum('fhow,fhkw->ok', grad_out, slab, preferred_element_type=jnp.fl...]
    concatenate x1 -> x0, local copies, waits for them, and re-layouts: 37.4 us -> none  [conv_weight_grad(): return jnp.concatenate(pieces, axis=0)]
    psum x4 -> x0, blocking collectives: 23.9 us -> none  [channel_total(): return lax.psum(values, 'ch')]
    all_to_all x3 -> x0, blocking collectives: 22.4 us -> none  [the longest x1 8.15 us: on_device(): lax.all_to_all(cotangent, 'ch', split_axis=0, concat_axis=2, tiled=True)]
  transfers between devices with their start and end apart: 9 -> 0, of which waited for: 7 -> 0; matrix products, arithmetic and copies ran while one was open for 9% -> 0% of each run, Pallas kernels for 0% -> 0%
where the time goes in v1:
time: 290 us
  Pallas kernels  277 us (96%)
  local copies, waits for them, and re-layouts  11.2 us (4%)
    pallas_call x8, Pallas kernels, exchange(): pl.pallas_call(body, out_shape=[jax.ShapeDtypeStruct(s, t) for s, t in ou...  220 us
    pallas_call x8, Pallas kernels, compute(): pl.pallas_call(body, out_shape=[jax.ShapeDtypeStruct(s, t) for s, t in ou...  57.7 us
    reshape x3, local copies, waits for them, and re-layouts, on_device(): w_conv.reshape(3, 3, 3, 96, 384).transpose(0, 2, 4, 1, 3)  10.5 us

profile of v1, /device:TPU:8, one launch (start us, length us, event | category | flops | bytes accessed | tf_op | source)
XLA Modules:
  0.0 289.8 jit_solution(1904992131616260373)
XLA Ops:
  0.6 0.7 pad_maximum_fusion
  1.3 0.7 broadcast_in_dim.2.refs_2_.gain_own
  2.0 26.6 %exchange_0.1 = (bf16[4,4,2,96,128]{4,3,2,1,0:T(8,128)(2,1)}, bf16[4,4,96,128]{3,2,1,0:T(8,128)(2,1)}, bf16[4,4,96,128]{3,2,1,0:T(8,128)(2,1)}, bf16[4,2,96,128]{3,2,1,0:T(8,128)(2,1)}, bf16[4,2,96,128]{3,2,1,0:T(8,128)(2,1)}) custom-call(bf16[4,2,96,128]{3,2,1,0:T(8,128)(2,1)} %feat.3, bf16[4,2,96,128]{3,2,1,0:T(8,128)(2,1)} %refs_1_.1, ...), custom_call_target="tpu_custom_call" | custom-call | tf_op jit(solution)/shard_map/exchange_0/pallas_call | solution.py:54
  28.6 6.2 %conv.1 = (bf16[4,2,96,128]{3,2,1,0:T(8,128)(2,1)}, bf16[384,2048]{1,0:T(8,128)(2,1)}, f32[8,128]{1,0:T(8,128)}, bf16[384,256]{1,0:T(8,128)(2,1)}) custom-call(bf16[4,2,96,128]{3,2,1,0:T(8,128)(2,1)} %feat.3, bf16[4,4,2,96,128]{4,3,2,1,0:T(8,128)(2,1)} %get-tuple-element.35.all_feat, bf16[4,4,96,128]{3,2,1,0:T(8,128)(2,1)} %get-tuple-element.36.prev_feat, ...), custom_call_target="tpu_custom_call" | custom-call | tf_op jit(solution)/shard_map/conv/pallas_call | solution.py:70
  34.8 6.2 %exchange_1.1.res_frame = bf16[4,2,96,128]{3,2,1,0:T(8,128)(2,1)} custom-call(bf16[4,2,96,128]{3,2,1,0:T(8,128)(2,1)} %get-tuple-element.40.refs_0_), custom_call_target="tpu_custom_call" | custom-call | tf_op jit(solution)/shard_map/exchange_1/pallas_call | solution.py:54
  41.0 2.7 project.1
  43.7 54.2 %exchange_2.1 = (bf16[8,384,256]{2,1,0:T(8,128)(2,1)}, bf16[8,384,256]{2,1,0:T(8,128)(2,1)}, bf16[4,256,384]{2,1,0:T(8,128)(2,1)}, bf16[4,256,384]{2,1,0:T(8,128)(2,1)}) custom-call(bf16[384,256]{1,0:T(8,128)(2,1)} %get-tuple-element.41.refs_0_, bf16[384,256]{1,0:T(8,128)(2,1)} %get-tuple-element.42.refs_1_, bf16[256,384]{1,0:T(8,128)(2,1)} %get-tuple-element.43.refs_2_, ...), custom_call_target="tpu_custom_call" | custom-call | tf_op jit(solution)/shard_map/exchange_2/pallas_call | solution.py:54
  97.9 12.0 %stats.1.refs_0_ = f32[8,8,256]{2,1,0:T(8,128)} custom-call(bf16[8,384,256]{2,1,0:T(8,128)(2,1)} %get-tuple-element.45.q, bf16[8,384,256]{2,1,0:T(8,128)(2,1)} %get-tuple-element.46.g, bf16[4,256,384]{2,1,0:T(8,128)(2,1)} %get-tuple-element.47.k, bf16[4,256,384]{2,1,0:T(8,128)(2,1)} %get-tuple-element.48.v), custom_call_target="tpu_custom_call" | custom-call | tf_op jit(solution)/shard_map/stats/pallas_call | solution.py:70
  109.9 15.8 %exchange_3.1.stats = f32[8,8,8,256]{3,2,1,0:T(8,128)} custom-call(f32[8,8,256]{2,1,0:T(8,128)} %stats.1.refs_0_), custom_call_target="tpu_custom_call" | custom-call | tf_op jit(solution)/shard_map/exchange_3/pallas_call | solution.py:54
  125.7 16.5 %attn.1 = (bf16[8,384,256]{2,1,0:T(8,128)(2,1)}, bf16[4,256,384]{2,1,0:T(8,128)(2,1)}, bf16[4,256,384]{2,1,0:T(8,128)(2,1)}) custom-call(bf16[8,384,256]{2,1,0:T(8,128)(2,1)} %get-tuple-element.45.q, bf16[8,384,256]{2,1,0:T(8,128)(2,1)} %get-tuple-element.46.g, bf16[4,256,384]{2,1,0:T(8,128)(2,1)} %get-tuple-element.47.k, ...), custom_call_target="tpu_custom_call" | custom-call | tf_op jit(solution)/shard_map/attn/pallas_call | solution.py:70
  142.2 24.7 %exchange_4.1 = (bf16[8,384,256]{2,1,0:T(8,128)(2,1)}, bf16[4,256,384]{2,1,0:T(8,128)(2,1)}, bf16[4,256,384]{2,1,0:T(8,128)(2,1)}) custom-call(bf16[8,384,256]{2,1,0:T(8,128)(2,1)} %get-tuple-element.49.refs_0_, bf16[4,256,384]{2,1,0:T(8,128)(2,1)} %get-tuple-element.50.refs_1_, bf16[4,256,384]{2,1,0:T(8,128)(2,1)} %get-tuple-element.51.refs_2_), custom_call_target="tpu_custom_call" | custom-call | tf_op jit(solution)/shard_map/exchange_4/pallas_call | solution.py:54
  166.9 3.8 %residual.1.refs_0_ = bf16[4,2,96,128]{3,2,1,0:T(8,128)(2,1)} custom-call(bf16[8,384,256]{2,1,0:T(8,128)(2,1)} %get-tuple-element.52.dq, bf16[4,256,384]{2,1,0:T(8,128)(2,1)} %get-tuple-element.53.dk, bf16[4,256,384]{2,1,0:T(8,128)(2,1)} %get-tuple-element.54.dv, bf16[4,2,96,128]{3,2,1,0:T(8,128)(2,1)} %exchange_1.1.res_frame, ...), custom_call_target="tpu_custom_call" | custom-call | tf_op jit(solution)/shard_map/residual/pallas_call | solution.py:70
  170.7 12.0 %exchange_5.1 = (bf16[4,2,96,128]{3,2,1,0:T(8,128)(2,1)}, bf16[4,96,128]{2,1,0:T(8,128)(2,1)}, bf16[4,96,128]{2,1,0:T(8,128)(2,1)}) custom-call(bf16[4,2,96,128]{3,2,1,0:T(8,128)(2,1)} %residual.1.refs_0_), custom_call_target="tpu_custom_call" | custom-call | tf_op jit(solution)/shard_map/exchange_5/pallas_call | solution.py:54
  182.7 2.9 %copy.13 = bf16[3,3,3,96,384]{4,2,3,1,0:T(4,128)(2,1)S(1)} copy(bf16[3,3,3,96,384]{4,3,2,1,0:T(8,128)(2,1)} %bitcast.15) | data formatting | bytes 3981312 | tf_op jit(solution)/shard_map/reshape | solution.py:445
  185.7 3.3 %reshape.25 = bf16[3,1152,288]{1,2,0:T(8,128)(2,1)} reshape(bf16[3,3,384,3,96]{2,1,4,3,0:T(4,128)(2,1)S(1)} %bitcast.12) | data formatting | bytes 3981312 | tf_op jit(solution)/shard_map/reshape | solution.py:445
  189.0 4.2 %copy.11.w_t = bf16[3,1152,288]{2,1,0:T(8,128)(2,1)} copy(bf16[3,1152,288]{1,2,0:T(8,128)(2,1)} %reshape.25) | data formatting | bytes 3981312 | tf_op jit(solution)/shard_map/reshape | solution.py:445
  193.2 9.2 %grad.1 = (bf16[8192,128]{1,0:T(8,128)(2,1)}, bf16[4,4,2,96,128]{4,3,2,1,0:T(8,128)(2,1)}, f32[8,128]{1,0:T(8,128)}) custom-call(bf16[4,2,96,128]{3,2,1,0:T(8,128)(2,1)} %get-tuple-element.55.own, bf16[4,96,128]{2,1,0:T(8,128)(2,1)} %get-tuple-element.56.prev_g, bf16[4,96,128]{2,1,0:T(8,128)(2,1)} %get-tuple-element.57.next_g, ...), custom_call_target="tpu_custom_call" | custom-call | tf_op jit(solution)/shard_map/grad/pallas_call | solution.py:70
  202.4 41.5 %exchange_6.1 = (bf16[32,256,128]{2,1,0:T(8,128)(2,1)}, bf16[4,4,2,96,128]{4,3,2,1,0:T(8,128)(2,1)}, f32[4,8,128]{2,1,0:T(8,128)}) custom-call(bf16[32,256,128]{2,1,0:T(8,128)(2,1)} %bitcast.17, bf16[4,4,2,96,128]{4,3,2,1,0:T(8,128)(2,1)} %get-tuple-element.61.refs_1_, f32[8,128]{1,0:T(8,128)} %get-tuple-element.62.refs_2_), custom_call_target="tpu_custom_call" | custom-call | tf_op jit(solution)/shard_map/exchange_6/pallas_call | solution.py:54
  244.0 3.4 %finish.1 = (bf16[4,2,96,128]{3,2,1,0:T(8,128)(2,1)}, bf16[256,128]{1,0:T(8,128)(2,1)}) custom-call(bf16[4,2,96,128]{3,2,1,0:T(8,128)(2,1)} %feat.3, bf16[4,2,96,128]{3,2,1,0:T(8,128)(2,1)} %get-tuple-element.55.own, bf16[4,4,2,96,128]{4,3,2,1,0:T(8,128)(2,1)} %get-tuple-element.63.part, f32[4,8,128]{2,1,0:T(8,128)} %get-tuple-element.64.inner, ...), custom_call_target="tpu_custom_call" | custom-call | tf_op jit(solution)/shard_map/finish/pallas_call | solution.py:70
  247.4 38.6 %exchange_7.1 = bf16[32,256,128]{2,1,0:T(8,128)(2,1)} custom-call(bf16[256,128]{1,0:T(8,128)(2,1)} %get-tuple-element.67.refs_0_), custom_call_target="tpu_custom_call" | custom-call | tf_op jit(solution)/shard_map/exchange_7/pallas_call | solution.py:54
  286.0 3.8 %widen.1 = f32[2592,384]{1,0:T(8,128)} custom-call(bf16[8192,128]{1,0:T(8,128)(2,1)} %bitcast.13), custom_call_target="tpu_custom_call" | custom-call | tf_op jit(solution)/shard_map/widen/pallas_call | solution.py:70

commit v2 on v1

--- a/solution.py
+++ b/solution.py
@@ -21,49 +21,100 @@
     return lax.axis_index("row"), lax.axis_index("ch")
 
 
-def exchange(cid, ins, outs, plan, count):
-    def body(*refs):
-        srcs, dsts = refs[: len(ins)], refs[len(ins) : len(ins) + len(outs)]
-        send, recv, own = refs[len(ins) + len(outs) :]
-        remote, local, peers = plan(srcs, dsts)
+def place(r, c):
+    return lax.rem(r, 4), lax.rem(r // 4, 2), r // 8, c // 2, lax.rem(c, 2)
+
+
+def device(x, y_hi, z, y_lo, core):
+    return z * 8 + y_hi * 4 + x, y_lo * 2 + core
+
+
+def owner(f, row):
+    x, y_hi, z, _, _ = place(row, 0)
+    return device(x, f // 2, z, f % 2, y_hi)
+
+
+class Links:
+    def __init__(self, send, recv):
+        self.send, self.recv, self.sent, self.at = send, recv, [], 0
+
+    def greet(self, peers, count):
         barrier = pltpu.get_barrier_semaphore()
         for peer in peers:
             pl.semaphore_signal(barrier, inc=1, device_id=peer, device_id_type=MESH)
+        pl.semaphore_wait(barrier, count)
+
+    def copy(self, src, dst, to, own=None, recv=None):
+        k = self.at
+        self.at += 1
+        mark = self.recv.at[k if recv is None else recv]
+        far = pltpu.make_async_remote_copy(
+            src_ref=src,
+            dst_ref=dst,
+            send_sem=self.send.at[k],
+            recv_sem=mark,
+            device_id=to,
+            device_id_type=MESH,
+        )
+        if own is None:
+            far.start()
+        else:
+            pl.when(jnp.logical_not(own))(far.start)
+            pl.when(own)(pltpu.make_async_copy(src, dst, mark).start)
+        self.sent.append((far, own))
+        return far
+
+    def arrive(self, dst, k):
+        pltpu.make_async_copy(dst, dst, self.recv.at[k]).wait()
+
+    def finish(self):
+        for far, own in self.sent:
+            if own is None:
+                far.wait_send()
+            else:
+                pl.when(jnp.logical_not(own))(far.wait_send)
+
+
+def exchange(cid, body, ins, outs, count, local=0, held=(), made=()):
+    def kernel(*refs):
+        n_in, n_out = len(ins) + len(held), len(outs) + len(made)
+        send, recv, own = refs[n_in + n_out :]
+        body(Links(send, recv), own, refs[:n_in], refs[n_in : n_in + n_out])
+
+    far = pl.BlockSpec(memory_space=pl.ANY)
+    near = pl.BlockSpec(memory_space=pltpu.VMEM)
+    return pl.pallas_call(
+        kernel,
+        out_shape=[jax.ShapeDtypeStruct(s, t) for s, t in list(outs) + list(made)],
+        in_specs=[far] * len(ins) + [near] * len(held),
+        out_specs=[far] * len(outs) + [near] * len(made),
+        scratch_shapes=[
+            pltpu.SemaphoreType.DMA((count,)),
+            pltpu.SemaphoreType.DMA((count,)),
+            pltpu.SemaphoreType.DMA((max(local, 1),)),
+        ],
+        compiler_params=pltpu.CompilerParams(
+            collective_id=cid, has_side_effects=True, vmem_limit_bytes=VMEM_BYTES
+        ),
+        name="exchange_%d" % cid,
+    )(*ins, *held)
+
+
+def simple(plan):
+    def body(links, own, srcs, dsts):
+        remote, local, peers = plan(srcs, dsts)
         here = [pltpu.make_async_copy(s, d, own.at[k]) for k, (s, d) in enumerate(local)]
         for copy in here:
             copy.start()
-        pl.semaphore_wait(barrier, len(peers))
-        there = [
-            pltpu.make_async_remote_copy(
-                src_ref=s,
-                dst_ref=d,
-                send_sem=send.at[k],
-                recv_sem=recv.at[k],
-                device_id=peer,
-                device_id_type=MESH,
-            )
-            for k, (s, d, peer) in enumerate(remote)
-        ]
-        for copy in there:
-            copy.start()
+        links.greet(peers, len(peers))
+        there = [links.copy(s, d, to) for s, d, to in remote]
         for copy in here:
             copy.wait()
         for copy in there:
-            copy.wait()
-
-    return pl.pallas_call(
-        body,
-        out_shape=[jax.ShapeDtypeStruct(s, t) for s, t in outs],
-        in_specs=[pl.BlockSpec(memory_space=pl.ANY)] * len(ins),
-        out_specs=[pl.BlockSpec(memory_space=pl.ANY)] * len(outs),
-        scratch_shapes=[
-            pltpu.SemaphoreType.DMA((count[0],)),
-            pltpu.SemaphoreType.DMA((count[0],)),
-            pltpu.SemaphoreType.DMA((max(count[1], 1),)),
-        ],
-        compiler_params=pltpu.CompilerParams(collective_id=cid, has_side_effects=True),
-        name="exchange_%d" % cid,
-    )(*ins)
+            copy.wait_recv()
+        links.finish()
+
+    return body
 
 
 def compute(body, outs, *ins, scratch=(), name):
@@ -102,104 +153,185 @@
     return lax.rem(r + ROWS - 1, ROWS), lax.rem(r + 1, ROWS)
 
 
-def start_plan(srcs, dsts):
-    feat, cot, gain = srcs
-    all_feat, prev_feat, next_feat, cot_frame, all_gain = dsts
+def same(a, b):
+    return jnp.logical_and(a[0] == b[0], a[1] == b[1])
+
+
+def greet_frames(links, me, sources, targets):
+    barrier = pltpu.get_barrier_semaphore()
+    for peer in sources:
+        def tell(peer=peer):
+            pl.semaphore_signal(barrier, inc=1, device_id=peer, device_id_type=MESH)
+
+        pl.when(jnp.logical_not(same(peer, me)))(tell)
+    _, y_hi, _, _, core = place(*me)
+    pl.semaphore_wait(barrier, len(targets) - 1 + (core - y_hi) * (core - y_hi))
+
+
+def start_body(links, own, srcs, dsts):
+    feat, cot, gain, w = srcs
+    all_feat, prev_feat, next_feat, cot_frame, all_gain, w_t = dsts
     r, c = coords()
     low, high = near_rows(r)
-    remote, peers = [], []
-    for row, c_to in ch_peers(r, c):
-        remote.append((feat, all_feat.at[c], (row, c_to)))
-        remote.append((cot.at[c_to], cot_frame.at[c], (row, c_to)))
-        remote.append((gain, all_gain.at[c], (row, c_to)))
-        peers.append((row, c_to))
+    x, y_hi, z, y_lo, core = place(r, c)
+    here = [
+        pltpu.make_async_copy(feat, all_feat.at[c], own.at[0]),
+        pltpu.make_async_copy(gain, all_gain.at[c], own.at[1]),
+    ]
+    for copy in here:
+        copy.start()
+    targets = [owner(f, r) for f in range(4)]
+    sources = [(z * 8 + core * 4 + x, b) for b in range(4)]
+    others = ch_peers(r, c) + [(row, b) for row in (low, high) for b in range(CH)]
+    greet_frames(links, (r, c), sources + others, targets + others)
+    for f in range(4):
+        links.copy(cot.at[f], cot_frame.at[c], targets[f], own=same(targets[f], (r, c)), recv=c)
+    there = []
+    for to in ch_peers(r, c):
+        there.append(links.copy(feat, all_feat.at[c], to))
+        there.append(links.copy(gain, all_gain.at[c], to))
     for d in range(CH):
         c_to = lax.rem(c + d, CH)
-        remote.append((feat.at[:, 1], prev_feat.at[c], (high, c_to)))
-        remote.append((feat.at[:, 0], next_feat.at[c], (low, c_to)))
-        peers += [(high, c_to), (low, c_to)]
-    local = [(feat, all_feat.at[c]), (cot.at[c], cot_frame.at[c]), (gain, all_gain.at[c])]
-    return remote, local, peers
-
-
-def frame_plan(srcs, dsts):
+        there.append(links.copy(feat.at[:, 1], prev_feat.at[c], (high, c_to)))
+        there.append(links.copy(feat.at[:, 0], next_feat.at[c], (low, c_to)))
+    for t in range(3):
+        for k in range(3):
+            piece = jnp.concatenate([w[9 * t + 3 * h + k] for h in range(3)], 0)
+            w_t[t, pl.ds(384 * k, 384), :] = piece.T
+    for copy in here:
+        copy.wait()
+    for b in range(CH):
+        links.arrive(cot_frame.at[b], b)
+    for copy in there:
+        copy.wait_recv()
+    links.finish()
+
+
+def frame_body(links, own, srcs, dsts):
     (res,), (res_frame,) = srcs, dsts
     r, c = coords()
-    peers = ch_peers(r, c)
-    remote = [(res.at[to[1]], res_frame.at[c], to) for to in peers]
-    return remote, [(res.at[c], res_frame.at[c])], peers
+    x, y_hi, z, y_lo, core = place(r, c)
+    targets = [owner(f, r) for f in range(4)]
+    sources = [(z * 8 + core * 4 + x, b) for b in range(4)]
+    greet_frames(links, (r, c), sources, targets)
+    for f in range(4):
+        links.copy(res.at[f], res_frame.at[c], targets[f], own=same(targets[f], (r, c)), recv=c)
+    for b in range(CH):
+        links.arrive(res_frame.at[b], b)
+    links.finish()
 
 
 def key_peers(r, c):
-    z, yx = r // 8, lax.rem(r, 8)
-    return [(lax.rem(z + d, 4) * 8 + yx, c) for d in range(1, 4)]
+    return [(lax.rem(r + 8 * d, ROWS), c) for d in range(1, 4)]
 
 
 def query_peers(r, c):
-    z, y, x = r // 8, lax.rem(r // 4, 2), lax.rem(r, 4)
+    x, y_hi, z, y_lo, core = place(r, c)
     found = []
-    for dy in range(2):
+    for dk in range(2):
         for dx in range(4):
-            if dy or dx:
-                found.append((z * 8 + lax.rem(y + dy, 2) * 4 + lax.rem(x + dx, 4), c))
+            if dk or dx:
+                found.append(device(lax.rem(x + dx, 4), y_hi, z, y_lo, lax.rem(core + dk, 2)))
     return found
 
 
-def gather_plan(srcs, dsts):
+def gather_body(links, own, srcs, dsts):
     q, g, k, v = srcs
     all_q, all_g, all_k, all_v = dsts
     r, c = coords()
-    z, yx = r // 8, lax.rem(r, 8)
-    remote, peers = [], []
-    for to in query_peers(r, c):
-        remote += [(q, all_q.at[yx], to), (g, all_g.at[yx], to)]
-        peers.append(to)
-    for to in key_peers(r, c):
-        remote += [(k, all_k.at[z], to), (v, all_v.at[z], to)]
-        peers.append(to)
-    local = [(q, all_q.at[yx]), (g, all_g.at[yx]), (k, all_k.at[z]), (v, all_v.at[z])]
-    return remote, local, peers
+    x, y_hi, z, y_lo, core = place(r, c)
+    slot = core * 4 + x
+    local = [(q, all_q.at[slot]), (g, all_g.at[slot]), (k, all_k.at[z]), (v, all_v.at[z])]
+    here = [pltpu.make_async_copy(s, d, own.at[i]) for i, (s, d) in enumerate(local)]
+    for copy in here:
+        copy.start()
+    sibling = (r, y_lo * 2 + 1 - core)
+    x_next, x_back = lax.rem(x + 1, 4), lax.rem(x + 3, 4)
+    z_next, z_back = lax.rem(z + 1, 4), lax.rem(z + 3, 4)
+    xs = [device(i, y_hi, z, y_lo, core) for i in (x_next, x_back)]
+    zs = [device(x, y_hi, i, y_lo, core) for i in (z_next, z_back)]
+    links.greet(xs + zs + [sibling], 5)
+    pairs = ((q, all_q, core * 4, x, xs), (g, all_g, core * 4, x, xs), (k, all_k, 0, z, zs), (v, all_v, 0, z, zs))
+    first = []
+    for src, dst, base, i, to in pairs:
+        first.append([links.copy(src, dst.at[base + i], peer) for peer in to])
+    relayed = []
+    for src, dst in ((q, all_q), (g, all_g)):
+        relayed.append(links.copy(src, dst.at[slot], sibling))
+    for n in (0, 2, 1, 3):
+        src, dst, base, i, to = pairs[n]
+        half = src.shape[0] // 2
+        for side in range(2):
+            first[n][side].wait_recv()
+            came = base + lax.rem(i + 3 - 2 * side, 4)
+            part = dst.at[came, pl.ds(half * side, half)]
+            relayed.append(links.copy(part, part, to[side]))
+            if n < 2:
+                relayed.append(links.copy(dst.at[came], dst.at[came], sibling))
+    far = relayed[2:]
+    for n, dst in ((0, all_q), (6, all_g)):
+        at = core * 4 + lax.rem(x + 2, 4)
+        far[n].wait_recv()
+        far[n + 2].wait_recv()
+        relayed.append(links.copy(dst.at[at], dst.at[at], sibling))
+    for n, copy in enumerate(relayed):
+        if n - 2 not in (0, 2, 6, 8):
+            copy.wait_recv()
+    for copy in here:
+        copy.wait()
+    links.finish()
 
 
 def stats_plan(srcs, dsts):
     (own,), (every,) = srcs, dsts
     r, c = coords()
-    yx = lax.rem(r, 8)
+    x, y_hi, z, y_lo, core = place(r, c)
+    slot = core * 4 + x
     peers = query_peers(r, c)
-    return [(own, every.at[yx], to) for to in peers], [(own, every.at[yx])], peers
+    return [(own, every.at[slot], to) for to in peers], [(own, every.at[slot])], peers
 
 
 def back_plan(srcs, dsts):
     dq, dk, dv = srcs
     all_q, all_k, all_v = dsts
     r, c = coords()
-    z, yx = r // 8, lax.rem(r, 8)
+    x, y_hi, z, y_lo, core = place(r, c)
+    slot = core * 4 + x
     remote, peers = [], []
     for to in query_peers(r, c):
-        remote.append((dq.at[lax.rem(to[0], 8)], all_q.at[yx], to))
+        there = lax.rem(to[1], 2) * 4 + lax.rem(to[0], 4)
+        remote.append((dq.at[there], all_q.at[slot], to))
         peers.append(to)
     for to in key_peers(r, c):
         at = to[0] // 8
         remote += [(dk.at[at], all_k.at[z], to), (dv.at[at], all_v.at[z], to)]
         peers.append(to)
-    local = [(dq.at[yx], all_q.at[yx]), (dk.at[z], all_k.at[z]), (dv.at[z], all_v.at[z])]
+    local = [(dq.at[slot], all_q.at[slot]), (dk.at[z], all_k.at[z]), (dv.at[z], all_v.at[z])]
     return remote, local, peers
 
 
-def grad_plan(srcs, dsts):
-    (g,), (own, prev_g, next_g) = srcs, dsts
+def grad_body(links, own, srcs, dsts):
+    (g,), (mine, prev_g, next_g) = srcs, dsts
     r, c = coords()
+    x, y_hi, z, y_lo, core = place(r, c)
+    frame = y_hi * 2 + y_lo
+    row = z * 8 + core * 4 + x
+    row_low, row_high = near_rows(row)
     low, high = near_rows(r)
-    remote, peers = [], []
-    for to in ch_peers(r, c):
-        remote.append((g.at[to[1]], own.at[c], to))
-        peers.append(to)
-    for d in range(CH):
-        c_to = lax.rem(c + d, CH)
-        remote.append((g.at[c_to, 1], prev_g.at[c], (high, c_to)))
-        remote.append((g.at[c_to, 0], next_g.at[c], (low, c_to)))
-        peers += [(high, c_to), (low, c_to)]
-    return remote, [(g.at[c], own.at[c])], peers
+    targets = [(row, b) for b in range(CH)]
+    around = [(i, b) for i in (row_low, row_high) for b in range(CH)]
+    sources = [owner(f, i) for i in (r, low, high) for f in range(4)]
+    greet_frames(links, (r, c), sources, targets + around)
+    for b in range(CH):
+        links.copy(g.at[b], mine.at[frame], (row, b), own=same((row, b), (r, c)), recv=frame)
+    for b in range(CH):
+        links.copy(g.at[b, 1], prev_g.at[frame], (row_high, b), recv=4 + frame)
+        links.copy(g.at[b, 0], next_g.at[frame], (row_low, b), recv=8 + frame)
+    for f in range(4):
+        links.arrive(mine.at[f], f)
+        links.arrive(prev_g.at[f], 4 + f)
+        links.arrive(next_g.at[f], 8 + f)
+    links.finish()
 
 
 def row_peers(r, c):
@@ -300,10 +432,9 @@
         s = dot(keys, q[b]) * scale
         m = jnp.max(s, 0, keepdims=True)
         e = jnp.exp(s - m)
-        stats[b, 0:1, :] = m
-        stats[b, 1:2, :] = jnp.sum(e, 0, keepdims=True)
-        stats[b, 2:3, :] = jnp.sum(e * dot(values, g[b]), 0, keepdims=True)
-        stats[b, 3:8, :] = jnp.zeros((5, 256), F32)
+        stats[0, pl.ds(b, 1), :] = m
+        stats[1, pl.ds(b, 1), :] = jnp.sum(e, 0, keepdims=True)
+        stats[2, pl.ds(b, 1), :] = jnp.sum(e * dot(values, g[b]), 0, keepdims=True)
         return carry
 
     lax.fori_loop(0, 8, step, 0)
@@ -316,11 +447,11 @@
     acc_v[...] = jnp.zeros_like(acc_v)
 
     def step(b, carry):
-        part = [stats[i, b] for i in range(8)]
-        top = functools.reduce(jnp.maximum, [p[0:1] for p in part])
-        shift = [jnp.exp(p[0:1] - top) for p in part]
-        total = sum(p[1:2] * w for p, w in zip(part, shift))
-        delta = sum(p[2:3] * w for p, w in zip(part, shift)) / total
+        part = [[stats[i, n, pl.ds(b, 1), :] for n in range(3)] for i in range(8)]
+        top = functools.reduce(jnp.maximum, [p[0] for p in part])
+        shift = [jnp.exp(p[0] - top) for p in part]
+        total = sum(p[1] * w for p, w in zip(part, shift))
+        delta = sum(p[2] * w for p, w in zip(part, shift)) / total
         offset = top + jnp.log(total)
         prob = jnp.exp(dot(keys, q[b]) * scale - offset)
         grad_s = (prob * (dot(values, g[b]) - delta)).astype(BF16)
@@ -442,9 +573,9 @@
     scale = 1.0 / math.sqrt(384)
     gain_own = jnp.broadcast_to(jnp.stack([gain_in, gain_attn])[:, :, None], (2, 96, 128))
     w_rows = w_conv.reshape(9, 288, 384)
-    w_t = w_conv.reshape(3, 3, 3, 96, 384).transpose(0, 2, 4, 1, 3).reshape(3, 1152, 288)
-    all_feat, prev_feat, next_feat, cot_frame, gains = exchange(
+    all_feat, prev_feat, next_feat, cot_frame, gains, w_t = exchange(
         0,
+        start_body,
         (features, cotangent, gain_own),
         [
             ((4, 4, 2, 96, 128), BF16),
@@ -453,8 +584,10 @@
             ((4, 2, 96, 128), BF16),
             ((4, 2, 96, 128), BF16),
         ],
-        start_plan,
-        (17, 3),
+        18,
+        local=2,
+        held=(w_conv,),
+        made=[((3, 1152, 288), BF16)],
     )
     res, act, inv_in, grad_o = compute(
         conv_kernel,
@@ -470,7 +603,7 @@
         scratch=[pltpu.VMEM((384, 256), BF16)],
         name="conv",
     )
-    (res_frame,) = exchange(1, (res,), [((4, 2, 96, 128), BF16)], frame_plan, (3, 1))
+    (res_frame,) = exchange(1, frame_body, (res,), [((4, 2, 96, 128), BF16)], 4)
     q, k, v = compute(
         project_kernel,
         [((384, 256), BF16), ((256, 384), BF16), ((256, 384), BF16)],
@@ -482,21 +615,22 @@
     )
     all_q, all_g, all_k, all_v = exchange(
         2,
+        gather_body,
         (q, grad_o, k, v),
         [((8, 384, 256), BF16)] * 2 + [((4, 256, 384), BF16)] * 2,
-        gather_plan,
-        (20, 4),
+        24,
+        local=4,
     )
     (stats,) = compute(
         functools.partial(stats_kernel, scale),
-        [((8, 8, 256), F32)],
+        [((3, 8, 256), F32)],
         all_q,
         all_g,
         all_k,
         all_v,
         name="stats",
     )
-    (all_stats,) = exchange(3, (stats,), [((8, 8, 8, 256), F32)], stats_plan, (7, 1))
+    (all_stats,) = exchange(3, simple(stats_plan), (stats,), [((8, 3, 8, 256), F32)], 7, local=1)
     dq, dk, dv = compute(
         functools.partial(attn_kernel, scale),
         [((8, 384, 256), BF16)] + [((4, 256, 384), BF16)] * 2,
@@ -510,10 +644,11 @@
     )
     all_dq, all_dk, all_dv = exchange(
         4,
+        simple(back_plan),
         (dq, dk, dv),
         [((8, 384, 256), BF16)] + [((4, 256, 384), BF16)] * 2,
-        back_plan,
-        (13, 3),
+        13,
+        local=3,
     )
     (grad,) = compute(
         residual_kernel,
@@ -530,10 +665,10 @@
     )
     own, prev_g, next_g = exchange(
         5,
+        grad_body,
         (grad,),
         [((4, 2, 96, 128), BF16), ((4, 96, 128), BF16), ((4, 96, 128), BF16)],
-        grad_plan,
-        (11, 1),
+        12,
     )
     weight, part, inner = compute(
         grad_kernel,
@@ -551,10 +686,11 @@
     )
     weights, parts, inners = exchange(
         6,
+        simple(scatter_plan),
         (weight.reshape(ROWS, 256, 128), part, inner),
         [((ROWS, 256, 128), BF16), ((4, 4, 2, 96, 128), BF16), ((4, 8, 128), F32)],
-        scatter_plan,
-        (37, 3),
+        37,
+        local=3,
     )
     out, weight_sum = compute(
         finish_kernel,
@@ -568,7 +704,7 @@
         weights,
         name="finish",
     )
-    (flat,) = exchange(7, (weight_sum,), [((ROWS, 256, 128), BF16)], spread_plan, (31, 1))
+    (flat,) = exchange(7, simple(spread_plan), (weight_sum,), [((ROWS, 256, 128), BF16)], 31, local=1)
     cell_scale = 1.0 / math.sqrt(32768)
     (grad_weights,) = compute(
         functools.partial(widen_kernel, cell_scale),

time: 290 us -> 244 us (0.84)
  Pallas kernels: 277 us -> 241 us
  local copies, waits for them, and re-layouts: 11.2 us -> 0.7 us
    pallas_call x8, Pallas kernels: 220 us -> 184 us  [exchange(): pl.pallas_call(kernel, out_shape=[jax.ShapeDtypeStruct(s, t) for s, t in...]
    reshape x3 -> x0, local copies, waits for them, and re-layouts: 10.5 us -> none  [on_device(): w_conv.reshape(3, 3, 3, 96, 384).transpose(0, 2, 4, 1, 3)]
where the time goes in v2:
time: 244 us; the launch traced here: 243 us
  Pallas kernels  241 us (99%)
    pallas_call x8, Pallas kernels, exchange(): pl.pallas_call(kernel, out_shape=[jax.ShapeDtypeStruct(s, t) for s, t in...  184 us
    pallas_call x8, Pallas kernels, compute(): pl.pallas_call(body, out_shape=[jax.ShapeDtypeStruct(s, t) for s, t in ou...  57.6 us

profile of v2, /device:TPU:8, one launch (start us, length us, event | category | flops | bytes accessed | tf_op | source)
XLA Modules:
  0.0 243.3 jit_solution(6633722887136129708)
XLA Ops:
  0.6 0.7 pad_maximum_fusion
  1.3 0.7 broadcast_in_dim.2.refs_2_.gain_own
  2.0 29.9 %exchange_0.1 = (bf16[4,4,2,96,128]{4,3,2,1,0:T(8,128)(2,1)}, bf16[4,4,96,128]{3,2,1,0:T(8,128)(2,1)}, bf16[4,4,96,128]{3,2,1,0:T(8,128)(2,1)}, bf16[4,2,96,128]...) custom-call(bf16[4,2,96,128]{3,2,1,0:T(8,128)(2,1)} %feat.3, ...), custom_call_target="tpu_custom_call" | custom-call | tf_op jit(solution)/shard_map/exchange_0/pallas_call | solution.py:86
  31.9 6.2 %conv.1 = (bf16[4,2,96,128]{3,2,1,0:T(8,128)(2,1)}, bf16[384,2048]{1,0:T(8,128)(2,1)}, f32[8,128]{1,0:T(8,128)}, bf16[384,256]{1,0:T(8,128)(2,1)}) custom-call(bf16[4,2,96,128]{3,2,1,0:T(8,128)(2,1)} %feat.3, bf16[4,4,2,96,128]{4,3,2,1,0:T(8,128)(2,1)} %get-tuple-element.36.all_feat, bf16[4,4,96,128]{3,2,1,0:T(8,128)(2,1)} %get-tuple-element.37.prev_feat, ...), custom_call_target="tpu_custom_call" | custom-call | tf_op jit(solution)/shard_map/conv/pallas_call | solution.py:121
  38.1 5.3 %exchange_1.1.res_frame = bf16[4,2,96,128]{3,2,1,0:T(8,128)(2,1)} custom-call(bf16[4,2,96,128]{3,2,1,0:T(8,128)(2,1)} %get-tuple-element.41.refs_0_), custom_call_target="tpu_custom_call" | custom-call | tf_op jit(solution)/shard_map/exchange_1/pallas_call | solution.py:86
  43.4 2.8 %project.1 = (bf16[384,256]{1,0:T(8,128)(2,1)}, bf16[256,384]{1,0:T(8,128)(2,1)}, bf16[256,384]{1,0:T(8,128)(2,1)}) custom-call(bf16[4,2,96,128]{3,2,1,0:T(8,128)(2,1)} %exchange_1.1.res_frame, bf16[4,2,96,128]{3,2,1,0:T(8,128)(2,1)} %get-tuple-element.39.gains, bf16[384,1152]{1,0:T(8,128)(2,1)} %w_qkv.3), custom_call_target="tpu_custom_call" | custom-call | tf_op jit(solution)/shard_map/project/pallas_call | solution.py:121
  46.1 25.4 %exchange_2.1 = (bf16[8,384,256]{2,1,0:T(8,128)(2,1)}, bf16[8,384,256]{2,1,0:T(8,128)(2,1)}, bf16[4,256,384]{2,1,0:T(8,128)(2,1)}, bf16[4,256,384]{2,1,0:T(8,128)(2,1)}) custom-call(bf16[384,256]{1,0:T(8,128)(2,1)} %get-tuple-element.42.refs_0_, bf16[384,256]{1,0:T(8,128)(2,1)} %get-tuple-element.43.refs_1_, bf16[256,384]{1,0:T(8,128)(2,1)} %get-tuple-element.44.refs_2_, ...), custom_call_target="tpu_custom_call" | custom-call | tf_op jit(solution)/shard_map/exchange_2/pallas_call | solution.py:86
  71.6 11.9 %stats.1.refs_0_ = f32[3,8,256]{2,1,0:T(8,128)} custom-call(bf16[8,384,256]{2,1,0:T(8,128)(2,1)} %get-tuple-element.46.q, bf16[8,384,256]{2,1,0:T(8,128)(2,1)} %get-tuple-element.47.g, bf16[4,256,384]{2,1,0:T(8,128)(2,1)} %get-tuple-element.48.k, bf16[4,256,384]{2,1,0:T(8,128)(2,1)} %get-tuple-element.49.v), custom_call_target="tpu_custom_call" | custom-call | tf_op jit(solution)/shard_map/stats/pallas_call | solution.py:121
  83.5 8.5 %exchange_3.1.stats = f32[8,3,8,256]{3,2,1,0:T(8,128)} custom-call(f32[3,8,256]{2,1,0:T(8,128)} %stats.1.refs_0_), custom_call_target="tpu_custom_call" | custom-call | tf_op jit(solution)/shard_map/exchange_3/pallas_call | solution.py:86
  92.0 16.4 %attn.1 = (bf16[8,384,256]{2,1,0:T(8,128)(2,1)}, bf16[4,256,384]{2,1,0:T(8,128)(2,1)}, bf16[4,256,384]{2,1,0:T(8,128)(2,1)}) custom-call(bf16[8,384,256]{2,1,0:T(8,128)(2,1)} %get-tuple-element.46.q, bf16[8,384,256]{2,1,0:T(8,128)(2,1)} %get-tuple-element.47.g, bf16[4,256,384]{2,1,0:T(8,128)(2,1)} %get-tuple-element.48.k, ...), custom_call_target="tpu_custom_call" | custom-call | tf_op jit(solution)/shard_map/attn/pallas_call | solution.py:121
  108.4 23.6 %exchange_4.1 = (bf16[8,384,256]{2,1,0:T(8,128)(2,1)}, bf16[4,256,384]{2,1,0:T(8,128)(2,1)}, bf16[4,256,384]{2,1,0:T(8,128)(2,1)}) custom-call(bf16[8,384,256]{2,1,0:T(8,128)(2,1)} %get-tuple-element.50.refs_0_, bf16[4,256,384]{2,1,0:T(8,128)(2,1)} %get-tuple-element.51.refs_1_, bf16[4,256,384]{2,1,0:T(8,128)(2,1)} %get-tuple-element.52.refs_2_), custom_call_target="tpu_custom_call" | custom-call | tf_op jit(solution)/shard_map/exchange_4/pallas_call | solution.py:86
  132.1 3.8 %residual.1.refs_0_ = bf16[4,2,96,128]{3,2,1,0:T(8,128)(2,1)} custom-call(bf16[8,384,256]{2,1,0:T(8,128)(2,1)} %get-tuple-element.53.dq, bf16[4,256,384]{2,1,0:T(8,128)(2,1)} %get-tuple-element.54.dk, bf16[4,256,384]{2,1,0:T(8,128)(2,1)} %get-tuple-element.55.dv, bf16[4,2,96,128]{3,2,1,0:T(8,128)(2,1)} %exchange_1.1.res_frame, ...), custom_call_target="tpu_custom_call" | custom-call | tf_op jit(solution)/shard_map/residual/pallas_call | solution.py:121
  135.8 10.4 %exchange_5.1 = (bf16[4,2,96,128]{3,2,1,0:T(8,128)(2,1)}, bf16[4,96,128]{2,1,0:T(8,128)(2,1)}, bf16[4,96,128]{2,1,0:T(8,128)(2,1)}) custom-call(bf16[4,2,96,128]{3,2,1,0:T(8,128)(2,1)} %residual.1.refs_0_), custom_call_target="tpu_custom_call" | custom-call | tf_op jit(solution)/shard_map/exchange_5/pallas_call | solution.py:86
  146.3 9.2 %grad.1 = (bf16[8192,128]{1,0:T(8,128)(2,1)}, bf16[4,4,2,96,128]{4,3,2,1,0:T(8,128)(2,1)}, f32[8,128]{1,0:T(8,128)}) custom-call(bf16[4,2,96,128]{3,2,1,0:T(8,128)(2,1)} %get-tuple-element.56.own, bf16[4,96,128]{2,1,0:T(8,128)(2,1)} %get-tuple-element.57.prev_g, bf16[4,96,128]{2,1,0:T(8,128)(2,1)} %get-tuple-element.58.next_g, ...), custom_call_target="tpu_custom_call" | custom-call | tf_op jit(solution)/shard_map/grad/pallas_call | solution.py:121
  155.5 40.9 %exchange_6.1 = (bf16[32,256,128]{2,1,0:T(8,128)(2,1)}, bf16[4,4,2,96,128]{4,3,2,1,0:T(8,128)(2,1)}, f32[4,8,128]{2,1,0:T(8,128)}) custom-call(bf16[32,256,128]{2,1,0:T(8,128)(2,1)} %bitcast.9, bf16[4,4,2,96,128]{4,3,2,1,0:T(8,128)(2,1)} %get-tuple-element.63.refs_1_, f32[8,128]{1,0:T(8,128)} %get-tuple-element.64.refs_2_), custom_call_target="tpu_custom_call" | custom-call | tf_op jit(solution)/shard_map/exchange_6/pallas_call | solution.py:86
  196.4 3.4 %finish.1 = (bf16[4,2,96,128]{3,2,1,0:T(8,128)(2,1)}, bf16[256,128]{1,0:T(8,128)(2,1)}) custom-call(bf16[4,2,96,128]{3,2,1,0:T(8,128)(2,1)} %feat.3, bf16[4,2,96,128]{3,2,1,0:T(8,128)(2,1)} %get-tuple-element.56.own, bf16[4,4,2,96,128]{4,3,2,1,0:T(8,128)(2,1)} %get-tuple-element.65.part, f32[4,8,128]{2,1,0:T(8,128)} %get-tuple-element.66.inner, ...), custom_call_target="tpu_custom_call" | custom-call | tf_op jit(solution)/shard_map/finish/pallas_call | solution.py:121
  199.8 39.7 %exchange_7.1 = bf16[32,256,128]{2,1,0:T(8,128)(2,1)} custom-call(bf16[256,128]{1,0:T(8,128)(2,1)} %get-tuple-element.69.refs_0_), custom_call_target="tpu_custom_call" | custom-call | tf_op jit(solution)/shard_map/exchange_7/pallas_call | solution.py:86
  239.5 3.8 %widen.1 = f32[2592,384]{1,0:T(8,128)} custom-call(bf16[8192,128]{1,0:T(8,128)(2,1)} %bitcast.6), custom_call_target="tpu_custom_call" | custom-call | tf_op jit(solution)/shard_map/widen/pallas_call | solution.py:121

commit v3 on v2

--- a/solution.py
+++ b/solution.py
@@ -98,6 +98,25 @@
         ),
         name="exchange_%d" % cid,
     )(*ins, *held)
+
+
+def fused(cid, body, held, made, scratch, count):
+    def kernel(*refs):
+        n_in, n_out = len(held), len(held) + len(made)
+        send, recv = refs[-2:]
+        body(Links(send, recv), refs[:n_in], refs[n_in:n_out], refs[n_out:-2])
+
+    return pl.pallas_call(
+        kernel,
+        out_shape=[jax.ShapeDtypeStruct(s, t) for s, t, _ in made],
+        in_specs=[pl.BlockSpec(memory_space=pltpu.VMEM)] * len(held),
+        out_specs=[pl.BlockSpec(memory_space=m) for _, _, m in made],
+        scratch_shapes=list(scratch) + [pltpu.SemaphoreType.DMA((count,))] * 2,
+        compiler_params=pltpu.CompilerParams(
+            collective_id=cid, has_side_effects=True, vmem_limit_bytes=VMEM_BYTES
+        ),
+        name="fused_%d" % cid,
+    )(*held)
 
 
 def simple(plan):
@@ -334,36 +353,6 @@
     links.finish()
 
 
-def row_peers(r, c):
-    return [(lax.rem(r + d, ROWS), c) for d in range(1, ROWS)]
-
-
-def scatter_plan(srcs, dsts):
-    weight, part, inner = srcs
-    all_weight, all_part, all_inner = dsts
-    r, c = coords()
-    remote, peers = [], []
-    for to in ch_peers(r, c):
-        remote += [(part.at[to[1]], all_part.at[c], to), (inner, all_inner.at[c], to)]
-        peers.append(to)
-    for to in row_peers(r, c):
-        remote.append((weight.at[to[0]], all_weight.at[r], to))
-        peers.append(to)
-    local = [
-        (part.at[c], all_part.at[c]),
-        (inner, all_inner.at[c]),
-        (weight.at[r], all_weight.at[r]),
-    ]
-    return remote, local, peers
-
-
-def spread_plan(srcs, dsts):
-    (own,), (every,) = srcs, dsts
-    r, c = coords()
-    peers = row_peers(r, c)
-    return [(own, every.at[r], to) for to in peers], [(own, every.at[r])], peers
-
-
 def sigmoid(v):
     return 1.0 / (1.0 + jnp.exp(-v))
 
@@ -493,13 +482,23 @@
             grad[b, h] = out[96 * b : 96 * b + 96, 128 * h : 128 * h + 128].astype(BF16)
 
 
-def grad_kernel(own, prev_g, next_g, act, w_t, all_feat, inv_in, gains, weight, part, inner, rows, lines):
-    r = lax.axis_index("row")
-    for f in range(4):
-        rows[f, 0] = jnp.where(r == 0, 0.0, prev_g[f].astype(F32)).astype(BF16)
-        rows[f, 1] = own[f, 0]
-        rows[f, 2] = own[f, 1]
-        rows[f, 3] = jnp.where(r == ROWS - 1, 0.0, next_g[f].astype(F32)).astype(BF16)
+def tail_kernel(links, held, made, scratch):
+    own, prev_g, next_g, act, w_t, all_feat, inv_in, gains, feat, gain_own = held
+    out, flat = made
+    rows, lines, weight, part, all_part, inner, all_inner, came1, came2, came3, sum1, sum2, sum3, mark = scratch
+    r, c = coords()
+    x, y_hi, z, y_lo, core = place(r, c)
+    xs = [device(lax.rem(x + d, 4), y_hi, z, y_lo, core) for d in range(1, 4)]
+    zs = [device(x, y_hi, lax.rem(z + d, 4), y_lo, core) for d in range(1, 4)]
+    x_at = [lax.rem(x + d, 4) for d in range(1, 4)]
+    z_at = [lax.rem(z + d, 4) for d in range(1, 4)]
+    across = device(x, 1 - y_hi, z, y_lo, core)
+    chs = ch_peers(r, c)
+    halves = (
+        (x, xs, x_at, z, zs, z_at),
+        (z, zs, z_at, x, xs, x_at),
+    )
+    links.greet(xs + zs + [across] + chs, 10)
     moved = []
     for f in range(4):
         both = []
@@ -519,6 +518,16 @@
                 at = (3 * (3 * t + h) + lane) * 288
                 weight[pl.ds(at, 288), :] = acc[:, 128 * lane : 128 * lane + 128].astype(BF16)
     weight[pl.ds(27 * 288, 416), :] = jnp.zeros((416, 128), BF16)
+    first = []
+    for half, (a, peers, ats, _, _, _) in enumerate(halves):
+        for d in range(3):
+            src = weight.at[pl.ds(4096 * half + 1024 * ats[d], 1024)]
+            first.append(links.copy(src, came1.at[half, d], peers[d]))
+    for f in range(4):
+        rows[f, 0] = jnp.where(r == 0, 0.0, prev_g[f].astype(F32)).astype(BF16)
+        rows[f, 1] = own[f, 0]
+        rows[f, 2] = own[f, 1]
+        rows[f, 3] = jnp.where(r == ROWS - 1, 0.0, next_g[f].astype(F32)).astype(BF16)
     for f in range(4):
         for h in range(3):
             for k in range(2):
@@ -533,40 +542,88 @@
             acc += dot(w_t[t], lines[source])
         for h in range(2):
             y = acc[:, 128 * h : 128 * h + 128]
-            out = move(y[:384], -1) + y[384:768] + move(y[768:], 1)
-            x = jnp.concatenate([all_feat[b, f, h] for b in range(CH)], 0).astype(F32)
-            before = x * inv_in[2 * f + h : 2 * f + h + 1, :] * gain
+            total = move(y[:384], -1) + y[384:768] + move(y[768:], 1)
+            v = jnp.concatenate([all_feat[b, f, h] for b in range(CH)], 0).astype(F32)
+            before = v * inv_in[2 * f + h : 2 * f + h + 1, :] * gain
             sig = sigmoid(before)
             slope = sig * (1.0 + before * (1.0 - sig))
-            inner[2 * f + h : 2 * f + h + 1, :] = jnp.sum(x * slope * gain * out, 0, keepdims=True)
+            inner[2 * f + h : 2 * f + h + 1, :] = jnp.sum(v * slope * gain * total, 0, keepdims=True)
             for b in range(CH):
-                part[b, f, h] = out[96 * b : 96 * b + 96].astype(BF16)
-
-
-def finish_kernel(feat, own, part, inner, inv_in, gain_own, weights, out, weight):
-    total = total_of(weights, ROWS)
-    weight[...] = total.astype(BF16)
-    mean = (inner[0] + inner[1] + inner[2] + inner[3]) / 384.0
+                part[b, f, h] = total[96 * b : 96 * b + 96].astype(BF16)
+    parts = []
+    for d in range(3):
+        parts.append(links.copy(part.at[chs[d][1]], all_part.at[d], chs[d]))
+        parts.append(links.copy(inner, all_inner.at[d], chs[d]))
+    for copy in first:
+        copy.wait_recv()
+    second = []
+    for half, (a, _, _, b, peers, ats) in enumerate(halves):
+        total = weight[pl.ds(4096 * half + 1024 * a, 1024), :].astype(F32)
+        for d in range(3):
+            total += came1[half, d].astype(F32)
+        sum1[half] = total.astype(BF16)
+        for d in range(3):
+            src = sum1.at[half, pl.ds(256 * ats[d], 256)]
+            second.append(links.copy(src, came2.at[half, d], peers[d]))
+    for copy in second:
+        copy.wait_recv()
+    third = []
+    for half, (a, _, _, b, _, _) in enumerate(halves):
+        total = sum1[half, pl.ds(256 * b, 256), :].astype(F32)
+        for d in range(3):
+            total += came2[half, d].astype(F32)
+        sum2[half] = total.astype(BF16)
+        src = sum2.at[half, pl.ds(128 * (1 - y_hi), 128)]
+        third.append(links.copy(src, came3.at[half], across))
+    for copy in third:
+        copy.wait_recv()
+    fourth, kept = [], []
+    for half, (a, _, _, b, _, _) in enumerate(halves):
+        total = sum2[half, pl.ds(128 * y_hi, 128), :].astype(F32) + came3[half].astype(F32)
+        sum3[half] = total.astype(BF16)
+        at = flat.at[pl.ds(4096 * half + 1024 * a + 256 * b + 128 * y_hi, 128)]
+        kept.append(pltpu.make_async_copy(sum3.at[half], at, mark.at[half]))
+        kept[half].start()
+        fourth.append(links.copy(sum3.at[half], at, across))
+    fifth = []
+    for half, (a, _, _, b, peers, _) in enumerate(halves):
+        kept[half].wait()
+        fourth[half].wait_recv()
+        at = flat.at[pl.ds(4096 * half + 1024 * a + 256 * b, 256)]
+        for d in range(3):
+            fifth.append(links.copy(at, at, peers[d]))
+    sixth = []
+    for half, (a, peers, _, _, _, _) in enumerate(halves):
+        for d in range(3):
+            fifth[3 * half + d].wait_recv()
+        at = flat.at[pl.ds(4096 * half + 1024 * a, 1024)]
+        for d in range(3):
+            sixth.append(links.copy(at, at, peers[d]))
+    for copy in parts:
+        copy.wait_recv()
+    mean = (inner[...] + all_inner[0] + all_inner[1] + all_inner[2]) / 384.0
     gain = gain_own[0].astype(F32)
     for f in range(4):
         for h in range(2):
-            x = feat[f, h].astype(F32)
+            v = feat[f, h].astype(F32)
             inv = inv_in[2 * f + h : 2 * f + h + 1, :]
-            act = part[0, f, h].astype(F32)
-            for b in range(1, CH):
-                act += part[b, f, h].astype(F32)
-            before = x * inv * gain
+            total = part[c, f, h].astype(F32)
+            for d in range(3):
+                total += all_part[d, f, h].astype(F32)
+            before = v * inv * gain
             sig = sigmoid(before)
-            scaled = act * (sig * (1.0 + before * (1.0 - sig))) * gain
+            scaled = total * (sig * (1.0 + before * (1.0 - sig))) * gain
             cube = inv * inv * inv * mean[2 * f + h : 2 * f + h + 1, :]
-            out[f, h] = (own[f, h].astype(F32) + inv * scaled - x * cube).astype(BF16)
+            out[f, h] = (own[f, h].astype(F32) + inv * scaled - v * cube).astype(BF16)
+    for copy in sixth:
+        copy.wait_recv()
+    links.finish()
 
 
 def widen_kernel(scale, flat, out):
-    for k in range(9):
-        for lane in range(3):
-            piece = flat[pl.ds((3 * k + lane) * 288, 288), :].astype(F32) * scale
-            out[pl.ds(288 * k, 288), pl.ds(128 * lane, 128)] = piece
+    for lane in range(3):
+        piece = flat[pl.ds(288 * lane, 288), :].astype(F32) * scale
+        out[:, pl.ds(128 * lane, 128)] = piece
 
 
 def on_device(features, gain_in, w_conv, gain_attn, w_qkv, w_out, cotangent):
@@ -670,48 +727,38 @@
         [((4, 2, 96, 128), BF16), ((4, 96, 128), BF16), ((4, 96, 128), BF16)],
         12,
     )
-    weight, part, inner = compute(
-        grad_kernel,
-        [((8192, 128), BF16), ((4, 4, 2, 96, 128), BF16), ((8, 128), F32)],
-        own,
-        prev_g,
-        next_g,
-        act,
-        w_t,
-        all_feat,
-        inv_in,
-        gains,
-        scratch=[pltpu.VMEM((4, 4, 96, 128), BF16), pltpu.VMEM((4, 288, 256), BF16)],
-        name="grad",
-    )
-    weights, parts, inners = exchange(
+    out, flat = fused(
         6,
-        simple(scatter_plan),
-        (weight.reshape(ROWS, 256, 128), part, inner),
-        [((ROWS, 256, 128), BF16), ((4, 4, 2, 96, 128), BF16), ((4, 8, 128), F32)],
-        37,
-        local=3,
-    )
-    out, weight_sum = compute(
-        finish_kernel,
-        [((4, 2, 96, 128), BF16), ((256, 128), BF16)],
-        features,
-        own,
-        parts,
-        inners,
-        inv_in,
-        gain_own,
-        weights,
-        name="finish",
-    )
-    (flat,) = exchange(7, simple(spread_plan), (weight_sum,), [((ROWS, 256, 128), BF16)], 31, local=1)
+        tail_kernel,
+        (own, prev_g, next_g, act, w_t, all_feat, inv_in, gains, features, gain_own),
+        [((4, 2, 96, 128), BF16, pltpu.VMEM), ((8192, 128), BF16, pl.ANY)],
+        [
+            pltpu.VMEM((4, 4, 96, 128), BF16),
+            pltpu.VMEM((4, 288, 256), BF16),
+            pltpu.VMEM((8192, 128), BF16),
+            pltpu.VMEM((4, 4, 2, 96, 128), BF16),
+            pltpu.VMEM((3, 4, 2, 96, 128), BF16),
+            pltpu.VMEM((8, 128), F32),
+            pltpu.VMEM((3, 8, 128), F32),
+            pltpu.VMEM((2, 3, 1024, 128), BF16),
+            pltpu.VMEM((2, 3, 256, 128), BF16),
+            pltpu.VMEM((2, 128, 128), BF16),
+            pltpu.VMEM((2, 1024, 128), BF16),
+            pltpu.VMEM((2, 256, 128), BF16),
+            pltpu.VMEM((2, 128, 128), BF16),
+            pltpu.SemaphoreType.DMA((2,)),
+        ],
+        34,
+    )
     cell_scale = 1.0 / math.sqrt(32768)
-    (grad_weights,) = compute(
+    grad_weights = pl.pallas_call(
         functools.partial(widen_kernel, cell_scale),
-        [((2592, 384), F32)],
-        flat.reshape(8192, 128),
+        grid=(9,),
+        out_shape=jax.ShapeDtypeStruct((2592, 384), F32),
+        in_specs=[pl.BlockSpec((864, 128), lambda i: (i, 0))],
+        out_specs=pl.BlockSpec((288, 384), lambda i: (i, 0)),
         name="widen",
-    )
+    )(flat)
     return out, grad_weights.reshape(27, 96, 384)
 
 

time: 244 us -> 207 us (0.85)
  Pallas kernels: 241 us -> 203 us
    pallas_call x8 -> x6, Pallas kernels: 184 us -> 103 us  [exchange(): pl.pallas_call(kernel, out_shape=[jax.ShapeDtypeStruct(s, t) for s, t in...]
    pallas_call x0 -> x2, Pallas kernels: none -> 58.3 us  [the longest x1 51.8 us: fused(): pl.pallas_call(kernel, out_shape=[jax.ShapeDtypeStruct(s, t) for s, t, _...]
    pallas_call x8 -> x5, Pallas kernels: 57.6 us -> 41.2 us  [compute(): pl.pallas_call(body, out_shape=[jax.ShapeDtypeStruct(s, t) for s, t in ou...]
where the time goes in v3:
time: 207 us; the launch traced here: 205 us
  Pallas kernels  203 us (98%)
    pallas_call x6, Pallas kernels, exchange(): pl.pallas_call(kernel, out_shape=[jax.ShapeDtypeStruct(s, t) for s, t in...  103 us
    pallas_call x1, Pallas kernels, fused(): pl.pallas_call(kernel, out_shape=[jax.ShapeDtypeStruct(s, t) for s, t, _...  51.8 us
    pallas_call x5, Pallas kernels, compute(): pl.pallas_call(body, out_shape=[jax.ShapeDtypeStruct(s, t) for s, t in ou...  41.2 us
    pallas_call x1, Pallas kernels, on_device(): pl.pallas_call(functools.partial(widen_kernel, cell_scale), grid=(9,), ou...  6.55 us

profile of v3, /device:TPU:8, one launch (start us, length us, event | category | flops | bytes accessed | tf_op | source)
XLA Modules:
  0.0 205.4 jit_solution(17514723242695512542)
XLA Ops:
  0.6 0.7 pad_maximum_fusion
  1.3 0.7 broadcast_in_dim.2.refs_2_.refs_9_
  2.0 29.9 %exchange_0.1 = (bf16[4,4,2,96,128]{4,3,2,1,0:T(8,128)(2,1)}, bf16[4,4,96,128]{3,2,1,0:T(8,128)(2,1)}, bf16[4,4,96,128]{3,2,1,0:T(8,128)(2,1)}, bf16[4,2,96,128]...) custom-call(bf16[4,2,96,128]{3,2,1,0:T(8,128)(2,1)} %refs_8_.1, ...), custom_call_target="tpu_custom_call" | custom-call | tf_op jit(solution)/shard_map/exchange_0/pallas_call | solution.py:86
  32.0 6.2 %conv.1 = (bf16[4,2,96,128]{3,2,1,0:T(8,128)(2,1)}, bf16[384,2048]{1,0:T(8,128)(2,1)}, f32[8,128]{1,0:T(8,128)}, bf16[384,256]{1,0:T(8,128)(2,1)}) custom-call(bf16[4,2,96,128]{3,2,1,0:T(8,128)(2,1)} %refs_8_.1, bf16[4,4,2,96,128]{4,3,2,1,0:T(8,128)(2,1)} %get-tuple-element.30.all_feat.refs_5_, bf16[4,4,96,128]{3,2,1,0:T(8,128)(2,1)} %get-tuple-element.31.prev_feat, ...), custom_call_target="tpu_custom_call" | custom-call | tf_op jit(solution)/shard_map/conv/pallas_call | solution.py:140
  38.1 5.3 %exchange_1.1.res_frame = bf16[4,2,96,128]{3,2,1,0:T(8,128)(2,1)} custom-call(bf16[4,2,96,128]{3,2,1,0:T(8,128)(2,1)} %get-tuple-element.35.refs_0_), custom_call_target="tpu_custom_call" | custom-call | tf_op jit(solution)/shard_map/exchange_1/pallas_call | solution.py:86
  43.4 2.8 %project.1 = (bf16[384,256]{1,0:T(8,128)(2,1)}, bf16[256,384]{1,0:T(8,128)(2,1)}, bf16[256,384]{1,0:T(8,128)(2,1)}) custom-call(bf16[4,2,96,128]{3,2,1,0:T(8,128)(2,1)} %exchange_1.1.res_frame, bf16[4,2,96,128]{3,2,1,0:T(8,128)(2,1)} %get-tuple-element.33.gains.refs_7_, bf16[384,1152]{1,0:T(8,128)(2,1)} %w_qkv.3), custom_call_target="tpu_custom_call" | custom-call | tf_op jit(solution)/shard_map/project/pallas_call | solution.py:140
  46.2 25.4 %exchange_2.1 = (bf16[8,384,256]{2,1,0:T(8,128)(2,1)}, bf16[8,384,256]{2,1,0:T(8,128)(2,1)}, bf16[4,256,384]{2,1,0:T(8,128)(2,1)}, bf16[4,256,384]{2,1,0:T(8,128)(2,1)}) custom-call(bf16[384,256]{1,0:T(8,128)(2,1)} %get-tuple-element.36.refs_0_, bf16[384,256]{1,0:T(8,128)(2,1)} %get-tuple-element.37.refs_1_, bf16[256,384]{1,0:T(8,128)(2,1)} %get-tuple-element.38.refs_2_, ...), custom_call_target="tpu_custom_call" | custom-call | tf_op jit(solution)/shard_map/exchange_2/pallas_call | solution.py:86
  71.6 12.0 %stats.1.refs_0_ = f32[3,8,256]{2,1,0:T(8,128)} custom-call(bf16[8,384,256]{2,1,0:T(8,128)(2,1)} %get-tuple-element.40.q, bf16[8,384,256]{2,1,0:T(8,128)(2,1)} %get-tuple-element.41.g, bf16[4,256,384]{2,1,0:T(8,128)(2,1)} %get-tuple-element.42.k, bf16[4,256,384]{2,1,0:T(8,128)(2,1)} %get-tuple-element.43.v), custom_call_target="tpu_custom_call" | custom-call | tf_op jit(solution)/shard_map/stats/pallas_call | solution.py:140
  83.6 8.5 %exchange_3.1.stats = f32[8,3,8,256]{3,2,1,0:T(8,128)} custom-call(f32[3,8,256]{2,1,0:T(8,128)} %stats.1.refs_0_), custom_call_target="tpu_custom_call" | custom-call | tf_op jit(solution)/shard_map/exchange_3/pallas_call | solution.py:86
  92.0 16.5 %attn.1 = (bf16[8,384,256]{2,1,0:T(8,128)(2,1)}, bf16[4,256,384]{2,1,0:T(8,128)(2,1)}, bf16[4,256,384]{2,1,0:T(8,128)(2,1)}) custom-call(bf16[8,384,256]{2,1,0:T(8,128)(2,1)} %get-tuple-element.40.q, bf16[8,384,256]{2,1,0:T(8,128)(2,1)} %get-tuple-element.41.g, bf16[4,256,384]{2,1,0:T(8,128)(2,1)} %get-tuple-element.42.k, ...), custom_call_target="tpu_custom_call" | custom-call | tf_op jit(solution)/shard_map/attn/pallas_call | solution.py:140
  108.5 23.6 %exchange_4.1 = (bf16[8,384,256]{2,1,0:T(8,128)(2,1)}, bf16[4,256,384]{2,1,0:T(8,128)(2,1)}, bf16[4,256,384]{2,1,0:T(8,128)(2,1)}) custom-call(bf16[8,384,256]{2,1,0:T(8,128)(2,1)} %get-tuple-element.44.refs_0_, bf16[4,256,384]{2,1,0:T(8,128)(2,1)} %get-tuple-element.45.refs_1_, bf16[4,256,384]{2,1,0:T(8,128)(2,1)} %get-tuple-element.46.refs_2_), custom_call_target="tpu_custom_call" | custom-call | tf_op jit(solution)/shard_map/exchange_4/pallas_call | solution.py:86
  132.1 3.8 %residual.1.refs_0_ = bf16[4,2,96,128]{3,2,1,0:T(8,128)(2,1)} custom-call(bf16[8,384,256]{2,1,0:T(8,128)(2,1)} %get-tuple-element.47.dq, bf16[4,256,384]{2,1,0:T(8,128)(2,1)} %get-tuple-element.48.dk, bf16[4,256,384]{2,1,0:T(8,128)(2,1)} %get-tuple-element.49.dv, bf16[4,2,96,128]{3,2,1,0:T(8,128)(2,1)} %exchange_1.1.res_frame, ...), custom_call_target="tpu_custom_call" | custom-call | tf_op jit(solution)/shard_map/residual/pallas_call | solution.py:140
  135.9 10.4 %exchange_5.1 = (bf16[4,2,96,128]{3,2,1,0:T(8,128)(2,1)}, bf16[4,96,128]{2,1,0:T(8,128)(2,1)}, bf16[4,96,128]{2,1,0:T(8,128)(2,1)}) custom-call(bf16[4,2,96,128]{3,2,1,0:T(8,128)(2,1)} %residual.1.refs_0_), custom_call_target="tpu_custom_call" | custom-call | tf_op jit(solution)/shard_map/exchange_5/pallas_call | solution.py:86
  146.4 51.8 %fused_6.1 = (bf16[4,2,96,128]{3,2,1,0:T(8,128)(2,1)}, bf16[8192,128]{1,0:T(8,128)(2,1)}) custom-call(bf16[4,2,96,128]{3,2,1,0:T(8,128)(2,1)} %get-tuple-element.50.refs_0_, bf16[4,96,128]{2,1,0:T(8,128)(2,1)} %get-tuple-element.51.refs_1_, bf16[4,96,128]{2,1,0:T(8,128)(2,1)} %get-tuple-element.52.refs_2_, bf16[384,2048]{1,0:T(8,128)(2,1)} %get-tuple-element.53.refs_3_, ...), custom_call_target="tpu_custom_call" | custom-call | tf_op jit(solution)/shard_map/fused_6/pallas_call | solution.py:109
  198.1 0.0 copy-start
  198.2 6.6 %widen.1 = f32[2592,384]{1,0:T(8,128)} custom-call(bf16[8192,128]{1,0:T(8,128)(2,1)} %get-tuple-element.57.flat), custom_call_target="tpu_custom_call" | custom-call | tf_op jit(solution)/shard_map/widen/pallas_call | solution.py:754
  204.7 0.0 copy-done
  204.7 0.7 copy.10
Async XLA Ops:
  198.1 6.6 %copy-start = (bf16[4,2,96,128]{3,2,1,0:T(8,128)(2,1)S(1)}, bf16[4,2,96,128]{3,2,1,0:T(8,128)(2,1)}, u32[]{:S(2)}) copy-start(bf16[4,2,96,128]{3,2,1,0:T(8,128)(2,1)} %get-tuple-element.60) | copy-start | bytes 589828

commit v4 on v3

--- a/solution.py
+++ b/solution.py
@@ -240,119 +240,6 @@
     links.finish()
 
 
-def key_peers(r, c):
-    return [(lax.rem(r + 8 * d, ROWS), c) for d in range(1, 4)]
-
-
-def query_peers(r, c):
-    x, y_hi, z, y_lo, core = place(r, c)
-    found = []
-    for dk in range(2):
-        for dx in range(4):
-            if dk or dx:
-                found.append(device(lax.rem(x + dx, 4), y_hi, z, y_lo, lax.rem(core + dk, 2)))
-    return found
-
-
-def gather_body(links, own, srcs, dsts):
-    q, g, k, v = srcs
-    all_q, all_g, all_k, all_v = dsts
-    r, c = coords()
-    x, y_hi, z, y_lo, core = place(r, c)
-    slot = core * 4 + x
-    local = [(q, all_q.at[slot]), (g, all_g.at[slot]), (k, all_k.at[z]), (v, all_v.at[z])]
-    here = [pltpu.make_async_copy(s, d, own.at[i]) for i, (s, d) in enumerate(local)]
-    for copy in here:
-        copy.start()
-    sibling = (r, y_lo * 2 + 1 - core)
-    x_next, x_back = lax.rem(x + 1, 4), lax.rem(x + 3, 4)
-    z_next, z_back = lax.rem(z + 1, 4), lax.rem(z + 3, 4)
-    xs = [device(i, y_hi, z, y_lo, core) for i in (x_next, x_back)]
-    zs = [device(x, y_hi, i, y_lo, core) for i in (z_next, z_back)]
-    links.greet(xs + zs + [sibling], 5)
-    pairs = ((q, all_q, core * 4, x, xs), (g, all_g, core * 4, x, xs), (k, all_k, 0, z, zs), (v, all_v, 0, z, zs))
-    first = []
-    for src, dst, base, i, to in pairs:
-        first.append([links.copy(src, dst.at[base + i], peer) for peer in to])
-    relayed = []
-    for src, dst in ((q, all_q), (g, all_g)):
-        relayed.append(links.copy(src, dst.at[slot], sibling))
-    for n in (0, 2, 1, 3):
-        src, dst, base, i, to = pairs[n]
-        half = src.shape[0] // 2
-        for side in range(2):
-            first[n][side].wait_recv()
-            came = base + lax.rem(i + 3 - 2 * side, 4)
-            part = dst.at[came, pl.ds(half * side, half)]
-            relayed.append(links.copy(part, part, to[side]))
-            if n < 2:
-                relayed.append(links.copy(dst.at[came], dst.at[came], sibling))
-    far = relayed[2:]
-    for n, dst in ((0, all_q), (6, all_g)):
-        at = core * 4 + lax.rem(x + 2, 4)
-        far[n].wait_recv()
-        far[n + 2].wait_recv()
-        relayed.append(links.copy(dst.at[at], dst.at[at], sibling))
-    for n, copy in enumerate(relayed):
-        if n - 2 not in (0, 2, 6, 8):
-            copy.wait_recv()
-    for copy in here:
-        copy.wait()
-    links.finish()
-
-
-def stats_plan(srcs, dsts):
-    (own,), (every,) = srcs, dsts
-    r, c = coords()
-    x, y_hi, z, y_lo, core = place(r, c)
-    slot = core * 4 + x
-    peers = query_peers(r, c)
-    return [(own, every.at[slot], to) for to in peers], [(own, every.at[slot])], peers
-
-
-def back_plan(srcs, dsts):
-    dq, dk, dv = srcs
-    all_q, all_k, all_v = dsts
-    r, c = coords()
-    x, y_hi, z, y_lo, core = place(r, c)
-    slot = core * 4 + x
-    remote, peers = [], []
-    for to in query_peers(r, c):
-        there = lax.rem(to[1], 2) * 4 + lax.rem(to[0], 4)
-        remote.append((dq.at[there], all_q.at[slot], to))
-        peers.append(to)
-    for to in key_peers(r, c):
-        at = to[0] // 8
-        remote += [(dk.at[at], all_k.at[z], to), (dv.at[at], all_v.at[z], to)]
-        peers.append(to)
-    local = [(dq.at[slot], all_q.at[slot]), (dk.at[z], all_k.at[z]), (dv.at[z], all_v.at[z])]
-    return remote, local, peers
-
-
-def grad_body(links, own, srcs, dsts):
-    (g,), (mine, prev_g, next_g) = srcs, dsts
-    r, c = coords()
-    x, y_hi, z, y_lo, core = place(r, c)
-    frame = y_hi * 2 + y_lo
-    row = z * 8 + core * 4 + x
-    row_low, row_high = near_rows(row)
-    low, high = near_rows(r)
-    targets = [(row, b) for b in range(CH)]
-    around = [(i, b) for i in (row_low, row_high) for b in range(CH)]
-    sources = [owner(f, i) for i in (r, low, high) for f in range(4)]
-    greet_frames(links, (r, c), sources, targets + around)
-    for b in range(CH):
-        links.copy(g.at[b], mine.at[frame], (row, b), own=same((row, b), (r, c)), recv=frame)
-    for b in range(CH):
-        links.copy(g.at[b, 1], prev_g.at[frame], (row_high, b), recv=4 + frame)
-        links.copy(g.at[b, 0], next_g.at[frame], (row_low, b), recv=8 + frame)
-    for f in range(4):
-        links.arrive(mine.at[f], f)
-        links.arrive(prev_g.at[f], 4 + f)
-        links.arrive(next_g.at[f], 8 + f)
-    links.finish()
-
-
 def sigmoid(v):
     return 1.0 / (1.0 + jnp.exp(-v))
 
@@ -403,83 +290,203 @@
     return x, lax.rsqrt(jnp.mean(x * x, 0, keepdims=True) + EPSILON)
 
 
-def project_kernel(res_frame, gains, w_qkv, q, k, v, full):
+def attn_body(scale, links, held, made, scratch):
+    res_frame, cot, gains, w_qkv, grad_o = held
+    mine, prev_g, next_g = made
+    (full, cot_full, q, g, k, v, k_t, exps, grad_p, grad_s, prob_row, tops, sums, deltas, stats, all_stats, weights, delta,
+     send_k, send_v, came_k, came_v, own_k, own_v, sib_out, sib_in, send_q, came_q, own_q, grad) = scratch
+    r, c = coords()
+    x, y_hi, z, y_lo, core = place(r, c)
+    slot = core * 4 + x
+    frame = y_hi * 2 + y_lo
+    sibling = (r, y_lo * 2 + 1 - core)
+    xs = [device(lax.rem(x + d, 4), y_hi, z, y_lo, core) for d in range(1, 4)]
+    cross = [device(lax.rem(x + d, 4), y_hi, z, y_lo, 1 - core) for d in range(1, 4)]
+    zs = [device(x, y_hi, lax.rem(z + d, 4), y_lo, core) for d in range(1, 4)]
+    row = z * 8 + core * 4 + x
+    row_low, row_high = near_rows(row)
+    low, high = near_rows(r)
+    around = [(i, b) for i in (row_low, row_high) for b in range(CH)]
+    alike = xs + zs + cross + [sibling]
+    sources = [owner(f, i) for i in (r, low, high) for f in range(4)]
+    greet_frames(links, (r, c), sources + alike, [(row, b) for b in range(CH)] + around + alike)
+
+    g[slot] = grad_o[...]
+    g_first = [links.copy(g.at[slot], g.at[slot], to) for to in (xs[0], xs[2], sibling)]
     gain = jnp.concatenate([gains[b, 1] for b in range(CH)], 0).astype(F32)
     gain = jnp.concatenate([gain, gain], 1)
-    x, inv = attn_norm(res_frame, full)
-    normed = (x * inv * gain).astype(BF16).astype(F32)
-    out = dot(normed.T.astype(BF16), w_qkv[...])
-    q[...] = out[:, :384].T.astype(BF16)
-    k[...] = out[:, 384:768].astype(BF16)
-    v[...] = out[:, 768:].astype(BF16)
-
-
-def stats_kernel(scale, q, g, k, v, stats):
-    keys, values = k[...].reshape(1024, 384), v[...].reshape(1024, 384)
-
-    def step(b, carry):
-        s = dot(keys, q[b]) * scale
-        m = jnp.max(s, 0, keepdims=True)
-        e = jnp.exp(s - m)
-        stats[0, pl.ds(b, 1), :] = m
-        stats[1, pl.ds(b, 1), :] = jnp.sum(e, 0, keepdims=True)
-        stats[2, pl.ds(b, 1), :] = jnp.sum(e * dot(values, g[b]), 0, keepdims=True)
-        return carry
-
-    lax.fori_loop(0, 8, step, 0)
-
-
-def attn_kernel(scale, q, g, k, v, stats, dq, dk, dv, acc_k, acc_v):
-    keys, values = k[...].reshape(1024, 384), v[...].reshape(1024, 384)
-    keys_t = keys.T
-    acc_k[...] = jnp.zeros_like(acc_k)
-    acc_v[...] = jnp.zeros_like(acc_v)
-
-    def step(b, carry):
-        part = [[stats[i, n, pl.ds(b, 1), :] for n in range(3)] for i in range(8)]
-        top = functools.reduce(jnp.maximum, [p[0] for p in part])
-        shift = [jnp.exp(p[0] - top) for p in part]
-        total = sum(p[1] * w for p, w in zip(part, shift))
-        delta = sum(p[2] * w for p, w in zip(part, shift)) / total
-        offset = top + jnp.log(total)
-        prob = jnp.exp(dot(keys, q[b]) * scale - offset)
-        grad_s = (prob * (dot(values, g[b]) - delta)).astype(BF16)
-        acc_v[...] += dot_t(prob.astype(BF16), g[b])
-        acc_k[...] += dot_t(grad_s, q[b])
-        dq[b] = (dot(keys_t, grad_s) * scale).astype(BF16)
-        return carry
-
-    lax.fori_loop(0, 8, step, 0)
-    dk[...] = (acc_k[...] * scale).astype(BF16).reshape(4, 256, 384)
-    dv[...] = acc_v[...].astype(BF16).reshape(4, 256, 384)
-
-
-def total_of(ref, count):
-    total = ref[0].astype(F32)
-    for i in range(1, count):
-        total += ref[i].astype(F32)
-    return total
-
-
-def residual_kernel(dq, dk, dv, res_frame, cot, gains, w_qkv, grad, full, cot_full):
-    gain = jnp.concatenate([gains[b, 1] for b in range(CH)], 0).astype(F32)
-    gain = jnp.concatenate([gain, gain], 1)
-    x, inv = attn_norm(res_frame, full)
+    centre, inv = attn_norm(res_frame, full)
+    normed = (centre * inv * gain).astype(BF16).astype(F32).T.astype(BF16)
+    k[z] = dot(normed, w_qkv[:, 384:768]).astype(BF16)
+    k_first = [links.copy(k.at[z], k.at[z], to) for to in (zs[0], zs[2])]
+    v[z] = dot(normed, w_qkv[:, 768:]).astype(BF16)
+    v_first = [links.copy(v.at[z], v.at[z], to) for to in (zs[0], zs[2])]
+    q[slot] = dot(normed, w_qkv[:, :384]).T.astype(BF16)
+    q_first = [links.copy(q.at[slot], q.at[slot], to) for to in (xs[0], xs[2], sibling)]
+
+    def turn(j):
+        k_t[:, pl.ds(pl.multiple_of(256 * j, 256), 256)] = k[j].T
+
+    def tile(b, j):
+        s = dot(k[j], q[b]) * scale
+        top = jnp.max(s, 0, keepdims=True)
+        e = jnp.exp(s - top)
+        p = dot(v[j], g[b])
+        exps[j, b] = e
+        grad_p[j, b] = p
+        tops[j, pl.ds(b, 1), :] = top
+        sums[j, pl.ds(b, 1), :] = jnp.sum(e, 0, keepdims=True)
+        deltas[j, pl.ds(b, 1), :] = jnp.sum(e * p, 0, keepdims=True)
+
+    def block(dk, dx):
+        other = core + dk - 2 * core * dk
+        return other * 4 + lax.rem(x + dx, 4)
+
+    def key(dz):
+        return lax.rem(z + dz, 4)
+
+    def tiles(count, which):
+        def step(n, carry):
+            dk, dx, dz = which(n)
+            tile(block(dk, dx), key(dz))
+            return carry
+
+        lax.fori_loop(0, count, step, 0)
+
+    def relay_ring(first, ref, base, i, rows, peers, forward):
+        on = []
+        for side in range(2):
+            first[side].wait_recv()
+            came = base + lax.rem(i + 3 - 2 * side, 4)
+            part = ref.at[came, pl.ds(rows * side, rows)]
+            on.append(links.copy(part, part, peers[2 * side]))
+            if forward:
+                on.append(links.copy(ref.at[came], ref.at[came], sibling))
+        return on
+
+    turn(z)
+    tile(slot, z)
+    g_on = relay_ring(g_first, g, core * 4, x, 192, xs, True)
+    k_on = relay_ring(k_first, k, 0, z, 128, zs, False)
+    q_on = relay_ring(q_first, q, core * 4, x, 192, xs, True)
+    v_on = relay_ring(v_first, v, 0, z, 128, zs, False)
+    q_first[2].wait_recv()
+    g_first[2].wait_recv()
+    tiles(2, lambda n: (0, 0, 1 + 2 * n))
+    tiles(3, lambda n: (1, 0, n + n // 2))
+    turn(key(1))
+    turn(key(3))
+    q_on[1].wait_recv()
+    q_on[3].wait_recv()
+    g_on[1].wait_recv()
+    g_on[3].wait_recv()
+
+    def beside(n):
+        dz = n // 4
+        return lax.rem(n // 2, 2), 1 + 2 * lax.rem(n, 2), dz + dz // 2
+
+    tiles(12, beside)
+    for on in (g_on, q_on):
+        on[0].wait_recv()
+        on[2].wait_recv()
+    at = core * 4 + lax.rem(x + 2, 4)
+    last = [links.copy(ref.at[at], ref.at[at], sibling) for ref in (g, q)]
+    for copy in k_on + v_on:
+        copy.wait_recv()
+    turn(key(2))
+
+    def beyond(n):
+        dx = n // 2
+        return lax.rem(n, 2), dx + dx // 2, 2
+
+    tiles(6, beyond)
+    tiles(4, lambda n: (0, 2, n))
+    for copy in last:
+        copy.wait_recv()
+    tiles(4, lambda n: (1, 2, n))
+
+    top = functools.reduce(jnp.maximum, [tops[j] for j in range(4)])
+    shift = [jnp.exp(tops[j] - top) for j in range(4)]
+    stats[0] = top
+    stats[1] = sum(sums[j] * shift[j] for j in range(4))
+    stats[2] = sum(deltas[j] * shift[j] for j in range(4))
+    shared = [links.copy(stats, all_stats.at[n], to) for n, to in enumerate(xs + cross + [sibling])]
+    for copy in shared:
+        copy.wait_recv()
+    parts = [stats] + [all_stats.at[n] for n in range(7)]
+    top = functools.reduce(jnp.maximum, [p[0] for p in parts])
+    total = sum(p[1] * jnp.exp(p[0] - top) for p in parts)
+    delta[...] = sum(p[2] * jnp.exp(p[0] - top) for p in parts) / total
+    for j in range(4):
+        weights[j] = jnp.exp(tops[j] - top) / total
+
+    back = []
+    for n, dz in enumerate((2, 1, 3, 0)):
+        j = key(dz)
+        rows = pl.ds(pl.multiple_of(256 * j, 256), 256)
+
+        def step(b, carry, j=j, rows=rows):
+            prob = exps[j, b] * weights[j, pl.ds(b, 1), :]
+            prob_row[b] = prob.astype(BF16)
+            grad_s[b, rows, :] = (prob * (grad_p[j, b] - delta[pl.ds(b, 1), :])).astype(BF16)
+            return carry
+
+        lax.fori_loop(0, 8, step, 0)
+        for_k = sum(dot_t(grad_s[b, rows, :], q[b]) for b in range(8)) * scale
+        for_v = sum(dot_t(prob_row[b], g[b]) for b in range(8))
+        if dz:
+            send_k[n] = for_k.astype(BF16)
+            send_v[n] = for_v.astype(BF16)
+            back.append(links.copy(send_k.at[n], came_k.at[n], zs[dz - 1]))
+            back.append(links.copy(send_v.at[n], came_v.at[n], zs[dz - 1]))
+        else:
+            own_k[...] = for_k
+            own_v[...] = for_v
+    sib = []
+    for dx in range(4):
+        sib_out[dx] = (dot(k_t[...], grad_s[block(1, dx)]) * scale).astype(BF16)
+        sib.append(links.copy(sib_out.at[dx], sib_in.at[dx], sibling))
+    for n, dx in enumerate((2, 1, 3, 0)):
+        for_q = dot(k_t[...], grad_s[block(0, dx)]) * scale
+        sib[dx].wait_recv()
+        for_q += sib_in[dx].astype(F32)
+        if dx:
+            send_q[n] = for_q.astype(BF16)
+            back.append(links.copy(send_q.at[n], came_q.at[n], xs[dx - 1]))
+        else:
+            own_q[...] = for_q
     for b in range(CH):
         for h in range(2):
             cot_full[pl.ds(96 * b, 96), pl.ds(128 * h, 128)] = cot[b, h]
-    w = w_qkv[...]
-    normed = (
-        dot(w[:, :384], total_of(dq, 8).astype(BF16))
-        + dot_t(w[:, 384:768], total_of(dk, 4).astype(BF16))
-        + dot_t(w[:, 768:], total_of(dv, 4).astype(BF16))
+    for copy in back:
+        copy.wait_recv()
+    for n in range(3):
+        own_k[...] += came_k[n].astype(F32)
+        own_v[...] += came_v[n].astype(F32)
+        own_q[...] += came_q[n].astype(F32)
+    back_normed = (
+        dot(w_qkv[:, :384], own_q[...].astype(BF16))
+        + dot_t(w_qkv[:, 384:768], own_k[...].astype(BF16))
+        + dot_t(w_qkv[:, 768:], own_v[...].astype(BF16))
     )
-    scaled = normed.astype(BF16).astype(F32) * gain
-    inner = jnp.mean(x * scaled, 0, keepdims=True)
-    out = cot_full[...].astype(F32) + inv * scaled - x * (inv * inv * inv * inner)
+    scaled = back_normed.astype(BF16).astype(F32) * gain
+    centre = full[...].astype(F32)
+    inner = jnp.mean(centre * scaled, 0, keepdims=True)
+    out = cot_full[...].astype(F32) + inv * scaled - centre * (inv * inv * inv * inner)
     for b in range(CH):
         for h in range(2):
             grad[b, h] = out[96 * b : 96 * b + 96, 128 * h : 128 * h + 128].astype(BF16)
+    for b in range(CH):
+        to = (row, b)
+        links.copy(grad.at[b], mine.at[frame], to, own=same(to, (r, c)), recv=64 + frame)
+    for b in range(CH):
+        links.copy(grad.at[b, 1], prev_g.at[frame], (row_high, b), recv=68 + frame)
+        links.copy(grad.at[b, 0], next_g.at[frame], (row_low, b), recv=72 + frame)
+    for f in range(4):
+        links.arrive(mine.at[f], 64 + f)
+        links.arrive(prev_g.at[f], 68 + f)
+        links.arrive(next_g.at[f], 72 + f)
+    links.finish()
 
 
 def tail_kernel(links, held, made, scratch):
@@ -621,9 +628,10 @@
 
 
 def widen_kernel(scale, flat, out):
-    for lane in range(3):
-        piece = flat[pl.ds(288 * lane, 288), :].astype(F32) * scale
-        out[:, pl.ds(128 * lane, 128)] = piece
+    for k in range(9):
+        for lane in range(3):
+            piece = flat[pl.ds((3 * k + lane) * 288, 288), :].astype(F32) * scale
+            out[pl.ds(288 * k, 288), pl.ds(128 * lane, 128)] = piece
 
 
 def on_device(features, gain_in, w_conv, gain_attn, w_qkv, w_out, cotangent):
@@ -661,71 +669,48 @@
         name="conv",
     )
     (res_frame,) = exchange(1, frame_body, (res,), [((4, 2, 96, 128), BF16)], 4)
-    q, k, v = compute(
-        project_kernel,
-        [((384, 256), BF16), ((256, 384), BF16), ((256, 384), BF16)],
-        res_frame,
-        gains,
-        w_qkv,
-        scratch=[pltpu.VMEM((384, 256), BF16)],
-        name="project",
-    )
-    all_q, all_g, all_k, all_v = exchange(
+    own, prev_g, next_g = fused(
         2,
-        gather_body,
-        (q, grad_o, k, v),
-        [((8, 384, 256), BF16)] * 2 + [((4, 256, 384), BF16)] * 2,
-        24,
-        local=4,
-    )
-    (stats,) = compute(
-        functools.partial(stats_kernel, scale),
-        [((3, 8, 256), F32)],
-        all_q,
-        all_g,
-        all_k,
-        all_v,
-        name="stats",
-    )
-    (all_stats,) = exchange(3, simple(stats_plan), (stats,), [((8, 3, 8, 256), F32)], 7, local=1)
-    dq, dk, dv = compute(
-        functools.partial(attn_kernel, scale),
-        [((8, 384, 256), BF16)] + [((4, 256, 384), BF16)] * 2,
-        all_q,
-        all_g,
-        all_k,
-        all_v,
-        all_stats,
-        scratch=[pltpu.VMEM((1024, 384), F32)] * 2,
-        name="attn",
-    )
-    all_dq, all_dk, all_dv = exchange(
-        4,
-        simple(back_plan),
-        (dq, dk, dv),
-        [((8, 384, 256), BF16)] + [((4, 256, 384), BF16)] * 2,
-        13,
-        local=3,
-    )
-    (grad,) = compute(
-        residual_kernel,
-        [((4, 2, 96, 128), BF16)],
-        all_dq,
-        all_dk,
-        all_dv,
-        res_frame,
-        cot_frame,
-        gains,
-        w_qkv,
-        scratch=[pltpu.VMEM((384, 256), BF16)] * 2,
-        name="residual",
-    )
-    own, prev_g, next_g = exchange(
-        5,
-        grad_body,
-        (grad,),
-        [((4, 2, 96, 128), BF16), ((4, 96, 128), BF16), ((4, 96, 128), BF16)],
-        12,
+        functools.partial(attn_body, scale),
+        (res_frame, cot_frame, gains, w_qkv, grad_o),
+        [
+            ((4, 2, 96, 128), BF16, pl.ANY),
+            ((4, 96, 128), BF16, pl.ANY),
+            ((4, 96, 128), BF16, pl.ANY),
+        ],
+        [
+            pltpu.VMEM((384, 256), BF16),
+            pltpu.VMEM((384, 256), BF16),
+            pltpu.VMEM((8, 384, 256), BF16),
+            pltpu.VMEM((8, 384, 256), BF16),
+            pltpu.VMEM((4, 256, 384), BF16),
+            pltpu.VMEM((4, 256, 384), BF16),
+            pltpu.VMEM((384, 1024), BF16),
+            pltpu.VMEM((4, 8, 256, 256), F32),
+            pltpu.VMEM((4, 8, 256, 256), F32),
+            pltpu.VMEM((8, 1024, 256), BF16),
+            pltpu.VMEM((8, 256, 256), BF16),
+            pltpu.VMEM((4, 8, 256), F32),
+            pltpu.VMEM((4, 8, 256), F32),
+            pltpu.VMEM((4, 8, 256), F32),
+            pltpu.VMEM((3, 8, 256), F32),
+            pltpu.VMEM((7, 3, 8, 256), F32),
+            pltpu.VMEM((4, 8, 256), F32),
+            pltpu.VMEM((8, 256), F32),
+            pltpu.VMEM((3, 256, 384), BF16),
+            pltpu.VMEM((3, 256, 384), BF16),
+            pltpu.VMEM((3, 256, 384), BF16),
+            pltpu.VMEM((3, 256, 384), BF16),
+            pltpu.VMEM((256, 384), F32),
+            pltpu.VMEM((256, 384), F32),
+            pltpu.VMEM((4, 384, 256), BF16),
+            pltpu.VMEM((4, 384, 256), BF16),
+            pltpu.VMEM((3, 384, 256), BF16),
+            pltpu.VMEM((3, 384, 256), BF16),
+            pltpu.VMEM((384, 256), F32),
+            pltpu.VMEM((4, 2, 96, 128), BF16),
+        ],
+        76,
     )
     out, flat = fused(
         6,
@@ -751,14 +736,12 @@
         34,
     )
     cell_scale = 1.0 / math.sqrt(32768)
-    grad_weights = pl.pallas_call(
+    (grad_weights,) = compute(
         functools.partial(widen_kernel, cell_scale),
-        grid=(9,),
-        out_shape=jax.ShapeDtypeStruct((2592, 384), F32),
-        in_specs=[pl.BlockSpec((864, 128), lambda i: (i, 0))],
-        out_specs=pl.BlockSpec((288, 384), lambda i: (i, 0)),
+        [((2592, 384), F32)],
+        flat,
         name="widen",
-    )(flat)
+    )
     return out, grad_weights.reshape(27, 96, 384)
 
 

time: 207 us -> 168 us (0.81)
  Pallas kernels: 203 us -> 164 us
    pallas_call x6 -> x2, Pallas kernels: 103 us -> 35.2 us  [exchange(): pl.pallas_call(kernel, out_shape=[jax.ShapeDtypeStruct(s, t) for s, t in...]
    pallas_call x1 -> x2, Pallas kernels: 51.8 us -> 119 us  [fused(): pl.pallas_call(kernel, out_shape=[jax.ShapeDtypeStruct(s, t) for s, t, _...]
    pallas_call x5 -> x2, Pallas kernels: 41.2 us -> 10 us  [compute(): pl.pallas_call(body, out_shape=[jax.ShapeDtypeStruct(s, t) for s, t in ou...]
    pallas_call x1 -> x0, Pallas kernels: 6.55 us -> none  [on_device(): pl.pallas_call(functools.partial(widen_kernel, cell_scale), grid=(9,), ou...]
where the time goes in v4:
time: 168 us; the launch traced here: 167 us
  Pallas kernels  164 us (98%)
    pallas_call x2, Pallas kernels, fused(): pl.pallas_call(kernel, out_shape=[jax.ShapeDtypeStruct(s, t) for s, t, _...  119 us
    pallas_call x2, Pallas kernels, exchange(): pl.pallas_call(kernel, out_shape=[jax.ShapeDtypeStruct(s, t) for s, t in...  35.2 us
    pallas_call x2, Pallas kernels, compute(): pl.pallas_call(body, out_shape=[jax.ShapeDtypeStruct(s, t) for s, t in ou...  10 us

profile of v4, /device:TPU:8, one launch (start us, length us, event | category | flops | bytes accessed | tf_op | source)
XLA Modules:
  0.0 166.9 jit_solution(6730971675836219083)
XLA Ops:
  0.6 0.7 pad_maximum_fusion
  1.3 0.7 broadcast_in_dim.2.refs_2_.refs_9_
  2.0 29.9 %exchange_0.1 = (bf16[4,4,2,96,128]{4,3,2,1,0:T(8,128)(2,1)}, bf16[4,4,96,128]{3,2,1,0:T(8,128)(2,1)}, bf16[4,4,96,128]{3,2,1,0:T(8,128)(2,1)}, bf16[4,2,96,128]...) custom-call(bf16[4,2,96,128]{3,2,1,0:T(8,128)(2,1)} %refs_8_.1, ...), custom_call_target="tpu_custom_call" | custom-call | tf_op jit(solution)/shard_map/exchange_0/pallas_call | solution.py:86
  32.0 6.2 %conv.1 = (bf16[4,2,96,128]{3,2,1,0:T(8,128)(2,1)}, bf16[384,2048]{1,0:T(8,128)(2,1)}, f32[8,128]{1,0:T(8,128)}, bf16[384,256]{1,0:T(8,128)(2,1)}) custom-call(bf16[4,2,96,128]{3,2,1,0:T(8,128)(2,1)} %refs_8_.1, bf16[4,4,2,96,128]{4,3,2,1,0:T(8,128)(2,1)} %get-tuple-element.17.all_feat.refs_5_, bf16[4,4,96,128]{3,2,1,0:T(8,128)(2,1)} %get-tuple-element.18.prev_feat, ...), custom_call_target="tpu_custom_call" | custom-call | tf_op jit(solution)/shard_map/conv/pallas_call | solution.py:140
  38.1 5.3 %exchange_1.1.refs_0_ = bf16[4,2,96,128]{3,2,1,0:T(8,128)(2,1)} custom-call(bf16[4,2,96,128]{3,2,1,0:T(8,128)(2,1)} %get-tuple-element.22.refs_0_), custom_call_target="tpu_custom_call" | custom-call | tf_op jit(solution)/shard_map/exchange_1/pallas_call | solution.py:86
  43.4 66.3 %fused_2.1 = (bf16[4,2,96,128]{3,2,1,0:T(8,128)(2,1)}, bf16[4,96,128]{2,1,0:T(8,128)(2,1)}, bf16[4,96,128]{2,1,0:T(8,128)(2,1)}) custom-call(bf16[4,2,96,128]{3,2,1,0:T(8,128)(2,1)} %exchange_1.1.refs_0_, bf16[4,2,96,128]{3,2,1,0:T(8,128)(2,1)} %get-tuple-element.21.cot.refs_1_, bf16[4,2,96,128]{3,2,1,0:T(8,128)(2,1)} %get-tuple-element.20.gains.refs_2_.refs_7_, ...), custom_call_target="tpu_custom_call" | custom-call | tf_op jit(solution)/shard_map/fused_2/pallas_call | solution.py:109
  109.8 52.6 %fused_6.1 = (bf16[4,2,96,128]{3,2,1,0:T(8,128)(2,1)}, bf16[8192,128]{1,0:T(8,128)(2,1)}) custom-call(bf16[4,2,96,128]{3,2,1,0:T(8,128)(2,1)} %get-tuple-element.24.refs_0_, bf16[4,96,128]{2,1,0:T(8,128)(2,1)} %get-tuple-element.25.refs_1_, bf16[4,96,128]{2,1,0:T(8,128)(2,1)} %get-tuple-element.26.refs_2_, bf16[384,2048]{1,0:T(8,128)(2,1)} %get-tuple-element.27.refs_3_, ...), custom_call_target="tpu_custom_call" | custom-call | tf_op jit(solution)/shard_map/fused_6/pallas_call | solution.py:109
  162.4 0.0 copy-start
  162.4 3.9 %widen.1 = f32[2592,384]{1,0:T(8,128)} custom-call(bf16[8192,128]{1,0:T(8,128)(2,1)} %get-tuple-element.31.flat), custom_call_target="tpu_custom_call" | custom-call | tf_op jit(solution)/shard_map/widen/pallas_call | solution.py:140
  166.2 0.0 copy-done
  166.2 0.7 copy.10
Async XLA Ops:
  162.4 3.9 %copy-start = (bf16[4,2,96,128]{3,2,1,0:T(8,128)(2,1)S(1)}, bf16[4,2,96,128]{3,2,1,0:T(8,128)(2,1)}, u32[]{:S(2)}) copy-start(bf16[4,2,96,128]{3,2,1,0:T(8,128)(2,1)} %get-tuple-element.34) | copy-start | bytes 589828

commit v5 on v4

--- a/solution.py
+++ b/solution.py
@@ -75,31 +75,6 @@
                 pl.when(jnp.logical_not(own))(far.wait_send)
 
 
-def exchange(cid, body, ins, outs, count, local=0, held=(), made=()):
-    def kernel(*refs):
-        n_in, n_out = len(ins) + len(held), len(outs) + len(made)
-        send, recv, own = refs[n_in + n_out :]
-        body(Links(send, recv), own, refs[:n_in], refs[n_in : n_in + n_out])
-
-    far = pl.BlockSpec(memory_space=pl.ANY)
-    near = pl.BlockSpec(memory_space=pltpu.VMEM)
-    return pl.pallas_call(
-        kernel,
-        out_shape=[jax.ShapeDtypeStruct(s, t) for s, t in list(outs) + list(made)],
-        in_specs=[far] * len(ins) + [near] * len(held),
-        out_specs=[far] * len(outs) + [near] * len(made),
-        scratch_shapes=[
-            pltpu.SemaphoreType.DMA((count,)),
-            pltpu.SemaphoreType.DMA((count,)),
-            pltpu.SemaphoreType.DMA((max(local, 1),)),
-        ],
-        compiler_params=pltpu.CompilerParams(
-            collective_id=cid, has_side_effects=True, vmem_limit_bytes=VMEM_BYTES
-        ),
-        name="exchange_%d" % cid,
-    )(*ins, *held)
-
-
 def fused(cid, body, held, made, scratch, count):
     def kernel(*refs):
         n_in, n_out = len(held), len(held) + len(made)
@@ -109,14 +84,14 @@
     return pl.pallas_call(
         kernel,
         out_shape=[jax.ShapeDtypeStruct(s, t) for s, t, _ in made],
-        in_specs=[pl.BlockSpec(memory_space=pltpu.VMEM)] * len(held),
+        in_specs=[pl.BlockSpec(memory_space=m) for _, m in held],
         out_specs=[pl.BlockSpec(memory_space=m) for _, _, m in made],
         scratch_shapes=list(scratch) + [pltpu.SemaphoreType.DMA((count,))] * 2,
         compiler_params=pltpu.CompilerParams(
             collective_id=cid, has_side_effects=True, vmem_limit_bytes=VMEM_BYTES
         ),
         name="fused_%d" % cid,
-    )(*held)
+    )(*[array for array, _ in held])
 
 
 def simple(plan):
@@ -187,83 +162,93 @@
     pl.semaphore_wait(barrier, len(targets) - 1 + (core - y_hi) * (core - y_hi))
 
 
-def start_body(links, own, srcs, dsts):
-    feat, cot, gain, w = srcs
-    all_feat, prev_feat, next_feat, cot_frame, all_gain, w_t = dsts
+def sigmoid(v):
+    return 1.0 / (1.0 + jnp.exp(-v))
+
+
+def gain_columns(rows, which):
+    blocks = [jnp.broadcast_to(rows[b, which : which + 1, :], (128, 128)).T[:96] for b in range(CH)]
+    return jnp.concatenate(blocks, 0)
+
+
+def front_body(links, held, made, scratch):
+    feat, cot, w_far, gain_in, gain_attn = held
+    act_out, feat_out, cot_frame, res_frame, inv_in, gain_rows = made
+    every, w, act, res, mark = scratch
     r, c = coords()
+    x, y_hi, z, y_lo, core = place(r, c)
     low, high = near_rows(r)
-    x, y_hi, z, y_lo, core = place(r, c)
-    here = [
-        pltpu.make_async_copy(feat, all_feat.at[c], own.at[0]),
-        pltpu.make_async_copy(gain, all_gain.at[c], own.at[1]),
-    ]
-    for copy in here:
-        copy.start()
+    c_sib, c_near = y_lo * 2 + 1 - core, (1 - y_lo) * 2 + core
+    sibling, near = (r, c_sib), (r, c_near)
     targets = [owner(f, r) for f in range(4)]
     sources = [(z * 8 + core * 4 + x, b) for b in range(4)]
-    others = ch_peers(r, c) + [(row, b) for row in (low, high) for b in range(CH)]
+    others = ch_peers(r, c) + [(low, c), (high, c)]
+    own_rows = pl.ds(1, 2)
+    here = pltpu.make_async_copy(feat, every.at[c, :, own_rows], mark.at[0])
+    here.start()
+    weights = pltpu.make_async_copy(w_far, w, mark.at[1])
+    weights.start()
+    gain_rows[c] = jnp.zeros((8, 128), F32)
+    pad = jnp.zeros((1, 32), F32)
+    gain_rows[c, 0:1, :] = jnp.concatenate([gain_in[...].astype(F32), pad], 1)
+    gain_rows[c, 1:2, :] = jnp.concatenate([gain_attn[...].astype(F32), pad], 1)
     greet_frames(links, (r, c), sources + others, targets + others)
-    for f in range(4):
-        links.copy(cot.at[f], cot_frame.at[c], targets[f], own=same(targets[f], (r, c)), recv=c)
-    there = []
-    for to in ch_peers(r, c):
-        there.append(links.copy(feat, all_feat.at[c], to))
-        there.append(links.copy(gain, all_gain.at[c], to))
-    for d in range(CH):
-        c_to = lax.rem(c + d, CH)
-        there.append(links.copy(feat.at[:, 1], prev_feat.at[c], (high, c_to)))
-        there.append(links.copy(feat.at[:, 0], next_feat.at[c], (low, c_to)))
-    for t in range(3):
-        for k in range(3):
-            piece = jnp.concatenate([w[9 * t + 3 * h + k] for h in range(3)], 0)
-            w_t[t, pl.ds(384 * k, 384), :] = piece.T
-    for copy in here:
-        copy.wait()
-    for b in range(CH):
-        links.arrive(cot_frame.at[b], b)
-    for copy in there:
-        copy.wait_recv()
-    links.finish()
-
-
-def frame_body(links, own, srcs, dsts):
-    (res,), (res_frame,) = srcs, dsts
-    r, c = coords()
-    x, y_hi, z, y_lo, core = place(r, c)
-    targets = [owner(f, r) for f in range(4)]
-    sources = [(z * 8 + core * 4 + x, b) for b in range(4)]
-    greet_frames(links, (r, c), sources, targets)
-    for f in range(4):
-        links.copy(res.at[f], res_frame.at[c], targets[f], own=same(targets[f], (r, c)), recv=c)
-    for b in range(CH):
-        links.arrive(res_frame.at[b], b)
-    links.finish()
-
-
-def sigmoid(v):
-    return 1.0 / (1.0 + jnp.exp(-v))
-
-
-def conv_kernel(feat, all_feat, prev_feat, next_feat, gains, w, cot, w_out, res, act, inv_in, grad_o, full):
-    r = lax.axis_index("row")
-    gain = jnp.concatenate([gains[b, 0] for b in range(CH)], 0).astype(F32)
-    for f in range(4):
-        for h in range(4):
-            blocks = [
-                prev_feat[b, f] if h == 0 else next_feat[b, f] if h == 3 else all_feat[b, f, h - 1]
-                for b in range(CH)
-            ]
-            x = jnp.concatenate(blocks, 0).astype(F32)
-            inv = lax.rsqrt(jnp.mean(x * x, 0, keepdims=True) + EPSILON)
-            before = x * inv * gain
-            a = before * sigmoid(before)
-            if h == 0:
-                a = jnp.where(r == 0, 0.0, a)
-            elif h == 3:
-                a = jnp.where(r == ROWS - 1, 0.0, a)
-            else:
-                inv_in[2 * f + h - 1, :] = inv[0]
-            act[:, pl.ds((4 * f + h) * 128, 128)] = a.astype(BF16)
+    edges = [
+        links.copy(feat.at[:, 1], every.at[c, :, 0], (high, c)),
+        links.copy(feat.at[:, 0], every.at[c, :, 3], (low, c)),
+    ]
+    to_near = links.copy(feat, every.at[c, :, own_rows], near)
+    to_sib = links.copy(feat, every.at[c, :, own_rows], sibling)
+    gains = [links.copy(gain_rows.at[c], gain_rows.at[c], to) for to in ch_peers(r, c)]
+    near_edges, sib_edges = [], []
+    for n, h in enumerate((0, 3)):
+        edges[n].wait_recv()
+        part = every.at[c, :, h]
+        near_edges.append(links.copy(part, part, near))
+        sib_edges.append(links.copy(part, part, sibling))
+    to_near.wait_recv()
+    part = every.at[c_near, :, own_rows]
+    passed = links.copy(part, part, sibling)
+    for f in range(4):
+        links.copy(cot.at[f], cot_frame.at[c], targets[f], own=same(targets[f], (r, c)), recv=40 + c)
+    for copy in gains:
+        copy.wait_recv()
+    gain = gain_columns(gain_rows, 0)
+    here.wait()
+    to_sib.wait_recv()
+    passed.wait_recv()
+    keep_feat = pltpu.make_async_copy(every.at[:, :, own_rows], feat_out, mark.at[0])
+    keep_feat.start()
+
+    def activate(f, h):
+        v = jnp.concatenate([every[b, f, h] for b in range(CH)], 0).astype(F32)
+        inv = lax.rsqrt(jnp.mean(v * v, 0, keepdims=True) + EPSILON)
+        before = v * inv * gain
+        a = before * sigmoid(before)
+        if h == 0:
+            a = jnp.where(r == 0, 0.0, a)
+        elif h == 3:
+            a = jnp.where(r == ROWS - 1, 0.0, a)
+        else:
+            inv_in[2 * f + h - 1 : 2 * f + h, :] = inv
+        act[:, pl.ds((4 * f + h) * 128, 128)] = a.astype(BF16)
+
+    for f in range(4):
+        activate(f, 1)
+        activate(f, 2)
+    far_edges = []
+    for n, h in enumerate((0, 3)):
+        near_edges[n].wait_recv()
+        part = every.at[c_near, :, h]
+        far_edges.append(links.copy(part, part, sibling))
+    for copy in sib_edges + far_edges:
+        copy.wait_recv()
+    for f in range(4):
+        activate(f, 0)
+        activate(f, 3)
+    keep_act = pltpu.make_async_copy(act, act_out, mark.at[2])
+    keep_act.start()
+    weights.wait()
     for f in range(4):
         acc = jnp.zeros((288, 256), F32)
         for t in range(3):
@@ -271,15 +256,20 @@
             if source < 0:
                 continue
             for h in range(3):
-                acc += dot(w[3 * t + h], act[:, pl.ds((4 * source + h) * 128, 256)])
+                taps = w[pl.ds(9 * t + 3 * h, 3)].reshape(288, 384)
+                acc += dot(taps, act[:, pl.ds((4 * source + h) * 128, 256)])
         for h in range(2):
             y = acc[:, 128 * h : 128 * h + 128]
             out = move(y[:96], 1) + y[96:192] + move(y[192:], -1)
-            res[f, h] = (feat[f, h].astype(F32) + out).astype(BF16)
+            res[f, h] = (every[c, f, h + 1].astype(F32) + out).astype(BF16)
+        links.copy(res.at[f], res_frame.at[c], targets[f], own=same(targets[f], (r, c)), recv=44 + c)
+    keep_feat.wait()
+    keep_act.wait()
     for b in range(CH):
-        for h in range(2):
-            full[pl.ds(96 * b, 96), pl.ds(128 * h, 128)] = cot[b, h]
-    grad_o[...] = dot(w_out[...], full[...]).astype(BF16)
+        links.arrive(cot_frame.at[b], 40 + b)
+    for b in range(CH):
+        links.arrive(res_frame.at[b], 44 + b)
+    links.finish()
 
 
 def attn_norm(res_frame, full):
@@ -291,10 +281,10 @@
 
 
 def attn_body(scale, links, held, made, scratch):
-    res_frame, cot, gains, w_qkv, grad_o = held
-    mine, prev_g, next_g = made
+    res_frame, cot, gain_rows, w_qkv, w_out, w_far = held
+    mine, prev_g, next_g, w_t_out = made
     (full, cot_full, q, g, k, v, k_t, exps, grad_p, grad_s, prob_row, tops, sums, deltas, stats, all_stats, weights, delta,
-     send_k, send_v, came_k, came_v, own_k, own_v, sib_out, sib_in, send_q, came_q, own_q, grad) = scratch
+     send_k, send_v, came_k, came_v, own_k, own_v, sib_out, sib_in, send_q, came_q, own_q, grad, w, w_t, mark) = scratch
     r, c = coords()
     x, y_hi, z, y_lo, core = place(r, c)
     slot = core * 4 + x
@@ -311,9 +301,14 @@
     sources = [owner(f, i) for i in (r, low, high) for f in range(4)]
     greet_frames(links, (r, c), sources + alike, [(row, b) for b in range(CH)] + around + alike)
 
-    g[slot] = grad_o[...]
+    weights_in = pltpu.make_async_copy(w_far, w, mark.at[0])
+    weights_in.start()
+    for b in range(CH):
+        for h in range(2):
+            cot_full[pl.ds(96 * b, 96), pl.ds(128 * h, 128)] = cot[b, h]
+    g[slot] = dot(w_out[...], cot_full[...]).astype(BF16)
     g_first = [links.copy(g.at[slot], g.at[slot], to) for to in (xs[0], xs[2], sibling)]
-    gain = jnp.concatenate([gains[b, 1] for b in range(CH)], 0).astype(F32)
+    gain = gain_columns(gain_rows, 1)
     gain = jnp.concatenate([gain, gain], 1)
     centre, inv = attn_norm(res_frame, full)
     normed = (centre * inv * gain).astype(BF16).astype(F32).T.astype(BF16)
@@ -366,6 +361,13 @@
 
     turn(z)
     tile(slot, z)
+    weights_in.wait()
+    for t in range(3):
+        for n in range(3):
+            piece = jnp.concatenate([w[9 * t + 3 * h + n] for h in range(3)], 0)
+            w_t[t, pl.ds(384 * n, 384), :] = piece.T
+    weights_out = pltpu.make_async_copy(w_t, w_t_out, mark.at[0])
+    weights_out.start()
     g_on = relay_ring(g_first, g, core * 4, x, 192, xs, True)
     k_on = relay_ring(k_first, k, 0, z, 128, zs, False)
     q_on = relay_ring(q_first, q, core * 4, x, 192, xs, True)
@@ -455,9 +457,7 @@
             back.append(links.copy(send_q.at[n], came_q.at[n], xs[dx - 1]))
         else:
             own_q[...] = for_q
-    for b in range(CH):
-        for h in range(2):
-            cot_full[pl.ds(96 * b, 96), pl.ds(128 * h, 128)] = cot[b, h]
+    weights_out.wait()
     for copy in back:
         copy.wait_recv()
     for n in range(3):
@@ -490,9 +490,9 @@
 
 
 def tail_kernel(links, held, made, scratch):
-    own, prev_g, next_g, act, w_t, all_feat, inv_in, gains, feat, gain_own = held
+    own, prev_g, next_g, act_far, w_t_far, feat_far, inv_in, gain_rows = held
     out, flat = made
-    rows, lines, weight, part, all_part, inner, all_inner, came1, came2, came3, sum1, sum2, sum3, mark = scratch
+    rows, lines, weight, part, all_part, inner, all_inner, came1, came2, came3, sum1, sum2, sum3, act, w_t, all_feat, mark = scratch
     r, c = coords()
     x, y_hi, z, y_lo, core = place(r, c)
     xs = [device(lax.rem(x + d, 4), y_hi, z, y_lo, core) for d in range(1, 4)]
@@ -505,6 +505,12 @@
         (x, xs, x_at, z, zs, z_at),
         (z, zs, z_at, x, xs, x_at),
     )
+    inside = [
+        pltpu.make_async_copy(src, dst, mark.at[2 + n])
+        for n, (src, dst) in enumerate(((act_far, act), (w_t_far, w_t), (feat_far, all_feat)))
+    ]
+    for copy in inside:
+        copy.start()
     links.greet(xs + zs + [across] + chs, 10)
     moved = []
     for f in range(4):
@@ -513,6 +519,7 @@
             y = own[f, h].astype(F32)
             both.append(jnp.concatenate([move(y, -1), y, move(y, 1)], 0).astype(BF16))
         moved.append(jnp.concatenate(both, 1))
+    inside[0].wait()
     for t in range(3):
         for h in range(3):
             acc = jnp.zeros((288, 384), F32)
@@ -539,7 +546,9 @@
         for h in range(3):
             for k in range(2):
                 lines[f, pl.ds(96 * h, 96), pl.ds(128 * k, 128)] = rows[f, 2 - h + k]
-    gain = jnp.concatenate([gains[b, 0] for b in range(CH)], 0).astype(F32)
+    gain = gain_columns(gain_rows, 0)
+    inside[1].wait()
+    inside[2].wait()
     for f in range(4):
         acc = jnp.zeros((1152, 256), F32)
         for t in range(3):
@@ -609,10 +618,10 @@
     for copy in parts:
         copy.wait_recv()
     mean = (inner[...] + all_inner[0] + all_inner[1] + all_inner[2]) / 384.0
-    gain = gain_own[0].astype(F32)
+    gain = jnp.broadcast_to(gain_rows[c, 0:1, :], (128, 128)).T[:96]
     for f in range(4):
         for h in range(2):
-            v = feat[f, h].astype(F32)
+            v = all_feat[c, f, h].astype(F32)
             inv = inv_in[2 * f + h : 2 * f + h + 1, :]
             total = part[c, f, h].astype(F32)
             for d in range(3):
@@ -636,47 +645,43 @@
 
 def on_device(features, gain_in, w_conv, gain_attn, w_qkv, w_out, cotangent):
     scale = 1.0 / math.sqrt(384)
-    gain_own = jnp.broadcast_to(jnp.stack([gain_in, gain_attn])[:, :, None], (2, 96, 128))
-    w_rows = w_conv.reshape(9, 288, 384)
-    all_feat, prev_feat, next_feat, cot_frame, gains, w_t = exchange(
+    near, far = pltpu.VMEM, pl.ANY
+    act, all_feat, cot_frame, res_frame, inv_in, gain_rows = fused(
         0,
-        start_body,
-        (features, cotangent, gain_own),
+        front_body,
         [
-            ((4, 4, 2, 96, 128), BF16),
-            ((4, 4, 96, 128), BF16),
-            ((4, 4, 96, 128), BF16),
-            ((4, 2, 96, 128), BF16),
-            ((4, 2, 96, 128), BF16),
+            (features, far),
+            (cotangent, far),
+            (w_conv, far),
+            (gain_in.reshape(1, 96), near),
+            (gain_attn.reshape(1, 96), near),
         ],
-        18,
-        local=2,
-        held=(w_conv,),
-        made=[((3, 1152, 288), BF16)],
+        [
+            ((384, 2048), BF16, far),
+            ((4, 4, 2, 96, 128), BF16, far),
+            ((4, 2, 96, 128), BF16, far),
+            ((4, 2, 96, 128), BF16, far),
+            ((8, 128), F32, near),
+            ((4, 8, 128), F32, near),
+        ],
+        [
+            pltpu.VMEM((4, 4, 4, 96, 128), BF16),
+            pltpu.VMEM((27, 96, 384), BF16),
+            pltpu.VMEM((384, 2048), BF16),
+            pltpu.VMEM((4, 2, 96, 128), BF16),
+            pltpu.SemaphoreType.DMA((3,)),
+        ],
+        48,
     )
-    res, act, inv_in, grad_o = compute(
-        conv_kernel,
-        [((4, 2, 96, 128), BF16), ((384, 2048), BF16), ((8, 128), F32), ((384, 256), BF16)],
-        features,
-        all_feat,
-        prev_feat,
-        next_feat,
-        gains,
-        w_rows,
-        cot_frame,
-        w_out,
-        scratch=[pltpu.VMEM((384, 256), BF16)],
-        name="conv",
-    )
-    (res_frame,) = exchange(1, frame_body, (res,), [((4, 2, 96, 128), BF16)], 4)
-    own, prev_g, next_g = fused(
+    own, prev_g, next_g, w_t = fused(
         2,
         functools.partial(attn_body, scale),
-        (res_frame, cot_frame, gains, w_qkv, grad_o),
+        [(res_frame, near), (cot_frame, near), (gain_rows, near), (w_qkv, near), (w_out, near), (w_conv, far)],
         [
             ((4, 2, 96, 128), BF16, pl.ANY),
             ((4, 96, 128), BF16, pl.ANY),
             ((4, 96, 128), BF16, pl.ANY),
+            ((3, 1152, 288), BF16, pl.ANY),
         ],
         [
             pltpu.VMEM((384, 256), BF16),
@@ -709,13 +714,25 @@
             pltpu.VMEM((3, 384, 256), BF16),
             pltpu.VMEM((384, 256), F32),
             pltpu.VMEM((4, 2, 96, 128), BF16),
+            pltpu.VMEM((27, 96, 384), BF16),
+            pltpu.VMEM((3, 1152, 288), BF16),
+            pltpu.SemaphoreType.DMA((1,)),
         ],
         76,
     )
     out, flat = fused(
         6,
         tail_kernel,
-        (own, prev_g, next_g, act, w_t, all_feat, inv_in, gains, features, gain_own),
+        [
+            (own, near),
+            (prev_g, near),
+            (next_g, near),
+            (act, far),
+            (w_t, far),
+            (all_feat, far),
+            (inv_in, near),
+            (gain_rows, near),
+        ],
         [((4, 2, 96, 128), BF16, pltpu.VMEM), ((8192, 128), BF16, pl.ANY)],
         [
             pltpu.VMEM((4, 4, 96, 128), BF16),
@@ -731,7 +748,10 @@
             pltpu.VMEM((2, 1024, 128), BF16),
             pltpu.VMEM((2, 256, 128), BF16),
             pltpu.VMEM((2, 128, 128), BF16),
-            pltpu.SemaphoreType.DMA((2,)),
+            pltpu.VMEM((384, 2048), BF16),
+            pltpu.VMEM((3, 1152, 288), BF16),
+            pltpu.VMEM((4, 4, 2, 96, 128), BF16),
+            pltpu.SemaphoreType.DMA((5,)),
         ],
         34,
     )

time: 168 us -> 153 us (0.911)
  Pallas kernels: 164 us -> 151 us
    pallas_call x2 -> x0, Pallas kernels: 35.2 us -> none  [exchange(): pl.pallas_call(kernel, out_shape=[jax.ShapeDtypeStruct(s, t) for s, t in...]
    pallas_call x2 -> x3, Pallas kernels: 119 us -> 147 us  [fused(): pl.pallas_call(kernel, out_shape=[jax.ShapeDtypeStruct(s, t) for s, t, _...]
    pallas_call x2 -> x1, Pallas kernels: 10 us -> 3.87 us  [compute(): pl.pallas_call(body, out_shape=[jax.ShapeDtypeStruct(s, t) for s, t in ou...]
where the time goes in v5:
time: 153 us; the launch traced here: 152 us
  Pallas kernels  151 us (99%)
    pallas_call x3, Pallas kernels, fused(): pl.pallas_call(kernel, out_shape=[jax.ShapeDtypeStruct(s, t) for s, t, _...  147 us
    pallas_call x1, Pallas kernels, compute(): pl.pallas_call(body, out_shape=[jax.ShapeDtypeStruct(s, t) for s, t in ou...  3.87 us

profile of v5, /device:TPU:8, one launch (start us, length us, event | category | flops | bytes accessed | tf_op | source)
XLA Modules:
  0.0 152.2 jit_solution(6285837925418809686)
XLA Ops:
  0.6 29.2 %fused_0.1 = (bf16[384,2048]{1,0:T(8,128)(2,1)}, bf16[4,4,2,96,128]{4,3,2,1,0:T(8,128)(2,1)}, bf16[4,2,96,128]{3,2,1,0:T(8,128)(2,1)}, bf16[4,2,96,128]{3,2,1,0:...) custom-call(bf16[4,2,96,128]{3,2,1,0:T(8,128)(2,1)} %refs_0_.1, bf16[4,2,96,128]{3,2,1,0:T(8,128)(2,1)} %refs_1_.1, ...), custom_call_target="tpu_custom_call" | custom-call | tf_op jit(solution)/shard_map/fused_0/pallas_call | solution.py:84
  29.9 65.5 %fused_2.1 = (bf16[4,2,96,128]{3,2,1,0:T(8,128)(2,1)}, bf16[4,96,128]{2,1,0:T(8,128)(2,1)}, bf16[4,96,128]{2,1,0:T(8,128)(2,1)}, bf16[3,1152,288]{2,1,0:T(8,128)(2,1)}) custom-call(bf16[4,2,96,128]{3,2,1,0:T(8,128)(2,1)} %get-tuple-element.14.refs_0_, bf16[4,2,96,128]{3,2,1,0:T(8,128)(2,1)} %get-tuple-element.15.refs_1_, ...), custom_call_target="tpu_custom_call" | custom-call | tf_op jit(solution)/shard_map/fused_2/pallas_call | solution.py:84
  95.4 52.2 %fused_6.1 = (bf16[4,2,96,128]{3,2,1,0:T(8,128)(2,1)}, bf16[8192,128]{1,0:T(8,128)(2,1)}) custom-call(bf16[4,2,96,128]{3,2,1,0:T(8,128)(2,1)} %get-tuple-element.17.refs_0_, bf16[4,96,128]{2,1,0:T(8,128)(2,1)} %get-tuple-element.18.refs_1_, bf16[4,96,128]{2,1,0:T(8,128)(2,1)} %get-tuple-element.19.refs_2_, bf16[384,2048]{1,0:T(8,128)(2,1)} %get-tuple-element.20.refs_3_, ...), custom_call_target="tpu_custom_call" | custom-call | tf_op jit(solution)/shard_map/fused_6/pallas_call | solution.py:84
  147.6 0.0 copy-start
  147.6 3.9 %widen.1 = f32[2592,384]{1,0:T(8,128)} custom-call(bf16[8192,128]{1,0:T(8,128)(2,1)} %get-tuple-element.25.flat), custom_call_target="tpu_custom_call" | custom-call | tf_op jit(solution)/shard_map/widen/pallas_call | solution.py:115
  151.5 0.0 copy-done
  151.5 0.7 copy.10
Async XLA Ops:
  147.6 3.9 %copy-start = (bf16[4,2,96,128]{3,2,1,0:T(8,128)(2,1)S(1)}, bf16[4,2,96,128]{3,2,1,0:T(8,128)(2,1)}, u32[]{:S(2)}) copy-start(bf16[4,2,96,128]{3,2,1,0:T(8,128)(2,1)} %get-tuple-element.28) | copy-start | bytes 589828

commit v6 on v5

v6 whole, which is shorter than its diff:
```python
import functools
import math
import types

import jax
import jax.numpy as jnp
from jax import lax
from jax.experimental import pallas as pl
from jax.experimental.pallas import tpu as pltpu
from jax.sharding import PartitionSpec as P

EPSILON = 1e-06
MESH = pl.DeviceIdType.MESH
F32 = jnp.float32
BF16 = jnp.bfloat16
ROWS = 32
SENDS = 128
COT, RES, OWN, PREV, NEXT = range(SENDS, SENDS + 20, 4)
CH = 4
VMEM_BYTES = 60 * 1024 * 1024


def coords():
    return lax.axis_index("row"), lax.axis_index("ch")


def place(r, c):
    return lax.rem(r, 4), lax.rem(r // 4, 2), r // 8, c // 2, lax.rem(c, 2)


def device(x, y_hi, z, y_lo, core):
    return z * 8 + y_hi * 4 + x, y_lo * 2 + core


def owner(f, row):
    x, y_hi, z, _, _ = place(row, 0)
    return device(x, f // 2, z, f % 2, y_hi)


class Links:
    def __init__(self, send, recv):
        self.send, self.recv, self.sent, self.at = send, recv, [], 0

    def greet(self, peers, count):
        barrier = pltpu.get_barrier_semaphore()
        for peer in peers:
            pl.semaphore_signal(barrier, inc=1, device_id=peer, device_id_type=MESH)
        pl.semaphore_wait(barrier, count)

    def copy(self, src, dst, to, own=None, recv=None):
        k = self.at
        self.at += 1
        mark = self.recv.at[k if recv is None else recv]
        far = pltpu.make_async_remote_copy(
            src_ref=src,
            dst_ref=dst,
            send_sem=self.send.at[k],
            recv_sem=mark,
            device_id=to,
            device_id_type=MESH,
        )
        if own is None:
            far.start()
        else:
            pl.when(jnp.logical_not(own))(far.start)
            pl.when(own)(pltpu.make_async_copy(src, dst, mark).start)
        self.sent.append((far, own))
        return far

    def arrive(self, dst, k):
        pltpu.make_async_copy(dst, dst, self.recv.at[k]).wait()

    def finish(self):
        for far, own in self.sent:
            if own is None:
                far.wait_send()
            else:
                pl.when(jnp.logical_not(own))(far.wait_send)


def fused(cid, body, held, made, scratch, count):
    names = [*held, *made, *scratch]

    def kernel(*refs):
        body(Links(*refs[-2:]), types.SimpleNamespace(**dict(zip(names, refs))))

    return pl.pallas_call(
        kernel,
        out_shape=[jax.ShapeDtypeStruct(s, t) for s, t, _ in made.values()],
        in_specs=[pl.BlockSpec(memory_space=m) for _, m in held.values()],
        out_specs=[pl.BlockSpec(memory_space=m) for _, _, m in made.values()],
        scratch_shapes=[*scratch.values()] + [pltpu.SemaphoreType.DMA((n,)) for n in count],
        compiler_params=pltpu.CompilerParams(
            collective_id=cid, has_side_effects=True, vmem_limit_bytes=VMEM_BYTES
        ),
        name="fused_%d" % cid,
    )(*[array for array, _ in held.values()])


def compute(body, outs, *ins, scratch=(), name):
    return pl.pallas_call(
        body,
        out_shape=[jax.ShapeDtypeStruct(s, t) for s, t in outs],
        in_specs=[pl.BlockSpec(memory_space=pltpu.VMEM)] * len(ins),
        out_specs=[pl.BlockSpec(memory_space=pltpu.VMEM)] * len(outs),
        scratch_shapes=list(scratch),
        compiler_params=pltpu.CompilerParams(vmem_limit_bytes=VMEM_BYTES),
        name=name,
    )(*ins)


def dot(a, b):
    return lax.dot_general(a, b, (((1,), (0,)), ((), ())), preferred_element_type=F32)


def dot_t(a, b):
    return lax.dot_general(a, b, (((1,), (1,)), ((), ())), preferred_element_type=F32)


def move(block, by):
    lanes = block.shape[1]
    at = lax.broadcasted_iota(jnp.int32, block.shape, 1)
    if by > 0:
        return jnp.where(at == 0, 0.0, pltpu.roll(block, 1, axis=1))
    return jnp.where(at == lanes - 1, 0.0, pltpu.roll(block, lanes - 1, axis=1))


def ch_peers(r, c):
    return [(r, lax.rem(c + d, CH)) for d in range(1, CH)]


def near_rows(r):
    return lax.rem(r + ROWS - 1, ROWS), lax.rem(r + 1, ROWS)


def same(a, b):
    return jnp.logical_and(a[0] == b[0], a[1] == b[1])


def greet_frames(me, sources, targets):
    barrier = pltpu.get_barrier_semaphore()
    for peer in sources:
        def tell(peer=peer):
            pl.semaphore_signal(barrier, inc=1, device_id=peer, device_id_type=MESH)

        pl.when(jnp.logical_not(same(peer, me)))(tell)
    _, y_hi, _, _, core = place(*me)
    pl.semaphore_wait(barrier, len(targets) - 2 + 2 * (core - y_hi) * (core - y_hi))


def sigmoid(v):
    return 1.0 / (1.0 + jnp.exp(-v))


def gain_columns(rows, which):
    blocks = [jnp.broadcast_to(rows[b, which : which + 1, :], (128, 128)).T[:96] for b in range(CH)]
    return jnp.concatenate(blocks, 0)


class Place:
    def __init__(self):
        r, c = self.r, self.c = self.me = coords()
        x, y_hi, z, y_lo, core = self.x, self.y_hi, self.z, self.y_lo, self.core = place(r, c)
        self.slot = core * 4 + x
        self.frame = y_hi * 2 + y_lo
        self.low, self.high = near_rows(r)
        self.c_near = (1 - y_lo) * 2 + core
        self.sibling = (r, y_lo * 2 + 1 - core)
        self.near = (r, self.c_near)
        self.chs = ch_peers(r, c)
        self.xs = [device(lax.rem(x + d, 4), y_hi, z, y_lo, core) for d in range(1, 4)]
        self.cross = [device(lax.rem(x + d, 4), y_hi, z, y_lo, 1 - core) for d in range(1, 4)]
        self.zs = [device(x, y_hi, lax.rem(z + d, 4), y_lo, core) for d in range(1, 4)]
        self.across = device(x, 1 - y_hi, z, y_lo, core)
        self.targets = [owner(f, r) for f in range(4)]
        self.row = z * 8 + core * 4 + x
        self.sources = [(self.row, b) for b in range(CH)]

    def greet(self):
        at = self
        alike = at.chs + at.xs + at.cross + at.zs + [at.across, (at.low, at.c), (at.high, at.c)]
        there = [(i, b) for i in near_rows(at.row) for b in range(CH)]
        whose = [owner(f, i) for i in (at.low, at.high) for f in range(4)]
        greet_frames(at.me, at.targets + at.sources + whose + alike, at.targets + at.sources + there + alike)


def front(links, at, m):
    r, c, near, sibling = at.r, at.c, at.near, at.sibling
    every, act = m.every, m.act
    here = pltpu.make_async_copy(m.feat, every.at[c, :, pl.ds(1, 2)], m.mark.at[0])
    here.start()
    weights = pltpu.make_async_copy(m.w_far, m.w, m.mark.at[1])
    weights.start()
    m.gain_rows[c] = jnp.zeros((8, 128), F32)
    pad = jnp.zeros((1, 32), F32)
    m.gain_rows[c, 0:1, :] = jnp.concatenate([m.gain_in[...].astype(F32), pad], 1)
    m.gain_rows[c, 1:2, :] = jnp.concatenate([m.gain_attn[...].astype(F32), pad], 1)
    at.greet()
    pairs = [pl.ds(2 * p, 2) for p in range(2)]
    to_near, edges = [], []
    for two in pairs:
        to_near.append(links.copy(m.feat.at[two], every.at[c, two, pl.ds(1, 2)], near))
        edges.append(links.copy(m.feat.at[two, 1], every.at[c, two, 0], (at.high, c)))
        edges.append(links.copy(m.feat.at[two, 0], every.at[c, two, 3], (at.low, c)))
    to_sib = links.copy(m.feat, every.at[c, :, pl.ds(1, 2)], sibling)
    gains = [links.copy(m.gain_rows.at[c], m.gain_rows.at[c], to) for to in at.chs]
    for f in range(4):
        own = same(at.targets[f], at.me)
        links.copy(m.cot.at[f], m.cot_frame.at[c], at.targets[f], own=own, recv=COT + c)
    passed, near_edges, sib_edges = [], [], []
    for p, two in enumerate(pairs):
        to_near[p].wait_recv()
        part = every.at[at.c_near, two, pl.ds(1, 2)]
        near_edges.append(links.copy(every.at[at.c_near, two, 2], every.at[at.c_near, two, 0], (at.high, c)))
        near_edges.append(links.copy(every.at[at.c_near, two, 1], every.at[at.c_near, two, 3], (at.low, c)))
        passed.append(links.copy(part, part, sibling))
        for n, h in enumerate((0, 3)):
            edges[2 * p + n].wait_recv()
            part = every.at[c, two, h]
            sib_edges.append(links.copy(part, part, sibling))
    for b in range(CH):
        links.arrive(m.cot_frame.at[b], COT + b)
    for b in range(CH):
        for h in range(2):
            m.cot_full[pl.ds(96 * b, 96), pl.ds(128 * h, 128)] = m.cot_frame[b, h]
    m.g[at.slot] = dot(m.w_out[...], m.cot_full[...]).astype(BF16)
    at.g_first = [links.copy(m.g.at[at.slot], m.g.at[at.slot], to) for to in (at.xs[0], at.xs[2], sibling)]
    for copy in gains:
        copy.wait_recv()
    gain = gain_columns(m.gain_rows, 0)

    def activate(f, h):
        v = jnp.concatenate([every[b, f, h] for b in range(CH)], 0).astype(F32)
        inv = lax.rsqrt(jnp.mean(v * v, 0, keepdims=True) + EPSILON)
        before = v * inv * gain
        a = before * sigmoid(before)
        if h == 0:
            a = jnp.where(r == 0, 0.0, a)
        elif h == 3:
            a = jnp.where(r == ROWS - 1, 0.0, a)
        else:
            m.inv_in[2 * f + h - 1 : 2 * f + h, :] = inv
        act[:, pl.ds((4 * f + h) * 128, 128)] = a.astype(BF16)

    here.wait()
    to_sib.wait_recv()
    passed[0].wait_recv()
    for f in range(2):
        activate(f, 1)
        activate(f, 2)
    far_edges = []
    for p, two in enumerate(pairs):
        for n, h in enumerate((0, 3)):
            near_edges[2 * p + n].wait_recv()
            part = every.at[at.c_near, two, h]
            far_edges.append(links.copy(part, part, sibling))
    passed[1].wait_recv()
    for f in range(2, 4):
        activate(f, 1)
        activate(f, 2)
    weights.wait()
    for p in range(2):
        for n in range(2):
            sib_edges[2 * p + n].wait_recv()
            far_edges[2 * p + n].wait_recv()
        for f in (2 * p, 2 * p + 1):
            activate(f, 0)
            activate(f, 3)
        for f in (2 * p, 2 * p + 1):
            acc = jnp.zeros((288, 256), F32)
            for t in range(3):
                source = f + t - 2
                if source < 0:
                    continue
                for h in range(3):
                    taps = m.w[pl.ds(9 * t + 3 * h, 3)].reshape(288, 384)
                    acc += dot(taps, act[:, pl.ds((4 * source + h) * 128, 256)])
            for h in range(2):
                y = acc[:, 128 * h : 128 * h + 128]
                out = move(y[:96], 1) + y[96:192] + move(y[192:], -1)
                m.res[f, h] = (every[c, f, h + 1].astype(F32) + out).astype(BF16)
            own = same(at.targets[f], at.me)
            links.copy(m.res.at[f], m.res_frame.at[c], at.targets[f], own=own, recv=RES + c)


def attention(links, at, m):
    scale = 1.0 / math.sqrt(384)
    x, z, core, slot, sibling = at.x, at.z, at.core, at.slot, at.sibling
    q, g, k, v, k_t = m.q, m.g, m.k, m.v, m.k_t
    w_qkv = m.w_qkv

    def relay_ring(first, ref, base, i, rows, peers, forward):
        on = []
        for side in range(2):
            first[side].wait_recv()
            came = base + lax.rem(i + 3 - 2 * side, 4)
            part = ref.at[came, pl.ds(rows * side, rows)]
            on.append(links.copy(part, part, peers[2 * side]))
            if forward:
                on.append(links.copy(ref.at[came], ref.at[came], sibling))
        return on

    g_on = relay_ring(at.g_first, g, core * 4, x, 192, at.xs, True)
    gain = gain_columns(m.gain_rows, 1)
    gain = jnp.concatenate([gain, gain], 1)
    for b in range(CH):
        links.arrive(m.res_frame.at[b], RES + b)
    for b in range(CH):
        for h in range(2):
            m.full[pl.ds(96 * b, 96), pl.ds(128 * h, 128)] = m.res_frame[b, h]
    centre = m.full[...].astype(F32)
    inv = lax.rsqrt(jnp.mean(centre * centre, 0, keepdims=True) + EPSILON)
    m.norm[z] = (centre * inv * gain).astype(BF16).astype(F32).T.astype(BF16)
    n_first = [links.copy(m.norm.at[z], m.norm.at[z], to) for to in (at.zs[0], at.zs[2])]
    q[slot] = dot(m.norm[z], w_qkv[:, :384]).T.astype(BF16)
    q_first = [links.copy(q.at[slot], q.at[slot], to) for to in (at.xs[0], at.xs[2], sibling)]

    def project(j):
        k[j] = dot(m.norm[j], w_qkv[:, 384:768]).astype(BF16)
        v[j] = dot(m.norm[j], w_qkv[:, 768:]).astype(BF16)
        k_t[:, pl.ds(pl.multiple_of(256 * j, 256), 256)] = k[j].T

    def tile(b, j):
        s = dot(k[j], q[b]) * scale
        top = jnp.max(s, 0, keepdims=True)
        e = jnp.exp(s - top)
        p = dot(v[j], g[b])
        m.exps[j, b] = e
        m.grad_p[j, b] = p
        m.tops[j, pl.ds(b, 1), :] = top
        m.sums[j, pl.ds(b, 1), :] = jnp.sum(e, 0, keepdims=True)
        m.deltas[j, pl.ds(b, 1), :] = jnp.sum(e * p, 0, keepdims=True)

    def block(dk, dx):
        other = core + dk - 2 * core * dk
        return other * 4 + lax.rem(x + dx, 4)

    def key(dz):
        return lax.rem(z + dz, 4)

    def tiles(count, unroll, which):
        def step(n, carry):
            dk, dx, dz = which(n)
            tile(block(dk, dx), key(dz))
            return carry

        lax.fori_loop(0, count, step, 0, unroll=unroll)

    project(z)
    g_on[1].wait_recv()
    g_on[3].wait_recv()
    g_on[0].wait_recv()
    g_on[2].wait_recv()
    far_x = core * 4 + lax.rem(x + 2, 4)
    g_last = links.copy(g.at[far_x], g.at[far_x], sibling)
    at.g_first[2].wait_recv()
    q_first[2].wait_recv()
    tiles(2, 2, lambda n: (n, 0, 0))
    for t in range(3):
        for n in range(3):
            piece = jnp.concatenate([m.w[9 * t + 3 * h + n] for h in range(3)], 0)
            m.w_t[t, pl.ds(384 * n, 384), :] = piece.T
    n_on = relay_ring(n_first, m.norm, 0, z, 128, at.zs, False)
    q_on = relay_ring(q_first, q, core * 4, x, 192, at.xs, True)
    project(key(1))
    project(key(3))
    tiles(4, 4, lambda n: (n // 2, 0, 1 + 2 * lax.rem(n, 2)))
    q_on[1].wait_recv()
    q_on[3].wait_recv()

    def beside(n):
        dz = n // 4
        return lax.rem(n // 2, 2), 1 + 2 * lax.rem(n, 2), dz + dz // 2

    tiles(12, 4, beside)
    q_on[0].wait_recv()
    q_on[2].wait_recv()
    q_last = links.copy(q.at[far_x], q.at[far_x], sibling)
    n_on[0].wait_recv()
    n_on[1].wait_recv()
    project(key(2))

    def beyond(n):
        dx = n // 2
        return lax.rem(n, 2), dx + dx // 2, 2

    tiles(6, 3, beyond)
    tiles(4, 4, lambda n: (0, 2, n))
    q_last.wait_recv()
    g_last.wait_recv()
    tiles(4, 4, lambda n: (1, 2, n))

    tops = [m.tops[j] for j in range(4)]
    top = functools.reduce(jnp.maximum, tops)
    shift = [jnp.exp(t - top) for t in tops]
    m.stats[0] = top
    m.stats[1] = sum(m.sums[j] * shift[j] for j in range(4))
    m.stats[2] = sum(m.deltas[j] * shift[j] for j in range(4))
    peers = at.xs + at.cross + [sibling]
    shared = [links.copy(m.stats, m.all_stats.at[n], to) for n, to in enumerate(peers)]
    for copy in shared:
        copy.wait_recv()
    parts = [m.stats] + [m.all_stats.at[n] for n in range(7)]
    top = functools.reduce(jnp.maximum, [p[0] for p in parts])
    total = sum(p[1] * jnp.exp(p[0] - top) for p in parts)
    m.delta[...] = sum(p[2] * jnp.exp(p[0] - top) for p in parts) / total
    for j in range(4):
        m.weights[j] = jnp.exp(m.tops[j] - top) / total

    def rows_of(j):
        return pl.ds(pl.multiple_of(256 * j, 256), 256)

    def weigh(b, j):
        prob = m.exps[j, b] * m.weights[j, pl.ds(b, 1), :]
        m.prob[b, rows_of(j), :] = prob.astype(BF16)
        m.grad_s[b, rows_of(j), :] = (prob * (m.grad_p[j, b] - m.delta[pl.ds(b, 1), :])).astype(BF16)

    def key_grad(j):
        for_k = sum(dot_t(m.grad_s[b, rows_of(j), :], q[b]) for b in range(8)) * scale
        for_v = sum(dot_t(m.prob[b, rows_of(j), :], g[b]) for b in range(8))
        return for_k, for_v

    for b in range(8):
        weigh(b, key(2))
    for n, grad in enumerate(key_grad(key(2))):
        m.far_kv[n] = grad.astype(BF16)
    halves = [pl.ds(0, 128), pl.ds(128, 128)]
    by = [at.zs[0], at.zs[2]]
    far = [[links.copy(m.far_kv.at[n, halves[i]], m.via_kv.at[i, n], by[i]) for n in range(2)] for i in range(2)]
    for dz in (0, 1, 3):
        for dx in range(4):
            weigh(block(1, dx), key(dz))
    sib = []
    for dx in range(4):
        m.sib_out[dx] = (dot(k_t[...], m.grad_s[block(1, dx)]) * scale).astype(BF16)
        sib.append(links.copy(m.sib_out.at[dx], m.sib_in.at[dx], sibling))
    for dz in (0, 1, 3):
        for dx in range(4):
            weigh(block(0, dx), key(dz))
    back = []
    for i, dz in enumerate((1, 3)):
        for n, grad in enumerate(key_grad(key(dz))):
            m.near_kv[i, n] = grad
            m.send_kv[i, n, halves[1 - i]] = grad[128 * (1 - i) : 128 * (2 - i)].astype(BF16)
            src, dst = m.send_kv.at[i, n, halves[1 - i]], m.came_kv.at[i, n, halves[1 - i]]
            back.append(links.copy(src, dst, by[i]))
    for n, dx in enumerate((2, 1, 3, 0)):
        for_q = dot(k_t[...], m.grad_s[block(0, dx)]) * scale
        sib[dx].wait_recv()
        for_q += m.sib_in[dx].astype(F32)
        if dx:
            m.send_q[n] = for_q.astype(BF16)
            back.append(links.copy(m.send_q.at[n], m.came_q.at[n], at.xs[dx - 1]))
        else:
            m.own_q[...] = for_q
    for i in range(2):
        for n in range(2):
            far[i][n].wait_recv()
            grad = m.near_kv[i, n, halves[i], :] + m.via_kv[i, n].astype(F32)
            m.send_kv[i, n, halves[i]] = grad.astype(BF16)
            back.append(links.copy(m.send_kv.at[i, n, halves[i]], m.came_kv.at[i, n, halves[i]], by[i]))
    for n, grad in enumerate(key_grad(z)):
        m.own_kv[n] = grad
    for copy in back:
        copy.wait_recv()
    for_q = m.own_q[...] + sum(m.came_q[n].astype(F32) for n in range(3))
    for_k, for_v = [m.own_kv[n] + m.came_kv[0, n].astype(F32) + m.came_kv[1, n].astype(F32) for n in range(2)]
    back_normed = (
        dot(w_qkv[:, :384], for_q.astype(BF16))
        + dot_t(w_qkv[:, 384:768], for_k.astype(BF16))
        + dot_t(w_qkv[:, 768:], for_v.astype(BF16))
    )
    scaled = back_normed.astype(BF16).astype(F32) * gain
    centre = m.full[...].astype(F32)
    inner = jnp.mean(centre * scaled, 0, keepdims=True)
    out = m.cot_full[...].astype(F32) + inv * scaled - centre * (inv * inv * inv * inner)
    for b in range(CH):
        for h in range(2):
            m.grad[b, h] = out[96 * b : 96 * b + 96, 128 * h : 128 * h + 128].astype(BF16)
    row_low, row_high = near_rows(at.row)
    for b in range(CH):
        to = at.sources[b]
        links.copy(m.grad.at[b], m.own.at[at.frame], to, own=same(to, at.me), recv=OWN + at.frame)
    for b in range(CH):
        links.copy(m.grad.at[b, 1], m.prev_g.at[at.frame], (row_high, b), recv=PREV + at.frame)
        links.copy(m.grad.at[b, 0], m.next_g.at[at.frame], (row_low, b), recv=NEXT + at.frame)


def tail(links, at, m):
    r, c, x, y_hi, z = at.r, at.c, at.x, at.y_hi, at.z
    xs, zs, across, chs = at.xs, at.zs, at.across, at.chs
    own, act, w_t, every, inv_in, gain_rows = m.own, m.act, m.w_t, m.every, m.inv_in, m.gain_rows
    rows, lines, weight, part, all_part, inner, all_inner = m.rows, m.lines, m.weight, m.part, m.all_part, m.inner, m.all_inner
    came1, came2, came3, sum1, sum2, sum3 = m.came1, m.came2, m.came3, m.sum1, m.sum2, m.sum3
    mark, flat, out = m.mark, m.flat, m.out
    x_at = [lax.rem(x + d, 4) for d in range(1, 4)]
    z_at = [lax.rem(z + d, 4) for d in range(1, 4)]
    halves = (
        (x, xs, x_at, z, zs, z_at),
        (z, zs, z_at, x, xs, x_at),
    )
    for f in range(4):
        links.arrive(own.at[f], OWN + f)
    moved = []
    for f in range(4):
        both = []
        for h in range(2):
            y = own[f, h].astype(F32)
            both.append(jnp.concatenate([move(y, -1), y, move(y, 1)], 0).astype(BF16))
        moved.append(jnp.concatenate(both, 1))
    for t in range(3):
        for h in range(3):
            acc = jnp.zeros((288, 384), F32)
            for f in range(4):
                source = f + t - 2
                if source < 0:
                    continue
                acc += dot_t(moved[f], act[:, pl.ds((4 * source + h) * 128, 256)])
            for lane in range(3):
                at = (3 * (3 * t + h) + lane) * 288
                weight[pl.ds(at, 288), :] = acc[:, 128 * lane : 128 * lane + 128].astype(BF16)
    weight[pl.ds(27 * 288, 416), :] = jnp.zeros((416, 128), BF16)
    first = []
    for half, (a, peers, ats, _, _, _) in enumerate(halves):
        for d in range(3):
            src = weight.at[pl.ds(4096 * half + 1024 * ats[d], 1024)]
            first.append(links.copy(src, came1.at[half, d], peers[d]))
    for f in range(4):
        links.arrive(m.prev_g.at[f], PREV + f)
        links.arrive(m.next_g.at[f], NEXT + f)
    for f in range(4):
        rows[f, 0] = jnp.where(r == 0, 0.0, m.prev_g[f].astype(F32)).astype(BF16)
        rows[f, 1] = own[f, 0]
        rows[f, 2] = own[f, 1]
        rows[f, 3] = jnp.where(r == ROWS - 1, 0.0, m.next_g[f].astype(F32)).astype(BF16)
    for f in range(4):
        for h in range(3):
            for k in range(2):
                lines[f, pl.ds(96 * h, 96), pl.ds(128 * k, 128)] = rows[f, 2 - h + k]
    gain = gain_columns(gain_rows, 0)
    for f in range(4):
        acc = jnp.zeros((1152, 256), F32)
        for t in range(3):
            source = f + 2 - t
            if source > 3:
                continue
            acc += dot(w_t[t], lines[source])
        for h in range(2):
            y = acc[:, 128 * h : 128 * h + 128]
            total = move(y[:384], -1) + y[384:768] + move(y[768:], 1)
            v = jnp.concatenate([every[b, f, h + 1] for b in range(CH)], 0).astype(F32)
            before = v * inv_in[2 * f + h : 2 * f + h + 1, :] * gain
            sig = sigmoid(before)
            slope = sig * (1.0 + before * (1.0 - sig))
            inner[2 * f + h : 2 * f + h + 1, :] = jnp.sum(v * slope * gain * total, 0, keepdims=True)
            for b in range(CH):
                part[b, f, h] = total[96 * b : 96 * b + 96].astype(BF16)
    parts = []
    for d in range(3):
        parts.append(links.copy(part.at[chs[d][1]], all_part.at[d], chs[d]))
        parts.append(links.copy(inner, all_inner.at[d], chs[d]))
    for copy in first:
        copy.wait_recv()
    second = []
    for half, (a, _, _, b, peers, ats) in enumerate(halves):
        total = weight[pl.ds(4096 * half + 1024 * a, 1024), :].astype(F32)
        for d in range(3):
            total += came1[half, d].astype(F32)
        sum1[half] = total.astype(BF16)
        for d in range(3):
            src = sum1.at[half, pl.ds(256 * ats[d], 256)]
            second.append(links.copy(src, came2.at[half, d], peers[d]))
    for copy in second:
        copy.wait_recv()
    third = []
    for half, (a, _, _, b, _, _) in enumerate(halves):
        total = sum1[half, pl.ds(256 * b, 256), :].astype(F32)
        for d in range(3):
            total += came2[half, d].astype(F32)
        sum2[half] = total.astype(BF16)
        src = sum2.at[half, pl.ds(128 * (1 - y_hi), 128)]
        third.append(links.copy(src, came3.at[half], across))
    for copy in third:
        copy.wait_recv()
    fourth, kept = [], []
    for half, (a, _, _, b, _, _) in enumerate(halves):
        total = sum2[half, pl.ds(128 * y_hi, 128), :].astype(F32) + came3[half].astype(F32)
        sum3[half] = total.astype(BF16)
        at = flat.at[pl.ds(4096 * half + 1024 * a + 256 * b + 128 * y_hi, 128)]
        kept.append(pltpu.make_async_copy(sum3.at[half], at, mark.at[half]))
        kept[half].start()
        fourth.append(links.copy(sum3.at[half], at, across))
    fifth = []
    for half, (a, _, _, b, peers, _) in enumerate(halves):
        kept[half].wait()
        fourth[half].wait_recv()
        at = flat.at[pl.ds(4096 * half + 1024 * a + 256 * b, 256)]
        for d in range(3):
            fifth.append(links.copy(at, at, peers[d]))
    sixth = []
    for half, (a, peers, _, _, _, _) in enumerate(halves):
        for d in range(3):
            fifth[3 * half + d].wait_recv()
        at = flat.at[pl.ds(4096 * half + 1024 * a, 1024)]
        for d in range(3):
            sixth.append(links.copy(at, at, peers[d]))
    for copy in parts:
        copy.wait_recv()
    mean = (inner[...] + all_inner[0] + all_inner[1] + all_inner[2]) / 384.0
    gain = jnp.broadcast_to(gain_rows[c, 0:1, :], (128, 128)).T[:96]
    for f in range(4):
        for h in range(2):
            v = every[c, f, h + 1].astype(F32)
            inv = inv_in[2 * f + h : 2 * f + h + 1, :]
            total = part[c, f, h].astype(F32)
            for d in range(3):
                total += all_part[d, f, h].astype(F32)
            before = v * inv * gain
            sig = sigmoid(before)
            scaled = total * (sig * (1.0 + before * (1.0 - sig))) * gain
            cube = inv * inv * inv * mean[2 * f + h : 2 * f + h + 1, :]
            out[f, h] = (own[f, h].astype(F32) + inv * scaled - v * cube).astype(BF16)
    for copy in sixth:
        copy.wait_recv()


def whole(links, m):
    at = Place()
    front(links, at, m)
    attention(links, at, m)
    tail(links, at, m)
    links.finish()


def widen_kernel(scale, flat, out):
    for k in range(9):
        for lane in range(3):
            piece = flat[pl.ds((3 * k + lane) * 288, 288), :].astype(F32) * scale
            out[pl.ds(288 * k, 288), pl.ds(128 * lane, 128)] = piece


def on_device(features, gain_in, w_conv, gain_attn, w_qkv, w_out, cotangent):
    near, far = pltpu.VMEM, pl.ANY
    held = {
        "feat": (features, far),
        "cot": (cotangent, far),
        "w_far": (w_conv, far),
        "gain_in": (gain_in.reshape(1, 96), near),
        "gain_attn": (gain_attn.reshape(1, 96), near),
        "w_qkv": (w_qkv, near),
        "w_out": (w_out, near),
    }
    made = {"out": ((4, 2, 96, 128), BF16, near), "flat": ((8192, 128), BF16, far)}
    b16 = {
        "every": (4, 4, 4, 96, 128),
        "w": (27, 96, 384),
        "act": (384, 2048),
        "res": (4, 2, 96, 128),
        "cot_frame": (4, 2, 96, 128),
        "res_frame": (4, 2, 96, 128),
        "full": (384, 256),
        "cot_full": (384, 256),
        "norm": (4, 256, 384),
        "q": (8, 384, 256),
        "g": (8, 384, 256),
        "k": (4, 256, 384),
        "v": (4, 256, 384),
        "k_t": (384, 1024),
        "prob": (8, 1024, 256),
        "grad_s": (8, 1024, 256),
        "far_kv": (2, 256, 384),
        "via_kv": (2, 2, 128, 384),
        "send_kv": (2, 2, 256, 384),
        "came_kv": (2, 2, 256, 384),
        "sib_out": (4, 384, 256),
        "sib_in": (4, 384, 256),
        "send_q": (3, 384, 256),
        "came_q": (3, 384, 256),
        "grad": (4, 2, 96, 128),
        "own": (4, 2, 96, 128),
        "prev_g": (4, 96, 128),
        "next_g": (4, 96, 128),
        "w_t": (3, 1152, 288),
        "rows": (4, 4, 96, 128),
        "lines": (4, 288, 256),
        "weight": (8192, 128),
        "part": (4, 4, 2, 96, 128),
        "all_part": (3, 4, 2, 96, 128),
        "came1": (2, 3, 1024, 128),
        "came2": (2, 3, 256, 128),
        "came3": (2, 128, 128),
        "sum1": (2, 1024, 128),
        "sum2": (2, 256, 128),
        "sum3": (2, 128, 128),
    }
    f32 = {
        "inv_in": (8, 128),
        "gain_rows": (4, 8, 128),
        "exps": (4, 8, 256, 256),
        "grad_p": (4, 8, 256, 256),
        "tops": (4, 8, 256),
        "sums": (4, 8, 256),
        "deltas": (4, 8, 256),
        "stats": (3, 8, 256),
        "all_stats": (7, 3, 8, 256),
        "weights": (4, 8, 256),
        "delta": (8, 256),
        "near_kv": (2, 2, 256, 384),
        "own_kv": (2, 256, 384),
        "own_q": (384, 256),
        "inner": (8, 128),
        "all_inner": (3, 8, 128),
    }
    scratch = {n: pltpu.VMEM(s, BF16) for n, s in b16.items()}
    scratch |= {n: pltpu.VMEM(s, F32) for n, s in f32.items()}
    scratch["mark"] = pltpu.SemaphoreType.DMA((2,))
    out, flat = fused(0, whole, held, made, scratch, (SENDS, NEXT + 4))
    cell_scale = 1.0 / math.sqrt(32768)
    (grad_weights,) = compute(
        functools.partial(widen_kernel, cell_scale),
        [((2592, 384), F32)],
        flat,
        name="widen",
    )
    return out, grad_weights.reshape(27, 96, 384)


def solution(mesh):
    return jax.shard_map(
        on_device,
        mesh=mesh,
        in_specs=(
            P(None, "row", "ch", None),
            P("ch"),
            P(None, "ch", None),
            P("ch"),
            P(),
            P(),
            P(None, "row", "ch", None),
        ),
        out_specs=(P(None, "row", "ch", None), P(None, "ch", None)),
        check_vma=False,
    )
```

time: 153 us -> 135 us (0.88)
  Pallas kernels: 151 us -> 133 us
    pallas_call x3 -> x1, Pallas kernels: 147 us -> 129 us  [fused(): pl.pallas_call(kernel, out_shape=[jax.ShapeDtypeStruct(s, t) for s, t, _...]
where the time goes in v6:
time: 135 us; the launch traced here: 134 us
  Pallas kernels  133 us (99%)
    pallas_call x1, Pallas kernels, fused(): pl.pallas_call(kernel, out_shape=[jax.ShapeDtypeStruct(s, t) for s, t, _...  129 us
    pallas_call x1, Pallas kernels, compute(): pl.pallas_call(body, out_shape=[jax.ShapeDtypeStruct(s, t) for s, t in ou...  3.87 us

profile of v6, /device:TPU:8, one launch (start us, length us, event | category | flops | bytes accessed | tf_op | source)
XLA Modules:
  0.0 134.0 jit_solution(1941199456114075872)
XLA Ops:
  0.6 128.8 %fused_0.1 = (bf16[4,2,96,128]{3,2,1,0:T(8,128)(2,1)}, bf16[8192,128]{1,0:T(8,128)(2,1)}) custom-call(bf16[4,2,96,128]{3,2,1,0:T(8,128)(2,1)} %refs_0_.1, bf16[4,2,96,128]{3,2,1,0:T(8,128)(2,1)} %refs_1_.1, bf16[27,96,384]{2,1,0:T(8,128)(2,1)} %refs_2_.1, bf16[1,96]{1,0:T(2,128)(2,1)} %bitcast.4, bf16[1,96]{1,0:T(2,128)(2,1)} %bitcast.5, ...), custom_call_target="tpu_custom_call" | custom-call | tf_op jit(solution)/shard_map/fused_0/pallas_call | solution.py:87
  129.4 0.0 copy-start
  129.4 3.9 %widen.1 = f32[2592,384]{1,0:T(8,128)} custom-call(bf16[8192,128]{1,0:T(8,128)(2,1)} %get-tuple-element.5.flat), custom_call_target="tpu_custom_call" | custom-call | tf_op jit(solution)/shard_map/widen/pallas_call | solution.py:101
  133.3 0.0 copy-done
  133.3 0.7 copy.10
Async XLA Ops:
  129.4 3.9 %copy-start = (bf16[4,2,96,128]{3,2,1,0:T(8,128)(2,1)S(1)}, bf16[4,2,96,128]{3,2,1,0:T(8,128)(2,1)}, u32[]{:S(2)}) copy-start(bf16[4,2,96,128]{3,2,1,0:T(8,128)(2,1)} %get-tuple-element.8) | copy-start | bytes 589828

commit v7 on v6

--- a/solution.py
+++ b/solution.py
@@ -97,18 +97,6 @@
     )(*[array for array, _ in held.values()])
 
 
-def compute(body, outs, *ins, scratch=(), name):
-    return pl.pallas_call(
-        body,
-        out_shape=[jax.ShapeDtypeStruct(s, t) for s, t in outs],
-        in_specs=[pl.BlockSpec(memory_space=pltpu.VMEM)] * len(ins),
-        out_specs=[pl.BlockSpec(memory_space=pltpu.VMEM)] * len(outs),
-        scratch_shapes=list(scratch),
-        compiler_params=pltpu.CompilerParams(vmem_limit_bytes=VMEM_BYTES),
-        name=name,
-    )(*ins)
-
-
 def dot(a, b):
     return lax.dot_general(a, b, (((1,), (0,)), ((), ())), preferred_element_type=F32)
 
@@ -187,7 +175,7 @@
 def front(links, at, m):
     r, c, near, sibling = at.r, at.c, at.near, at.sibling
     every, act = m.every, m.act
-    here = pltpu.make_async_copy(m.feat, every.at[c, :, pl.ds(1, 2)], m.mark.at[0])
+    here = pltpu.make_async_copy(m.feat, every.at[c], m.mark.at[0])
     here.start()
     weights = pltpu.make_async_copy(m.w_far, m.w, m.mark.at[1])
     weights.start()
@@ -197,27 +185,60 @@
     m.gain_rows[c, 1:2, :] = jnp.concatenate([m.gain_attn[...].astype(F32), pad], 1)
     at.greet()
     pairs = [pl.ds(2 * p, 2) for p in range(2)]
-    to_near, edges = [], []
-    for two in pairs:
-        to_near.append(links.copy(m.feat.at[two], every.at[c, two, pl.ds(1, 2)], near))
-        edges.append(links.copy(m.feat.at[two, 1], every.at[c, two, 0], (at.high, c)))
-        edges.append(links.copy(m.feat.at[two, 0], every.at[c, two, 3], (at.low, c)))
-    to_sib = links.copy(m.feat, every.at[c, :, pl.ds(1, 2)], sibling)
     gains = [links.copy(m.gain_rows.at[c], m.gain_rows.at[c], to) for to in at.chs]
+    to_near = [links.copy(m.feat.at[two], every.at[c, two], near) for two in pairs]
+    to_sib = links.copy(m.feat, every.at[c], sibling)
+    for copy in gains:
+        copy.wait_recv()
+    gain = gain_columns(m.gain_rows, 0)
+    passed = []
+    for p, two in enumerate(pairs):
+        to_near[p].wait_recv()
+        part = every.at[at.c_near, two]
+        passed.append(links.copy(part, part, sibling))
     for f in range(4):
         own = same(at.targets[f], at.me)
         links.copy(m.cot.at[f], m.cot_frame.at[c], at.targets[f], own=own, recv=COT + c)
-    passed, near_edges, sib_edges = [], [], []
+
+    def activate(f, h):
+        v = jnp.concatenate([every[b, f, h] for b in range(CH)], 0).astype(F32)
+        inv = lax.rsqrt(jnp.mean(v * v, 0, keepdims=True) + EPSILON)
+        before = v * inv * gain
+        m.inv_in[2 * f + h : 2 * f + h + 1, :] = inv
+        act[:, pl.ds((2 * f + h) * 128, 128)] = (before * sigmoid(before)).astype(BF16)
+
+    here.wait()
+    to_sib.wait_recv()
+    weights.wait()
+    edges = []
     for p, two in enumerate(pairs):
-        to_near[p].wait_recv()
-        part = every.at[at.c_near, two, pl.ds(1, 2)]
-        near_edges.append(links.copy(every.at[at.c_near, two, 2], every.at[at.c_near, two, 0], (at.high, c)))
-        near_edges.append(links.copy(every.at[at.c_near, two, 1], every.at[at.c_near, two, 3], (at.low, c)))
-        passed.append(links.copy(part, part, sibling))
-        for n, h in enumerate((0, 3)):
-            edges[2 * p + n].wait_recv()
-            part = every.at[c, two, h]
-            sib_edges.append(links.copy(part, part, sibling))
+        passed[p].wait_recv()
+        for f in (2 * p, 2 * p + 1):
+            activate(f, 0)
+            activate(f, 1)
+        for f in (2 * p, 2 * p + 1):
+            by_tap = []
+            for h in range(3):
+                acc = jnp.zeros((288, 256), F32)
+                for t in range(3):
+                    source = f + t - 2
+                    if source >= 0:
+                        taps = m.w[pl.ds(9 * t + 3 * h, 3)].reshape(288, 384)
+                        acc += dot(taps, act[:, pl.ds(256 * source, 256)])
+                by_tap.append((acc[:, :128], acc[:, 128:]))
+            lines = (
+                by_tap[2][0],
+                by_tap[2][1] + by_tap[1][0],
+                by_tap[1][1] + by_tap[0][0],
+                by_tap[0][1],
+            )
+            lines = [move(y[:96], 1) + y[96:192] + move(y[192:], -1) for y in lines]
+            m.edge_out[0, f] = lines[0].astype(BF16)
+            m.edge_out[1, f] = lines[3].astype(BF16)
+            m.conv_own[f, 0] = lines[1]
+            m.conv_own[f, 1] = lines[2]
+        edges.append(links.copy(m.edge_out.at[0, two], m.edge_in.at[0, two], (at.low, c)))
+        edges.append(links.copy(m.edge_out.at[1, two], m.edge_in.at[1, two], (at.high, c)))
     for b in range(CH):
         links.arrive(m.cot_frame.at[b], COT + b)
     for b in range(CH):
@@ -225,60 +246,14 @@
             m.cot_full[pl.ds(96 * b, 96), pl.ds(128 * h, 128)] = m.cot_frame[b, h]
     m.g[at.slot] = dot(m.w_out[...], m.cot_full[...]).astype(BF16)
     at.g_first = [links.copy(m.g.at[at.slot], m.g.at[at.slot], to) for to in (at.xs[0], at.xs[2], sibling)]
-    for copy in gains:
-        copy.wait_recv()
-    gain = gain_columns(m.gain_rows, 0)
-
-    def activate(f, h):
-        v = jnp.concatenate([every[b, f, h] for b in range(CH)], 0).astype(F32)
-        inv = lax.rsqrt(jnp.mean(v * v, 0, keepdims=True) + EPSILON)
-        before = v * inv * gain
-        a = before * sigmoid(before)
-        if h == 0:
-            a = jnp.where(r == 0, 0.0, a)
-        elif h == 3:
-            a = jnp.where(r == ROWS - 1, 0.0, a)
-        else:
-            m.inv_in[2 * f + h - 1 : 2 * f + h, :] = inv
-        act[:, pl.ds((4 * f + h) * 128, 128)] = a.astype(BF16)
-
-    here.wait()
-    to_sib.wait_recv()
-    passed[0].wait_recv()
-    for f in range(2):
-        activate(f, 1)
-        activate(f, 2)
-    far_edges = []
-    for p, two in enumerate(pairs):
-        for n, h in enumerate((0, 3)):
-            near_edges[2 * p + n].wait_recv()
-            part = every.at[at.c_near, two, h]
-            far_edges.append(links.copy(part, part, sibling))
-    passed[1].wait_recv()
-    for f in range(2, 4):
-        activate(f, 1)
-        activate(f, 2)
-    weights.wait()
     for p in range(2):
-        for n in range(2):
-            sib_edges[2 * p + n].wait_recv()
-            far_edges[2 * p + n].wait_recv()
+        edges[2 * p].wait_recv()
+        edges[2 * p + 1].wait_recv()
         for f in (2 * p, 2 * p + 1):
-            activate(f, 0)
-            activate(f, 3)
-        for f in (2 * p, 2 * p + 1):
-            acc = jnp.zeros((288, 256), F32)
-            for t in range(3):
-                source = f + t - 2
-                if source < 0:
-                    continue
-                for h in range(3):
-                    taps = m.w[pl.ds(9 * t + 3 * h, 3)].reshape(288, 384)
-                    acc += dot(taps, act[:, pl.ds((4 * source + h) * 128, 256)])
-            for h in range(2):
-                y = acc[:, 128 * h : 128 * h + 128]
-                out = move(y[:96], 1) + y[96:192] + move(y[192:], -1)
-                m.res[f, h] = (every[c, f, h + 1].astype(F32) + out).astype(BF16)
+            before = jnp.where(r == 0, 0.0, m.edge_in[1, f].astype(F32))
+            after = jnp.where(r == ROWS - 1, 0.0, m.edge_in[0, f].astype(F32))
+            m.res[f, 0] = (every[c, f, 0].astype(F32) + (m.conv_own[f, 0] + before)).astype(BF16)
+            m.res[f, 1] = (every[c, f, 1].astype(F32) + (m.conv_own[f, 1] + after)).astype(BF16)
             own = same(at.targets[f], at.me)
             links.copy(m.res.at[f], m.res_frame.at[c], at.targets[f], own=own, recv=RES + c)
 
@@ -501,13 +476,17 @@
     )
     for f in range(4):
         links.arrive(own.at[f], OWN + f)
-    moved = []
+        links.arrive(m.prev_g.at[f], PREV + f)
+        links.arrive(m.next_g.at[f], NEXT + f)
     for f in range(4):
-        both = []
-        for h in range(2):
-            y = own[f, h].astype(F32)
-            both.append(jnp.concatenate([move(y, -1), y, move(y, 1)], 0).astype(BF16))
-        moved.append(jnp.concatenate(both, 1))
+        rows[f, 0] = jnp.where(r == 0, 0.0, m.prev_g[f].astype(F32)).astype(BF16)
+        rows[f, 1] = own[f, 0]
+        rows[f, 2] = own[f, 1]
+        rows[f, 3] = jnp.where(r == ROWS - 1, 0.0, m.next_g[f].astype(F32)).astype(BF16)
+        for h in range(4):
+            y = rows[f, h].astype(F32)
+            at_lanes = pl.ds(128 * h, 128)
+            m.moved[f, :, at_lanes] = jnp.concatenate([move(y, -1), y, move(y, 1)], 0).astype(BF16)
     for t in range(3):
         for h in range(3):
             acc = jnp.zeros((288, 384), F32)
@@ -515,7 +494,7 @@
                 source = f + t - 2
                 if source < 0:
                     continue
-                acc += dot_t(moved[f], act[:, pl.ds((4 * source + h) * 128, 256)])
+                acc += dot_t(m.moved[f, :, pl.ds(128 * (2 - h), 256)], act[:, pl.ds(256 * source, 256)])
             for lane in range(3):
                 at = (3 * (3 * t + h) + lane) * 288
                 weight[pl.ds(at, 288), :] = acc[:, 128 * lane : 128 * lane + 128].astype(BF16)
@@ -525,14 +504,6 @@
         for d in range(3):
             src = weight.at[pl.ds(4096 * half + 1024 * ats[d], 1024)]
             first.append(links.copy(src, came1.at[half, d], peers[d]))
-    for f in range(4):
-        links.arrive(m.prev_g.at[f], PREV + f)
-        links.arrive(m.next_g.at[f], NEXT + f)
-    for f in range(4):
-        rows[f, 0] = jnp.where(r == 0, 0.0, m.prev_g[f].astype(F32)).astype(BF16)
-        rows[f, 1] = own[f, 0]
-        rows[f, 2] = own[f, 1]
-        rows[f, 3] = jnp.where(r == ROWS - 1, 0.0, m.next_g[f].astype(F32)).astype(BF16)
     for f in range(4):
         for h in range(3):
             for k in range(2):
@@ -548,7 +519,7 @@
         for h in range(2):
             y = acc[:, 128 * h : 128 * h + 128]
             total = move(y[:384], -1) + y[384:768] + move(y[768:], 1)
-            v = jnp.concatenate([every[b, f, h + 1] for b in range(CH)], 0).astype(F32)
+            v = jnp.concatenate([every[b, f, h] for b in range(CH)], 0).astype(F32)
             before = v * inv_in[2 * f + h : 2 * f + h + 1, :] * gain
             sig = sigmoid(before)
             slope = sig * (1.0 + before * (1.0 - sig))
@@ -610,7 +581,7 @@
     gain = jnp.broadcast_to(gain_rows[c, 0:1, :], (128, 128)).T[:96]
     for f in range(4):
         for h in range(2):
-            v = every[c, f, h + 1].astype(F32)
+            v = every[c, f, h].astype(F32)
             inv = inv_in[2 * f + h : 2 * f + h + 1, :]
             total = part[c, f, h].astype(F32)
             for d in range(3):
@@ -632,11 +603,23 @@
     links.finish()
 
 
-def widen_kernel(scale, flat, out):
+def widen_kernel(scale, flat, out, near, wide, into, back):
+    come = [
+        pltpu.make_async_copy(flat.at[pl.ds(864 * k, 864)], near.at[k], into.at[k]) for k in range(9)
+    ]
+    go = [
+        pltpu.make_async_copy(wide.at[k], out.at[pl.ds(288 * k, 288)], back.at[k]) for k in range(9)
+    ]
+    for copy in come:
+        copy.start()
     for k in range(9):
+        come[k].wait()
         for lane in range(3):
-            piece = flat[pl.ds((3 * k + lane) * 288, 288), :].astype(F32) * scale
-            out[pl.ds(288 * k, 288), pl.ds(128 * lane, 128)] = piece
+            piece = near[k, pl.ds(288 * lane, 288), :].astype(F32) * scale
+            wide[k, :, pl.ds(128 * lane, 128)] = piece
+        go[k].start()
+    for copy in go:
+        copy.wait()
 
 
 def on_device(features, gain_in, w_conv, gain_attn, w_qkv, w_out, cotangent):
@@ -652,9 +635,12 @@
     }
     made = {"out": ((4, 2, 96, 128), BF16, near), "flat": ((8192, 128), BF16, far)}
     b16 = {
-        "every": (4, 4, 4, 96, 128),
+        "every": (4, 4, 2, 96, 128),
         "w": (27, 96, 384),
-        "act": (384, 2048),
+        "act": (384, 1024),
+        "edge_out": (2, 4, 96, 128),
+        "edge_in": (2, 4, 96, 128),
+        "moved": (4, 288, 512),
         "res": (4, 2, 96, 128),
         "cot_frame": (4, 2, 96, 128),
         "res_frame": (4, 2, 96, 128),
@@ -695,6 +681,7 @@
     }
     f32 = {
         "inv_in": (8, 128),
+        "conv_own": (4, 2, 96, 128),
         "gain_rows": (4, 8, 128),
         "exps": (4, 8, 256, 256),
         "grad_p": (4, 8, 256, 256),
@@ -716,12 +703,20 @@
     scratch["mark"] = pltpu.SemaphoreType.DMA((2,))
     out, flat = fused(0, whole, held, made, scratch, (SENDS, NEXT + 4))
     cell_scale = 1.0 / math.sqrt(32768)
-    (grad_weights,) = compute(
+    grad_weights = pl.pallas_call(
         functools.partial(widen_kernel, cell_scale),
-        [((2592, 384), F32)],
-        flat,
+        out_shape=jax.ShapeDtypeStruct((2592, 384), F32),
+        in_specs=[pl.BlockSpec(memory_space=pl.ANY)],
+        out_specs=pl.BlockSpec(memory_space=pl.ANY),
+        scratch_shapes=[
+            pltpu.VMEM((9, 864, 128), BF16),
+            pltpu.VMEM((9, 288, 384), F32),
+            pltpu.SemaphoreType.DMA((9,)),
+            pltpu.SemaphoreType.DMA((9,)),
+        ],
+        compiler_params=pltpu.CompilerParams(vmem_limit_bytes=VMEM_BYTES),
         name="widen",
-    )
+    )(flat)
     return out, grad_weights.reshape(27, 96, 384)
 
 

time: 135 us -> 130 us (0.963)
  Pallas kernels: 133 us -> 128 us
    pallas_call x1, Pallas kernels: 129 us -> 125 us  [fused(): pl.pallas_call(kernel, out_shape=[jax.ShapeDtypeStruct(s, t) for s, t, _...]
where the time goes in v7:
time: 130 us; the launch traced here: 129 us
  Pallas kernels  128 us (98%)
    pallas_call x1, Pallas kernels, fused(): pl.pallas_call(kernel, out_shape=[jax.ShapeDtypeStruct(s, t) for s, t, _...  125 us
    pallas_call x1, Pallas kernels, on_device(): pl.pallas_call(functools.partial(widen_kernel, cell_scale), out_shape=jax...  3.09 us

profile of v7, /device:TPU:8, one launch (start us, length us, event | category | flops | bytes accessed | tf_op | source)
XLA Modules:
  0.0 129.3 jit_solution(11383378596604767554)
XLA Ops:
  0.6 124.8 %fused_0.1 = (bf16[4,2,96,128]{3,2,1,0:T(8,128)(2,1)}, bf16[8192,128]{1,0:T(8,128)(2,1)}) custom-call(bf16[4,2,96,128]{3,2,1,0:T(8,128)(2,1)} %refs_0_.1, bf16[4,2,96,128]{3,2,1,0:T(8,128)(2,1)} %refs_1_.1, bf16[27,96,384]{2,1,0:T(8,128)(2,1)} %refs_2_.1, bf16[1,96]{1,0:T(2,128)(2,1)} %bitcast.4, bf16[1,96]{1,0:T(2,128)(2,1)} %bitcast.5, ...), custom_call_target="tpu_custom_call" | custom-call | tf_op jit(solution)/shard_map/fused_0/pallas_call | solution.py:87
  125.5 0.0 copy-start
  125.5 3.1 %widen.1 = f32[2592,384]{1,0:T(8,128)} custom-call(bf16[8192,128]{1,0:T(8,128)(2,1)} %get-tuple-element.5.flat), custom_call_target="tpu_custom_call" | custom-call | tf_op jit(solution)/shard_map/widen/pallas_call | solution.py:706
  128.6 0.0 copy-done
  128.6 0.7 copy.10
Async XLA Ops:
  125.5 3.1 %copy-start = (bf16[4,2,96,128]{3,2,1,0:T(8,128)(2,1)S(1)}, bf16[4,2,96,128]{3,2,1,0:T(8,128)(2,1)}, u32[]{:S(2)}) copy-start(bf16[4,2,96,128]{3,2,1,0:T(8,128)(2,1)} %get-tuple-element.8) | copy-start | bytes 589828

commit v8 on v7

--- a/solution.py
+++ b/solution.py
@@ -466,14 +466,53 @@
     xs, zs, across, chs = at.xs, at.zs, at.across, at.chs
     own, act, w_t, every, inv_in, gain_rows = m.own, m.act, m.w_t, m.every, m.inv_in, m.gain_rows
     rows, lines, weight, part, all_part, inner, all_inner = m.rows, m.lines, m.weight, m.part, m.all_part, m.inner, m.all_inner
-    came1, came2, came3, sum1, sum2, sum3 = m.came1, m.came2, m.came3, m.sum1, m.sum2, m.sum3
     mark, flat, out = m.mark, m.flat, m.out
-    x_at = [lax.rem(x + d, 4) for d in range(1, 4)]
-    z_at = [lax.rem(z + d, 4) for d in range(1, 4)]
-    halves = (
-        (x, xs, x_at, z, zs, z_at),
-        (z, zs, z_at, x, xs, x_at),
-    )
+    ring_x = (x, [lax.rem(x + d, 4) for d in range(1, 4)], xs)
+    ring_z = (z, [lax.rem(z + d, 4) for d in range(1, 4)], zs)
+    ring_y = (y_hi, [1 - y_hi], [across])
+    stripes = []
+    for n, (base, size, rings) in enumerate(
+        (
+            (0, 2048, (ring_y, ring_x, ring_z)),
+            (2048, 3072, (ring_x, ring_z, ring_y)),
+            (5120, 3072, (ring_z, ring_y, ring_x)),
+        )
+    ):
+        steps, at_row = [], base
+        for p, (place_on, places, peers) in enumerate(rings):
+            size //= len(peers) + 1
+            start = at_row
+            at_row = at_row + place_on * size
+            came, total = getattr(m, "came_%d_%d" % (n, p)), getattr(m, "total_%d_%d" % (n, p))
+            steps.append((start, size, places, peers, at_row, came, total))
+        stripes.append(steps)
+
+    def rows_at(start, size):
+        return pl.ds(pl.multiple_of(start, 16), size)
+
+    def give(steps, p):
+        start, size, places, peers, _, came, _ = steps[p]
+        sent = []
+        for d, peer in enumerate(peers):
+            if p == 0:
+                src = weight.at[rows_at(start + places[d] * size, size)]
+            else:
+                src = steps[p - 1][6].at[rows_at(places[d] * size, size)]
+            sent.append(links.copy(src, came.at[d], peer))
+        return sent
+
+    def take(steps, p, sent):
+        start, size, _, peers, mine, came, total = steps[p]
+        for copy in sent:
+            copy.wait_recv()
+        if p == 0:
+            value = weight[rows_at(mine, size), :].astype(F32)
+        else:
+            value = steps[p - 1][6][rows_at(mine - start, size), :].astype(F32)
+        for d in range(len(peers)):
+            value += came[d].astype(F32)
+        total[...] = value.astype(BF16)
+
     for f in range(4):
         links.arrive(own.at[f], OWN + f)
         links.arrive(m.prev_g.at[f], PREV + f)
@@ -487,6 +526,7 @@
             y = rows[f, h].astype(F32)
             at_lanes = pl.ds(128 * h, 128)
             m.moved[f, :, at_lanes] = jnp.concatenate([move(y, -1), y, move(y, 1)], 0).astype(BF16)
+    first = []
     for t in range(3):
         for h in range(3):
             acc = jnp.zeros((288, 384), F32)
@@ -498,12 +538,9 @@
             for lane in range(3):
                 at = (3 * (3 * t + h) + lane) * 288
                 weight[pl.ds(at, 288), :] = acc[:, 128 * lane : 128 * lane + 128].astype(BF16)
-    weight[pl.ds(27 * 288, 416), :] = jnp.zeros((416, 128), BF16)
-    first = []
-    for half, (a, peers, ats, _, _, _) in enumerate(halves):
-        for d in range(3):
-            src = weight.at[pl.ds(4096 * half + 1024 * ats[d], 1024)]
-            first.append(links.copy(src, came1.at[half, d], peers[d]))
+        if t == 2:
+            weight[pl.ds(27 * 288, 416), :] = jnp.zeros((416, 128), BF16)
+        first.append(give(stripes[t], 0))
     for f in range(4):
         for h in range(3):
             for k in range(2):
@@ -526,55 +563,33 @@
             inner[2 * f + h : 2 * f + h + 1, :] = jnp.sum(v * slope * gain * total, 0, keepdims=True)
             for b in range(CH):
                 part[b, f, h] = total[96 * b : 96 * b + 96].astype(BF16)
-    parts = []
+    second, third, parts = [], [], []
+    for n, steps in enumerate(stripes):
+        take(steps, 0, first[n])
+        second.append(give(steps, 1))
     for d in range(3):
         parts.append(links.copy(part.at[chs[d][1]], all_part.at[d], chs[d]))
         parts.append(links.copy(inner, all_inner.at[d], chs[d]))
-    for copy in first:
-        copy.wait_recv()
-    second = []
-    for half, (a, _, _, b, peers, ats) in enumerate(halves):
-        total = weight[pl.ds(4096 * half + 1024 * a, 1024), :].astype(F32)
-        for d in range(3):
-            total += came1[half, d].astype(F32)
-        sum1[half] = total.astype(BF16)
-        for d in range(3):
-            src = sum1.at[half, pl.ds(256 * ats[d], 256)]
-            second.append(links.copy(src, came2.at[half, d], peers[d]))
-    for copy in second:
-        copy.wait_recv()
-    third = []
-    for half, (a, _, _, b, _, _) in enumerate(halves):
-        total = sum1[half, pl.ds(256 * b, 256), :].astype(F32)
-        for d in range(3):
-            total += came2[half, d].astype(F32)
-        sum2[half] = total.astype(BF16)
-        src = sum2.at[half, pl.ds(128 * (1 - y_hi), 128)]
-        third.append(links.copy(src, came3.at[half], across))
-    for copy in third:
-        copy.wait_recv()
-    fourth, kept = [], []
-    for half, (a, _, _, b, _, _) in enumerate(halves):
-        total = sum2[half, pl.ds(128 * y_hi, 128), :].astype(F32) + came3[half].astype(F32)
-        sum3[half] = total.astype(BF16)
-        at = flat.at[pl.ds(4096 * half + 1024 * a + 256 * b + 128 * y_hi, 128)]
-        kept.append(pltpu.make_async_copy(sum3.at[half], at, mark.at[half]))
-        kept[half].start()
-        fourth.append(links.copy(sum3.at[half], at, across))
-    fifth = []
-    for half, (a, _, _, b, peers, _) in enumerate(halves):
-        kept[half].wait()
-        fourth[half].wait_recv()
-        at = flat.at[pl.ds(4096 * half + 1024 * a + 256 * b, 256)]
-        for d in range(3):
-            fifth.append(links.copy(at, at, peers[d]))
-    sixth = []
-    for half, (a, peers, _, _, _, _) in enumerate(halves):
-        for d in range(3):
-            fifth[3 * half + d].wait_recv()
-        at = flat.at[pl.ds(4096 * half + 1024 * a, 1024)]
-        for d in range(3):
-            sixth.append(links.copy(at, at, peers[d]))
+    for n, steps in enumerate(stripes):
+        take(steps, 1, second[n])
+        third.append(give(steps, 2))
+    spread, kept = [], []
+    for n, steps in enumerate(stripes):
+        take(steps, 2, third[n])
+        _, size, _, peers, mine, _, total = steps[2]
+        at_flat = flat.at[rows_at(mine, size)]
+        kept.append(pltpu.make_async_copy(total, at_flat, mark.at[n]))
+        kept[n].start()
+        spread.append([links.copy(total, at_flat, peer) for peer in peers])
+    for p in (1, 0):
+        for n, steps in enumerate(stripes):
+            if p == 1:
+                kept[n].wait()
+            for copy in spread[n]:
+                copy.wait_recv()
+            _, size, _, peers, mine, _, _ = steps[p]
+            at_flat = flat.at[rows_at(mine, size)]
+            spread[n] = [links.copy(at_flat, at_flat, peer) for peer in peers]
     for copy in parts:
         copy.wait_recv()
     mean = (inner[...] + all_inner[0] + all_inner[1] + all_inner[2]) / 384.0
@@ -591,7 +606,7 @@
             scaled = total * (sig * (1.0 + before * (1.0 - sig))) * gain
             cube = inv * inv * inv * mean[2 * f + h : 2 * f + h + 1, :]
             out[f, h] = (own[f, h].astype(F32) + inv * scaled - v * cube).astype(BF16)
-    for copy in sixth:
+    for copy in spread[0] + spread[1] + spread[2]:
         copy.wait_recv()
 
 
@@ -672,13 +687,12 @@
         "weight": (8192, 128),
         "part": (4, 4, 2, 96, 128),
         "all_part": (3, 4, 2, 96, 128),
-        "came1": (2, 3, 1024, 128),
-        "came2": (2, 3, 256, 128),
-        "came3": (2, 128, 128),
-        "sum1": (2, 1024, 128),
-        "sum2": (2, 256, 128),
-        "sum3": (2, 128, 128),
     }
+    for n, (size, counts) in enumerate(((2048, (2, 4, 4)), (3072, (4, 4, 2)), (3072, (4, 2, 4)))):
+        for p, count in enumerate(counts):
+            size //= count
+            b16["came_%d_%d" % (n, p)] = (count - 1, size, 128)
+            b16["total_%d_%d" % (n, p)] = (size, 128)
     f32 = {
         "inv_in": (8, 128),
         "conv_own": (4, 2, 96, 128),
@@ -700,7 +714,7 @@
     }
     scratch = {n: pltpu.VMEM(s, BF16) for n, s in b16.items()}
     scratch |= {n: pltpu.VMEM(s, F32) for n, s in f32.items()}
-    scratch["mark"] = pltpu.SemaphoreType.DMA((2,))
+    scratch["mark"] = pltpu.SemaphoreType.DMA((3,))
     out, flat = fused(0, whole, held, made, scratch, (SENDS, NEXT + 4))
     cell_scale = 1.0 / math.sqrt(32768)
     grad_weights = pl.pallas_call(

time: 130 us -> 128 us (0.985)
  Pallas kernels: 128 us -> 126 us
    pallas_call x1, Pallas kernels: 125 us -> 123 us  [fused(): pl.pallas_call(kernel, out_shape=[jax.ShapeDtypeStruct(s, t) for s, t, _...]
where the time goes in v8:
time: 128 us
  Pallas kernels  126 us (98%)
    pallas_call x1, Pallas kernels, fused(): pl.pallas_call(kernel, out_shape=[jax.ShapeDtypeStruct(s, t) for s, t, _...  123 us
    pallas_call x1, Pallas kernels, on_device(): pl.pallas_call(functools.partial(widen_kernel, cell_scale), out_shape=jax...  3.09 us

profile of v8, /device:TPU:8, one launch (start us, length us, event | category | flops | bytes accessed | tf_op | source)
XLA Modules:
  0.0 127.5 jit_solution(17316489183823498447)
XLA Ops:
  0.6 123.1 %fused_0.1 = (bf16[4,2,96,128]{3,2,1,0:T(8,128)(2,1)}, bf16[8192,128]{1,0:T(8,128)(2,1)}) custom-call(bf16[4,2,96,128]{3,2,1,0:T(8,128)(2,1)} %refs_0_.1, bf16[4,2,96,128]{3,2,1,0:T(8,128)(2,1)} %refs_1_.1, bf16[27,96,384]{2,1,0:T(8,128)(2,1)} %refs_2_.1, bf16[1,96]{1,0:T(2,128)(2,1)} %bitcast.4, bf16[1,96]{1,0:T(2,128)(2,1)} %bitcast.5, ...), custom_call_target="tpu_custom_call" | custom-call | tf_op jit(solution)/shard_map/fused_0/pallas_call | solution.py:87
  123.7 0.0 copy-start
  123.7 3.1 %widen.1 = f32[2592,384]{1,0:T(8,128)} custom-call(bf16[8192,128]{1,0:T(8,128)(2,1)} %get-tuple-element.5.flat), custom_call_target="tpu_custom_call" | custom-call | tf_op jit(solution)/shard_map/widen/pallas_call | solution.py:720
  126.8 0.0 copy-done
  126.9 0.7 copy.10
Async XLA Ops:
  123.7 3.1 %copy-start = (bf16[4,2,96,128]{3,2,1,0:T(8,128)(2,1)S(1)}, bf16[4,2,96,128]{3,2,1,0:T(8,128)(2,1)}, u32[]{:S(2)}) copy-start(bf16[4,2,96,128]{3,2,1,0:T(8,128)(2,1)} %get-tuple-element.8) | copy-start | bytes 589828

commit v9 on v8

--- a/solution.py
+++ b/solution.py
@@ -324,10 +324,7 @@
     project(z)
     g_on[1].wait_recv()
     g_on[3].wait_recv()
-    g_on[0].wait_recv()
-    g_on[2].wait_recv()
     far_x = core * 4 + lax.rem(x + 2, 4)
-    g_last = links.copy(g.at[far_x], g.at[far_x], sibling)
     at.g_first[2].wait_recv()
     q_first[2].wait_recv()
     tiles(2, 2, lambda n: (n, 0, 0))
@@ -337,6 +334,9 @@
             m.w_t[t, pl.ds(384 * n, 384), :] = piece.T
     n_on = relay_ring(n_first, m.norm, 0, z, 128, at.zs, False)
     q_on = relay_ring(q_first, q, core * 4, x, 192, at.xs, True)
+    g_on[0].wait_recv()
+    g_on[2].wait_recv()
+    g_last = links.copy(g.at[far_x], g.at[far_x], sibling)
     project(key(1))
     project(key(3))
     tiles(4, 4, lambda n: (n // 2, 0, 1 + 2 * lax.rem(n, 2)))
@@ -393,58 +393,63 @@
     def key_grad(j):
         for_k = sum(dot_t(m.grad_s[b, rows_of(j), :], q[b]) for b in range(8)) * scale
         for_v = sum(dot_t(m.prob[b, rows_of(j), :], g[b]) for b in range(8))
-        return for_k, for_v
-
-    for b in range(8):
-        weigh(b, key(2))
-    for n, grad in enumerate(key_grad(key(2))):
-        m.far_kv[n] = grad.astype(BF16)
-    halves = [pl.ds(0, 128), pl.ds(128, 128)]
-    by = [at.zs[0], at.zs[2]]
-    far = [[links.copy(m.far_kv.at[n, halves[i]], m.via_kv.at[i, n], by[i]) for n in range(2)] for i in range(2)]
-    for dz in (0, 1, 3):
+        return dot_t(w_qkv[:, 384:768], for_k.astype(BF16)) + dot_t(w_qkv[:, 768:], for_v.astype(BF16))
+
+    halves = [pl.ds(0, 192), pl.ds(192, 192)]
+    rings = ((at.zs[0], at.zs[2]), (at.xs[0], at.xs[2]))
+    by_way, back = {}, []
+
+    def send_far(kind, value):
+        m.far[kind] = value.astype(BF16)
+        for i in range(2):
+            by_way[kind, i] = links.copy(m.far.at[kind, halves[i]], m.via.at[kind, i], rings[kind][i])
+
+    def send_half(kind, i, half, value):
+        m.send[kind, i, halves[half]] = value.astype(BF16)
+        src, dst = m.send.at[kind, i, halves[half]], m.came.at[kind, i, halves[half]]
+        back.append(links.copy(src, dst, rings[kind][i]))
+
+    def send_near(kind, i, value):
+        m.nearest[kind, i] = value
+        send_half(kind, i, 1 - i, value[192 * (1 - i) : 192 * (2 - i)])
+
+    def send_added(kind):
+        for i in range(2):
+            by_way[kind, i].wait_recv()
+            send_half(kind, i, i, m.nearest[kind, i, halves[i], :] + m.via[kind, i].astype(F32))
+
+    for dz in range(4):
         for dx in range(4):
             weigh(block(1, dx), key(dz))
     sib = []
     for dx in range(4):
         m.sib_out[dx] = (dot(k_t[...], m.grad_s[block(1, dx)]) * scale).astype(BF16)
         sib.append(links.copy(m.sib_out.at[dx], m.sib_in.at[dx], sibling))
-    for dz in (0, 1, 3):
+    for dz in range(4):
         for dx in range(4):
             weigh(block(0, dx), key(dz))
-    back = []
-    for i, dz in enumerate((1, 3)):
-        for n, grad in enumerate(key_grad(key(dz))):
-            m.near_kv[i, n] = grad
-            m.send_kv[i, n, halves[1 - i]] = grad[128 * (1 - i) : 128 * (2 - i)].astype(BF16)
-            src, dst = m.send_kv.at[i, n, halves[1 - i]], m.came_kv.at[i, n, halves[1 - i]]
-            back.append(links.copy(src, dst, by[i]))
-    for n, dx in enumerate((2, 1, 3, 0)):
-        for_q = dot(k_t[...], m.grad_s[block(0, dx)]) * scale
+
+    def query_grad(dx):
+        value = dot(k_t[...], m.grad_s[block(0, dx)]) * scale
         sib[dx].wait_recv()
-        for_q += m.sib_in[dx].astype(F32)
-        if dx:
-            m.send_q[n] = for_q.astype(BF16)
-            back.append(links.copy(m.send_q.at[n], m.came_q.at[n], at.xs[dx - 1]))
-        else:
-            m.own_q[...] = for_q
-    for i in range(2):
-        for n in range(2):
-            far[i][n].wait_recv()
-            grad = m.near_kv[i, n, halves[i], :] + m.via_kv[i, n].astype(F32)
-            m.send_kv[i, n, halves[i]] = grad.astype(BF16)
-            back.append(links.copy(m.send_kv.at[i, n, halves[i]], m.came_kv.at[i, n, halves[i]], by[i]))
-    for n, grad in enumerate(key_grad(z)):
-        m.own_kv[n] = grad
+        return value + m.sib_in[dx].astype(F32)
+
+    send_far(0, key_grad(key(2)))
+    send_far(1, query_grad(2))
+    send_near(1, 0, query_grad(1))
+    send_near(1, 1, query_grad(3))
+    send_near(0, 0, key_grad(key(1)))
+    send_near(0, 1, key_grad(key(3)))
+    send_added(1)
+    send_added(0)
+    m.own_sum[0] = key_grad(z)
+    m.own_sum[1] = query_grad(0)
     for copy in back:
         copy.wait_recv()
-    for_q = m.own_q[...] + sum(m.came_q[n].astype(F32) for n in range(3))
-    for_k, for_v = [m.own_kv[n] + m.came_kv[0, n].astype(F32) + m.came_kv[1, n].astype(F32) for n in range(2)]
-    back_normed = (
-        dot(w_qkv[:, :384], for_q.astype(BF16))
-        + dot_t(w_qkv[:, 384:768], for_k.astype(BF16))
-        + dot_t(w_qkv[:, 768:], for_v.astype(BF16))
-    )
+    by_key, by_query = [
+        m.own_sum[n] + m.came[n, 0].astype(F32) + m.came[n, 1].astype(F32) for n in range(2)
+    ]
+    back_normed = dot(w_qkv[:, :384], by_query.astype(BF16)) + by_key
     scaled = back_normed.astype(BF16).astype(F32) * gain
     centre = m.full[...].astype(F32)
     inner = jnp.mean(centre * scaled, 0, keepdims=True)
@@ -669,14 +674,12 @@
         "k_t": (384, 1024),
         "prob": (8, 1024, 256),
         "grad_s": (8, 1024, 256),
-        "far_kv": (2, 256, 384),
-        "via_kv": (2, 2, 128, 384),
-        "send_kv": (2, 2, 256, 384),
-        "came_kv": (2, 2, 256, 384),
+        "far": (2, 384, 256),
+        "via": (2, 2, 192, 256),
+        "send": (2, 2, 384, 256),
+        "came": (2, 2, 384, 256),
         "sib_out": (4, 384, 256),
         "sib_in": (4, 384, 256),
-        "send_q": (3, 384, 256),
-        "came_q": (3, 384, 256),
         "grad": (4, 2, 96, 128),
         "own": (4, 2, 96, 128),
         "prev_g": (4, 96, 128),
@@ -706,9 +709,8 @@
         "all_stats": (7, 3, 8, 256),
         "weights": (4, 8, 256),
         "delta": (8, 256),
-        "near_kv": (2, 2, 256, 384),
-        "own_kv": (2, 256, 384),
-        "own_q": (384, 256),
+        "nearest": (2, 2, 384, 256),
+        "own_sum": (2, 384, 256),
         "inner": (8, 128),
         "all_inner": (3, 8, 128),
     }

time: 128 us -> 127 us (level)
  Pallas kernels: 126 us -> 124 us
    pallas_call x1, Pallas kernels: 123 us -> 121 us  [fused(): pl.pallas_call(kernel, out_shape=[jax.ShapeDtypeStruct(s, t) for s, t, _...]
where the time goes in v9:
time: 127 us; the launch traced here: 126 us
  Pallas kernels  124 us (98%)
    pallas_call x1, Pallas kernels, fused(): pl.pallas_call(kernel, out_shape=[jax.ShapeDtypeStruct(s, t) for s, t, _...  121 us
    pallas_call x1, Pallas kernels, on_device(): pl.pallas_call(functools.partial(widen_kernel, cell_scale), out_shape=jax...  3.09 us

profile of v9, /device:TPU:8, one launch (start us, length us, event | category | flops | bytes accessed | tf_op | source)
XLA Modules:
  0.0 125.8 jit_solution(7817065602204301235)
XLA Ops:
  0.6 121.3 %fused_0.1 = (bf16[4,2,96,128]{3,2,1,0:T(8,128)(2,1)}, bf16[8192,128]{1,0:T(8,128)(2,1)}) custom-call(bf16[4,2,96,128]{3,2,1,0:T(8,128)(2,1)} %refs_0_.1, bf16[4,2,96,128]{3,2,1,0:T(8,128)(2,1)} %refs_1_.1, bf16[27,96,384]{2,1,0:T(8,128)(2,1)} %refs_2_.1, bf16[1,96]{1,0:T(2,128)(2,1)} %bitcast.4, bf16[1,96]{1,0:T(2,128)(2,1)} %bitcast.5, ...), custom_call_target="tpu_custom_call" | custom-call | tf_op jit(solution)/shard_map/fused_0/pallas_call | solution.py:87
  122.0 0.0 copy-start
  122.0 3.1 %widen.1 = f32[2592,384]{1,0:T(8,128)} custom-call(bf16[8192,128]{1,0:T(8,128)(2,1)} %get-tuple-element.5.flat), custom_call_target="tpu_custom_call" | custom-call | tf_op jit(solution)/shard_map/widen/pallas_call | solution.py:722
  125.1 0.0 copy-done
  125.1 0.7 copy.10
Async XLA Ops:
  122.0 3.1 %copy-start = (bf16[4,2,96,128]{3,2,1,0:T(8,128)(2,1)S(1)}, bf16[4,2,96,128]{3,2,1,0:T(8,128)(2,1)}, u32[]{:S(2)}) copy-start(bf16[4,2,96,128]{3,2,1,0:T(8,128)(2,1)} %get-tuple-element.8) | copy-start | bytes 589828

commit v10 on v9

--- a/solution.py
+++ b/solution.py
@@ -14,7 +14,7 @@
 F32 = jnp.float32
 BF16 = jnp.bfloat16
 ROWS = 32
-SENDS = 128
+SENDS = 168
 COT, RES, OWN, PREV, NEXT = range(SENDS, SENDS + 20, 4)
 CH = 4
 VMEM_BYTES = 60 * 1024 * 1024
@@ -475,12 +475,16 @@
     ring_x = (x, [lax.rem(x + d, 4) for d in range(1, 4)], xs)
     ring_z = (z, [lax.rem(z + d, 4) for d in range(1, 4)], zs)
     ring_y = (y_hi, [1 - y_hi], [across])
+    by_y, by_x, by_z = (ring_y, ring_x, ring_z), (ring_x, ring_z, ring_y), (ring_z, ring_y, ring_x)
     stripes = []
     for n, (base, size, rings) in enumerate(
         (
-            (0, 2048, (ring_y, ring_x, ring_z)),
-            (2048, 3072, (ring_x, ring_z, ring_y)),
-            (5120, 3072, (ring_z, ring_y, ring_x)),
+            (0, 1024, by_y),
+            (2048, 1536, by_x),
+            (5120, 1536, by_z),
+            (1024, 1024, by_y),
+            (3584, 1536, by_x),
+            (6656, 1536, by_z),
         )
     ):
         steps, at_row = [], base
@@ -531,7 +535,7 @@
             y = rows[f, h].astype(F32)
             at_lanes = pl.ds(128 * h, 128)
             m.moved[f, :, at_lanes] = jnp.concatenate([move(y, -1), y, move(y, 1)], 0).astype(BF16)
-    first = []
+    flying = [None] * 6
     for t in range(3):
         for h in range(3):
             acc = jnp.zeros((288, 384), F32)
@@ -545,7 +549,8 @@
                 weight[pl.ds(at, 288), :] = acc[:, 128 * lane : 128 * lane + 128].astype(BF16)
         if t == 2:
             weight[pl.ds(27 * 288, 416), :] = jnp.zeros((416, 128), BF16)
-        first.append(give(stripes[t], 0))
+        flying[t] = give(stripes[t], 0)
+        flying[t + 3] = give(stripes[t + 3], 0)
     for f in range(4):
         for h in range(3):
             for k in range(2):
@@ -568,33 +573,37 @@
             inner[2 * f + h : 2 * f + h + 1, :] = jnp.sum(v * slope * gain * total, 0, keepdims=True)
             for b in range(CH):
                 part[b, f, h] = total[96 * b : 96 * b + 96].astype(BF16)
-    second, third, parts = [], [], []
-    for n, steps in enumerate(stripes):
-        take(steps, 0, first[n])
-        second.append(give(steps, 1))
+    parts, kept = [], [None] * 6
+
+    def advance(group, p):
+        for n in range(3 * group, 3 * group + 3):
+            steps = stripes[n]
+            if p < 3:
+                take(steps, p, flying[n])
+            else:
+                for copy in flying[n]:
+                    copy.wait_recv()
+            if p < 2:
+                flying[n] = give(steps, p + 1)
+                continue
+            _, size, _, peers, mine, _, total = steps[4 - p]
+            src = dst = flat.at[rows_at(mine, size)]
+            if p == 2:
+                src = total
+                kept[n] = pltpu.make_async_copy(total, dst, mark.at[n])
+                kept[n].start()
+            elif p == 3:
+                kept[n].wait()
+            flying[n] = [links.copy(src, dst, peer) for peer in peers]
+
+    advance(0, 0)
+    advance(0, 1)
+    advance(1, 0)
     for d in range(3):
         parts.append(links.copy(part.at[chs[d][1]], all_part.at[d], chs[d]))
         parts.append(links.copy(inner, all_inner.at[d], chs[d]))
-    for n, steps in enumerate(stripes):
-        take(steps, 1, second[n])
-        third.append(give(steps, 2))
-    spread, kept = [], []
-    for n, steps in enumerate(stripes):
-        take(steps, 2, third[n])
-        _, size, _, peers, mine, _, total = steps[2]
-        at_flat = flat.at[rows_at(mine, size)]
-        kept.append(pltpu.make_async_copy(total, at_flat, mark.at[n]))
-        kept[n].start()
-        spread.append([links.copy(total, at_flat, peer) for peer in peers])
-    for p in (1, 0):
-        for n, steps in enumerate(stripes):
-            if p == 1:
-                kept[n].wait()
-            for copy in spread[n]:
-                copy.wait_recv()
-            _, size, _, peers, mine, _, _ = steps[p]
-            at_flat = flat.at[rows_at(mine, size)]
-            spread[n] = [links.copy(at_flat, at_flat, peer) for peer in peers]
+    for group, p in ((0, 2), (1, 1), (0, 3), (1, 2), (0, 4), (1, 3), (1, 4)):
+        advance(group, p)
     for copy in parts:
         copy.wait_recv()
     mean = (inner[...] + all_inner[0] + all_inner[1] + all_inner[2]) / 384.0
@@ -611,8 +620,9 @@
             scaled = total * (sig * (1.0 + before * (1.0 - sig))) * gain
             cube = inv * inv * inv * mean[2 * f + h : 2 * f + h + 1, :]
             out[f, h] = (own[f, h].astype(F32) + inv * scaled - v * cube).astype(BF16)
-    for copy in spread[0] + spread[1] + spread[2]:
-        copy.wait_recv()
+    for sent in flying:
+        for copy in sent:
+            copy.wait_recv()
 
 
 def whole(links, m):
@@ -691,7 +701,7 @@
         "part": (4, 4, 2, 96, 128),
         "all_part": (3, 4, 2, 96, 128),
     }
-    for n, (size, counts) in enumerate(((2048, (2, 4, 4)), (3072, (4, 4, 2)), (3072, (4, 2, 4)))):
+    for n, (size, counts) in enumerate(2 * ((1024, (2, 4, 4)), (1536, (4, 4, 2)), (1536, (4, 2, 4)))):
         for p, count in enumerate(counts):
             size //= count
             b16["came_%d_%d" % (n, p)] = (count - 1, size, 128)
@@ -716,7 +726,7 @@
     }
     scratch = {n: pltpu.VMEM(s, BF16) for n, s in b16.items()}
     scratch |= {n: pltpu.VMEM(s, F32) for n, s in f32.items()}
-    scratch["mark"] = pltpu.SemaphoreType.DMA((3,))
+    scratch["mark"] = pltpu.SemaphoreType.DMA((6,))
     out, flat = fused(0, whole, held, made, scratch, (SENDS, NEXT + 4))
     cell_scale = 1.0 / math.sqrt(32768)
     grad_weights = pl.pallas_call(

time: 127 us -> 129 us (1.016)
  no operation moved by 1% of the time
where the time goes in v10:
time: 129 us; the launch traced here: 127 us
  Pallas kernels  125 us (97%)
    pallas_call x1, Pallas kernels, fused(): pl.pallas_call(kernel, out_shape=[jax.ShapeDtypeStruct(s, t) for s, t, _...  122 us
    pallas_call x1, Pallas kernels, on_device(): pl.pallas_call(functools.partial(widen_kernel, cell_scale), out_shape=jax...  3.09 us

profile of v10, /device:TPU:8, one launch (start us, length us, event | category | flops | bytes accessed | tf_op | source)
XLA Modules:
  0.0 126.7 jit_solution(6108629133111740400)
XLA Ops:
  0.6 122.3 %fused_0.1 = (bf16[4,2,96,128]{3,2,1,0:T(8,128)(2,1)}, bf16[8192,128]{1,0:T(8,128)(2,1)}) custom-call(bf16[4,2,96,128]{3,2,1,0:T(8,128)(2,1)} %refs_0_.1, bf16[4,2,96,128]{3,2,1,0:T(8,128)(2,1)} %refs_1_.1, bf16[27,96,384]{2,1,0:T(8,128)(2,1)} %refs_2_.1, bf16[1,96]{1,0:T(2,128)(2,1)} %bitcast.4, bf16[1,96]{1,0:T(2,128)(2,1)} %bitcast.5, ...), custom_call_target="tpu_custom_call" | custom-call | tf_op jit(solution)/shard_map/fused_0/pallas_call | solution.py:87
  122.9 0.0 copy-start
  122.9 3.1 %widen.1 = f32[2592,384]{1,0:T(8,128)} custom-call(bf16[8192,128]{1,0:T(8,128)(2,1)} %get-tuple-element.5.flat), custom_call_target="tpu_custom_call" | custom-call | tf_op jit(solution)/shard_map/widen/pallas_call | solution.py:732
  126.0 0.0 copy-done
  126.0 0.7 copy.10
Async XLA Ops:
  122.9 3.1 %copy-start = (bf16[4,2,96,128]{3,2,1,0:T(8,128)(2,1)S(1)}, bf16[4,2,96,128]{3,2,1,0:T(8,128)(2,1)}, u32[]{:S(2)}) copy-start(bf16[4,2,96,128]{3,2,1,0:T(8,128)(2,1)} %get-tuple-element.8) | copy-start | bytes 589828

commit v11 on v9

--- a/solution.py
+++ b/solution.py
@@ -179,6 +179,12 @@
     here.start()
     weights = pltpu.make_async_copy(m.w_far, m.w, m.mark.at[1])
     weights.start()
+    projections = [
+        pltpu.make_async_copy(m.w_out_far, m.w_out, m.mark.at[2]),
+        pltpu.make_async_copy(m.w_qkv_far, m.w_qkv, m.mark.at[3]),
+    ]
+    for copy in projections:
+        copy.start()
     m.gain_rows[c] = jnp.zeros((8, 128), F32)
     pad = jnp.zeros((1, 32), F32)
     m.gain_rows[c, 0:1, :] = jnp.concatenate([m.gain_in[...].astype(F32), pad], 1)
@@ -200,12 +206,12 @@
         own = same(at.targets[f], at.me)
         links.copy(m.cot.at[f], m.cot_frame.at[c], at.targets[f], own=own, recv=COT + c)
 
-    def activate(f, h):
-        v = jnp.concatenate([every[b, f, h] for b in range(CH)], 0).astype(F32)
+    def activate(n):
+        v = jnp.concatenate([every[b, n // 2, lax.rem(n, 2)] for b in range(CH)], 0).astype(F32)
         inv = lax.rsqrt(jnp.mean(v * v, 0, keepdims=True) + EPSILON)
         before = v * inv * gain
-        m.inv_in[2 * f + h : 2 * f + h + 1, :] = inv
-        act[:, pl.ds((2 * f + h) * 128, 128)] = (before * sigmoid(before)).astype(BF16)
+        m.inv_in[pl.ds(n, 1), :] = inv
+        act[:, pl.ds(pl.multiple_of(128 * n, 128), 128)] = (before * sigmoid(before)).astype(BF16)
 
     here.wait()
     to_sib.wait_recv()
@@ -213,9 +219,12 @@
     edges = []
     for p, two in enumerate(pairs):
         passed[p].wait_recv()
-        for f in (2 * p, 2 * p + 1):
-            activate(f, 0)
-            activate(f, 1)
+
+        def step(n, carry, p=p):
+            activate(4 * p + n)
+            return carry
+
+        lax.fori_loop(0, 4, step, 0, unroll=2)
         for f in (2 * p, 2 * p + 1):
             by_tap = []
             for h in range(3):
@@ -244,6 +253,8 @@
     for b in range(CH):
         for h in range(2):
             m.cot_full[pl.ds(96 * b, 96), pl.ds(128 * h, 128)] = m.cot_frame[b, h]
+    for copy in projections:
+        copy.wait()
     m.g[at.slot] = dot(m.w_out[...], m.cot_full[...]).astype(BF16)
     at.g_first = [links.copy(m.g.at[at.slot], m.g.at[at.slot], to) for to in (at.xs[0], at.xs[2], sibling)]
     for p in range(2):
@@ -418,30 +429,50 @@
             by_way[kind, i].wait_recv()
             send_half(kind, i, i, m.nearest[kind, i, halves[i], :] + m.via[kind, i].astype(F32))
 
-    for dz in range(4):
-        for dx in range(4):
-            weigh(block(1, dx), key(dz))
-    sib = []
-    for dx in range(4):
-        m.sib_out[dx] = (dot(k_t[...], m.grad_s[block(1, dx)]) * scale).astype(BF16)
-        sib.append(links.copy(m.sib_out.at[dx], m.sib_in.at[dx], sibling))
-    for dz in range(4):
-        for dx in range(4):
-            weigh(block(0, dx), key(dz))
+    def weigh_all(dk):
+        def step(n, carry):
+            weigh(block(dk, lax.rem(n, 4)), key(n // 4))
+            return carry
+
+        lax.fori_loop(0, 16, step, 0, unroll=4)
+
+    def query_grads(dk, put):
+        def step(dx, carry):
+            put(dx, dot(k_t[...], m.grad_s[block(dk, dx)]) * scale)
+            return carry
+
+        lax.fori_loop(0, 4, step, 0)
+
+    def for_sibling(dx, value):
+        m.sib_out[dx] = value.astype(BF16)
+
+    def for_own(dx, value):
+        m.own_q[dx] = value
+
+    weigh_all(1)
+    query_grads(1, for_sibling)
+    sib = links.copy(m.sib_out, m.sib_in, sibling)
+    weigh_all(0)
+    send_far(0, key_grad(key(2)))
+    query_grads(0, for_own)
+    sib.wait_recv()
 
     def query_grad(dx):
-        value = dot(k_t[...], m.grad_s[block(0, dx)]) * scale
-        sib[dx].wait_recv()
-        return value + m.sib_in[dx].astype(F32)
-
-    send_far(0, key_grad(key(2)))
+        return m.own_q[dx] + m.sib_in[dx].astype(F32)
+
     send_far(1, query_grad(2))
     send_near(1, 0, query_grad(1))
     send_near(1, 1, query_grad(3))
-    send_near(0, 0, key_grad(key(1)))
-    send_near(0, 1, key_grad(key(3)))
+
+    def near_keys(i, carry):
+        m.nearest[0, i] = key_grad(key(1 + 2 * i))
+        return carry
+
+    lax.fori_loop(0, 2, near_keys, 0)
+    for i in range(2):
+        send_half(0, i, 1 - i, m.nearest[0, i, halves[1 - i], :])
+    send_added(0)
     send_added(1)
-    send_added(0)
     m.own_sum[0] = key_grad(z)
     m.own_sum[1] = query_grad(0)
     for copy in back:
@@ -623,15 +654,17 @@
     links.finish()
 
 
-def widen_kernel(scale, flat, out, near, wide, into, back):
+def widen_kernel(scale, flat, grad, out, grad_out, near, wide, into, back):
     come = [
         pltpu.make_async_copy(flat.at[pl.ds(864 * k, 864)], near.at[k], into.at[k]) for k in range(9)
     ]
     go = [
         pltpu.make_async_copy(wide.at[k], out.at[pl.ds(288 * k, 288)], back.at[k]) for k in range(9)
     ]
+    passing = pltpu.make_async_copy(grad, grad_out, into.at[9])
     for copy in come:
         copy.start()
+    passing.start()
     for k in range(9):
         come[k].wait()
         for lane in range(3):
@@ -640,6 +673,7 @@
         go[k].start()
     for copy in go:
         copy.wait()
+    passing.wait()
 
 
 def on_device(features, gain_in, w_conv, gain_attn, w_qkv, w_out, cotangent):
@@ -650,13 +684,15 @@
         "w_far": (w_conv, far),
         "gain_in": (gain_in.reshape(1, 96), near),
         "gain_attn": (gain_attn.reshape(1, 96), near),
-        "w_qkv": (w_qkv, near),
-        "w_out": (w_out, near),
+        "w_qkv_far": (w_qkv, far),
+        "w_out_far": (w_out, far),
     }
     made = {"out": ((4, 2, 96, 128), BF16, near), "flat": ((8192, 128), BF16, far)}
     b16 = {
         "every": (4, 4, 2, 96, 128),
         "w": (27, 96, 384),
+        "w_qkv": (384, 1152),
+        "w_out": (384, 384),
         "act": (384, 1024),
         "edge_out": (2, 4, 96, 128),
         "edge_in": (2, 4, 96, 128),
@@ -711,28 +747,29 @@
         "delta": (8, 256),
         "nearest": (2, 2, 384, 256),
         "own_sum": (2, 384, 256),
+        "own_q": (4, 384, 256),
         "inner": (8, 128),
         "all_inner": (3, 8, 128),
     }
     scratch = {n: pltpu.VMEM(s, BF16) for n, s in b16.items()}
     scratch |= {n: pltpu.VMEM(s, F32) for n, s in f32.items()}
-    scratch["mark"] = pltpu.SemaphoreType.DMA((3,))
+    scratch["mark"] = pltpu.SemaphoreType.DMA((4,))
     out, flat = fused(0, whole, held, made, scratch, (SENDS, NEXT + 4))
     cell_scale = 1.0 / math.sqrt(32768)
-    grad_weights = pl.pallas_call(
+    grad_weights, out = pl.pallas_call(
         functools.partial(widen_kernel, cell_scale),
-        out_shape=jax.ShapeDtypeStruct((2592, 384), F32),
-        in_specs=[pl.BlockSpec(memory_space=pl.ANY)],
-        out_specs=pl.BlockSpec(memory_space=pl.ANY),
+        out_shape=[jax.ShapeDtypeStruct((2592, 384), F32), jax.ShapeDtypeStruct(out.shape, BF16)],
+        in_specs=[pl.BlockSpec(memory_space=pl.ANY)] * 2,
+        out_specs=[pl.BlockSpec(memory_space=pl.ANY)] * 2,
         scratch_shapes=[
             pltpu.VMEM((9, 864, 128), BF16),
             pltpu.VMEM((9, 288, 384), F32),
-            pltpu.SemaphoreType.DMA((9,)),
+            pltpu.SemaphoreType.DMA((10,)),
             pltpu.SemaphoreType.DMA((9,)),
         ],
         compiler_params=pltpu.CompilerParams(vmem_limit_bytes=VMEM_BYTES),
         name="widen",
-    )(flat)
+    )(flat, out)
     return out, grad_weights.reshape(27, 96, 384)
 
 

time: 127 us -> 129 us (1.016)
  Pallas kernels: 124 us -> 126 us
    pallas_call x1, Pallas kernels: 3.09 us -> 7.24 us  [on_device(): pl.pallas_call(functools.partial(widen_kernel, cell_scale), out_shape=[ja...]
    pallas_call x1, Pallas kernels: 121 us -> 119 us  [fused(): pl.pallas_call(kernel, out_shape=[jax.ShapeDtypeStruct(s, t) for s, t, _...]
where the time goes in v11:
time: 129 us; the launch traced here: 127 us
  Pallas kernels  126 us (98%)
    pallas_call x1, Pallas kernels, fused(): pl.pallas_call(kernel, out_shape=[jax.ShapeDtypeStruct(s, t) for s, t, _...  119 us
    pallas_call x1, Pallas kernels, on_device(): pl.pallas_call(functools.partial(widen_kernel, cell_scale), out_shape=[ja...  7.24 us

profile of v11, /device:TPU:8, one launch (start us, length us, event | category | flops | bytes accessed | tf_op | source)
XLA Modules:
  0.0 127.2 jit_solution(8441468344941693544)
XLA Ops:
  0.6 119.1 %fused_0.1 = (bf16[4,2,96,128]{3,2,1,0:T(8,128)(2,1)}, bf16[8192,128]{1,0:T(8,128)(2,1)}) custom-call(bf16[4,2,96,128]{3,2,1,0:T(8,128)(2,1)} %refs_0_.1, bf16[4,2,96,128]{3,2,1,0:T(8,128)(2,1)} %refs_1_.1, bf16[27,96,384]{2,1,0:T(8,128)(2,1)} %refs_2_.1, bf16[1,96]{1,0:T(2,128)(2,1)} %bitcast.3, bf16[1,96]{1,0:T(2,128)(2,1)} %bitcast.4, ...), custom_call_target="tpu_custom_call" | custom-call | tf_op jit(solution)/shard_map/fused_0/pallas_call | solution.py:87
  119.7 7.2 %widen.1 = (f32[2592,384]{1,0:T(8,128)}, bf16[4,2,96,128]{3,2,1,0:T(8,128)(2,1)}) custom-call(bf16[8192,128]{1,0:T(8,128)(2,1)} %get-tuple-element.6.flat, bf16[4,2,96,128]{3,2,1,0:T(8,128)(2,1)} %get-tuple-element.7.grad), custom_call_target="tpu_custom_call" | custom-call | tf_op jit(solution)/shard_map/widen/pallas_call | solution.py:759

commit v12 on v11

--- a/solution.py
+++ b/solution.py
@@ -549,19 +549,24 @@
             value += came[d].astype(F32)
         total[...] = value.astype(BF16)
 
+    def prepare(f, h):
+        y = rows[f, h].astype(F32)
+        m.moved[f, :, pl.ds(128 * h, 128)] = jnp.concatenate([move(y, -1), y, move(y, 1)], 0).astype(BF16)
+
     for f in range(4):
         links.arrive(own.at[f], OWN + f)
+    for f in range(4):
+        for h in range(2):
+            rows[f, h + 1] = own[f, h]
+            prepare(f, h + 1)
+    for f in range(4):
         links.arrive(m.prev_g.at[f], PREV + f)
         links.arrive(m.next_g.at[f], NEXT + f)
     for f in range(4):
         rows[f, 0] = jnp.where(r == 0, 0.0, m.prev_g[f].astype(F32)).astype(BF16)
-        rows[f, 1] = own[f, 0]
-        rows[f, 2] = own[f, 1]
         rows[f, 3] = jnp.where(r == ROWS - 1, 0.0, m.next_g[f].astype(F32)).astype(BF16)
-        for h in range(4):
-            y = rows[f, h].astype(F32)
-            at_lanes = pl.ds(128 * h, 128)
-            m.moved[f, :, at_lanes] = jnp.concatenate([move(y, -1), y, move(y, 1)], 0).astype(BF16)
+        prepare(f, 0)
+        prepare(f, 3)
     first = []
     for t in range(3):
         for h in range(3):
@@ -613,19 +618,19 @@
     for n, steps in enumerate(stripes):
         take(steps, 2, third[n])
         _, size, _, peers, mine, _, total = steps[2]
-        at_flat = flat.at[rows_at(mine, size)]
-        kept.append(pltpu.make_async_copy(total, at_flat, mark.at[n]))
-        kept[n].start()
-        spread.append([links.copy(total, at_flat, peer) for peer in peers])
+        m.spread[rows_at(mine, size), :] = total[...]
+        spread.append([links.copy(total, m.spread.at[rows_at(mine, size)], peer) for peer in peers])
     for p in (1, 0):
         for n, steps in enumerate(stripes):
-            if p == 1:
-                kept[n].wait()
             for copy in spread[n]:
                 copy.wait_recv()
             _, size, _, peers, mine, _, _ = steps[p]
-            at_flat = flat.at[rows_at(mine, size)]
-            spread[n] = [links.copy(at_flat, at_flat, peer) for peer in peers]
+            src = dst = m.spread.at[rows_at(mine, size)]
+            if p == 0:
+                dst = flat.at[rows_at(mine, size)]
+                kept.append(pltpu.make_async_copy(src, dst, mark.at[n]))
+                kept[n].start()
+            spread[n] = [links.copy(src, dst, peer) for peer in peers]
     for copy in parts:
         copy.wait_recv()
     mean = (inner[...] + all_inner[0] + all_inner[1] + all_inner[2]) / 384.0
@@ -642,6 +647,8 @@
             scaled = total * (sig * (1.0 + before * (1.0 - sig))) * gain
             cube = inv * inv * inv * mean[2 * f + h : 2 * f + h + 1, :]
             out[f, h] = (own[f, h].astype(F32) + inv * scaled - v * cube).astype(BF16)
+    for copy in kept:
+        copy.wait()
     for copy in spread[0] + spread[1] + spread[2]:
         copy.wait_recv()
 
@@ -654,18 +661,22 @@
     links.finish()
 
 
-def widen_kernel(scale, flat, grad, out, grad_out, near, wide, into, back):
+def widen_kernel(scale, flat, grad, out, grad_out, near, wide, through, into, back):
     come = [
         pltpu.make_async_copy(flat.at[pl.ds(864 * k, 864)], near.at[k], into.at[k]) for k in range(9)
     ]
     go = [
         pltpu.make_async_copy(wide.at[k], out.at[pl.ds(288 * k, 288)], back.at[k]) for k in range(9)
     ]
-    passing = pltpu.make_async_copy(grad, grad_out, into.at[9])
+    enter = pltpu.make_async_copy(grad, through, into.at[9])
+    leave = pltpu.make_async_copy(through, grad_out, back.at[9])
     for copy in come:
         copy.start()
-    passing.start()
+    enter.start()
     for k in range(9):
+        if k == 4:
+            enter.wait()
+            leave.start()
         come[k].wait()
         for lane in range(3):
             piece = near[k, pl.ds(288 * lane, 288), :].astype(F32) * scale
@@ -673,7 +684,7 @@
         go[k].start()
     for copy in go:
         copy.wait()
-    passing.wait()
+    leave.wait()
 
 
 def on_device(features, gain_in, w_conv, gain_attn, w_qkv, w_out, cotangent):
@@ -724,6 +735,7 @@
         "rows": (4, 4, 96, 128),
         "lines": (4, 288, 256),
         "weight": (8192, 128),
+        "spread": (8192, 128),
         "part": (4, 4, 2, 96, 128),
         "all_part": (3, 4, 2, 96, 128),
     }
@@ -764,8 +776,9 @@
         scratch_shapes=[
             pltpu.VMEM((9, 864, 128), BF16),
             pltpu.VMEM((9, 288, 384), F32),
+            pltpu.VMEM((4, 2, 96, 128), BF16),
             pltpu.SemaphoreType.DMA((10,)),
-            pltpu.SemaphoreType.DMA((9,)),
+            pltpu.SemaphoreType.DMA((10,)),
         ],
         compiler_params=pltpu.CompilerParams(vmem_limit_bytes=VMEM_BYTES),
         name="widen",

time: 129 us -> 125 us (0.969)
  Pallas kernels: 126 us -> 122 us
    pallas_call x1, Pallas kernels: 7.24 us -> 3.24 us  [on_device(): pl.pallas_call(functools.partial(widen_kernel, cell_scale), out_shape=[ja...]
where the time goes in v12:
time: 125 us; the launch traced here: 123 us
  Pallas kernels  122 us (98%)
    pallas_call x1, Pallas kernels, fused(): pl.pallas_call(kernel, out_shape=[jax.ShapeDtypeStruct(s, t) for s, t, _...  119 us
    pallas_call x1, Pallas kernels, on_device(): pl.pallas_call(functools.partial(widen_kernel, cell_scale), out_shape=[ja...  3.24 us

profile of v12, /device:TPU:8, one launch (start us, length us, event | category | flops | bytes accessed | tf_op | source)
XLA Modules:
  0.0 122.8 jit_solution(17916335704071170916)
XLA Ops:
  0.6 118.7 %fused_0.1 = (bf16[4,2,96,128]{3,2,1,0:T(8,128)(2,1)}, bf16[8192,128]{1,0:T(8,128)(2,1)}) custom-call(bf16[4,2,96,128]{3,2,1,0:T(8,128)(2,1)} %refs_0_.1, bf16[4,2,96,128]{3,2,1,0:T(8,128)(2,1)} %refs_1_.1, bf16[27,96,384]{2,1,0:T(8,128)(2,1)} %refs_2_.1, bf16[1,96]{1,0:T(2,128)(2,1)} %bitcast.3, bf16[1,96]{1,0:T(2,128)(2,1)} %bitcast.4, ...), custom_call_target="tpu_custom_call" | custom-call | tf_op jit(solution)/shard_map/fused_0/pallas_call | solution.py:87
  119.4 3.2 %widen.1 = (f32[2592,384]{1,0:T(8,128)}, bf16[4,2,96,128]{3,2,1,0:T(8,128)(2,1)}) custom-call(bf16[8192,128]{1,0:T(8,128)(2,1)} %get-tuple-element.6.flat, bf16[4,2,96,128]{3,2,1,0:T(8,128)(2,1)} %get-tuple-element.7.grad), custom_call_target="tpu_custom_call" | custom-call | tf_op jit(solution)/shard_map/widen/pallas_call | solution.py:771

commit v13 on v12

--- a/solution.py
+++ b/solution.py
@@ -577,8 +577,8 @@
                     continue
                 acc += dot_t(m.moved[f, :, pl.ds(128 * (2 - h), 256)], act[:, pl.ds(256 * source, 256)])
             for lane in range(3):
-                at = (3 * (3 * t + h) + lane) * 288
-                weight[pl.ds(at, 288), :] = acc[:, 128 * lane : 128 * lane + 128].astype(BF16)
+                line = (3 * (3 * t + h) + lane) * 288
+                weight[pl.ds(line, 288), :] = acc[:, 128 * lane : 128 * lane + 128].astype(BF16)
         if t == 2:
             weight[pl.ds(27 * 288, 416), :] = jnp.zeros((416, 128), BF16)
         first.append(give(stripes[t], 0))
@@ -605,12 +605,18 @@
             for b in range(CH):
                 part[b, f, h] = total[96 * b : 96 * b + 96].astype(BF16)
     second, third, parts = [], [], []
+    parts.append(links.copy(part.at[at.sibling[1]], all_part.at[0], at.sibling))
+    joined = links.copy(part.at[(1 - at.y_lo) * 2 + 1 - at.core], m.assist, at.sibling)
+    for d in range(3):
+        parts.append(links.copy(inner, all_inner.at[d], chs[d]))
     for n, steps in enumerate(stripes):
         take(steps, 0, first[n])
         second.append(give(steps, 1))
-    for d in range(3):
-        parts.append(links.copy(part.at[chs[d][1]], all_part.at[d], chs[d]))
-        parts.append(links.copy(inner, all_inner.at[d], chs[d]))
+    joined.wait_recv()
+    for f in range(4):
+        both = part[at.c_near, f].astype(F32) + m.assist[f].astype(F32)
+        m.near_part[f] = both.astype(BF16)
+    parts.append(links.copy(m.near_part, all_part.at[1], at.near))
     for n, steps in enumerate(stripes):
         take(steps, 1, second[n])
         third.append(give(steps, 2))
@@ -640,7 +646,7 @@
             v = every[c, f, h].astype(F32)
             inv = inv_in[2 * f + h : 2 * f + h + 1, :]
             total = part[c, f, h].astype(F32)
-            for d in range(3):
+            for d in range(2):
                 total += all_part[d, f, h].astype(F32)
             before = v * inv * gain
             sig = sigmoid(before)
@@ -737,7 +743,9 @@
         "weight": (8192, 128),
         "spread": (8192, 128),
         "part": (4, 4, 2, 96, 128),
-        "all_part": (3, 4, 2, 96, 128),
+        "all_part": (2, 4, 2, 96, 128),
+        "assist": (4, 2, 96, 128),
+        "near_part": (4, 2, 96, 128),
     }
     for n, (size, counts) in enumerate(((2048, (2, 4, 4)), (3072, (4, 4, 2)), (3072, (4, 2, 4)))):
         for p, count in enumerate(counts):

time: 125 us -> 120 us (0.960)
  Pallas kernels: 122 us -> 118 us
    pallas_call x1, Pallas kernels: 119 us -> 115 us  [fused(): pl.pallas_call(kernel, out_shape=[jax.ShapeDtypeStruct(s, t) for s, t, _...]
where the time goes in v13:
time: 120 us; the launch traced here: 119 us
  Pallas kernels  118 us (98%)
    pallas_call x1, Pallas kernels, fused(): pl.pallas_call(kernel, out_shape=[jax.ShapeDtypeStruct(s, t) for s, t, _...  115 us
    pallas_call x1, Pallas kernels, on_device(): pl.pallas_call(functools.partial(widen_kernel, cell_scale), out_shape=[ja...  3.24 us

profile of v13, /device:TPU:8, one launch (start us, length us, event | category | flops | bytes accessed | tf_op | source)
XLA Modules:
  0.0 118.7 jit_solution(7183572881232775020)
XLA Ops:
  0.6 114.6 %fused_0.1 = (bf16[4,2,96,128]{3,2,1,0:T(8,128)(2,1)}, bf16[8192,128]{1,0:T(8,128)(2,1)}) custom-call(bf16[4,2,96,128]{3,2,1,0:T(8,128)(2,1)} %refs_0_.1, bf16[4,2,96,128]{3,2,1,0:T(8,128)(2,1)} %refs_1_.1, bf16[27,96,384]{2,1,0:T(8,128)(2,1)} %refs_2_.1, bf16[1,96]{1,0:T(2,128)(2,1)} %bitcast.3, bf16[1,96]{1,0:T(2,128)(2,1)} %bitcast.4, ...), custom_call_target="tpu_custom_call" | custom-call | tf_op jit(solution)/shard_map/fused_0/pallas_call | solution.py:87
  115.2 3.2 %widen.1 = (f32[2592,384]{1,0:T(8,128)}, bf16[4,2,96,128]{3,2,1,0:T(8,128)(2,1)}) custom-call(bf16[8192,128]{1,0:T(8,128)(2,1)} %get-tuple-element.6.flat, bf16[4,2,96,128]{3,2,1,0:T(8,128)(2,1)} %get-tuple-element.7.grad), custom_call_target="tpu_custom_call" | custom-call | tf_op jit(solution)/shard_map/widen/pallas_call | solution.py:779

commit v14 on v13

--- a/solution.py
+++ b/solution.py
@@ -170,6 +170,18 @@
         there = [(i, b) for i in near_rows(at.row) for b in range(CH)]
         whose = [owner(f, i) for i in (at.low, at.high) for f in range(4)]
         greet_frames(at.me, at.targets + at.sources + whose + alike, at.targets + at.sources + there + alike)
+
+
+def relay_ring(links, sibling, first, ref, base, i, rows, peers, forward):
+    on = []
+    for side in range(2):
+        first[side].wait_recv()
+        came = base + lax.rem(i + 3 - 2 * side, 4)
+        part = ref.at[came, pl.ds(rows * side, rows)]
+        on.append(links.copy(part, part, peers[2 * side]))
+        if forward:
+            on.append(links.copy(ref.at[came], ref.at[came], sibling))
+    return on
 
 
 def front(links, at, m):
@@ -194,6 +206,9 @@
     gains = [links.copy(m.gain_rows.at[c], m.gain_rows.at[c], to) for to in at.chs]
     to_near = [links.copy(m.feat.at[two], every.at[c, two], near) for two in pairs]
     to_sib = links.copy(m.feat, every.at[c], sibling)
+    for f in range(4):
+        own = same(at.targets[f], at.me)
+        links.copy(m.cot.at[f], m.cot_frame.at[c], at.targets[f], own=own, recv=COT + c)
     for copy in gains:
         copy.wait_recv()
     gain = gain_columns(m.gain_rows, 0)
@@ -202,9 +217,6 @@
         to_near[p].wait_recv()
         part = every.at[at.c_near, two]
         passed.append(links.copy(part, part, sibling))
-    for f in range(4):
-        own = same(at.targets[f], at.me)
-        links.copy(m.cot.at[f], m.cot_frame.at[c], at.targets[f], own=own, recv=COT + c)
 
     def activate(n):
         v = jnp.concatenate([every[b, n // 2, lax.rem(n, 2)] for b in range(CH)], 0).astype(F32)
@@ -213,6 +225,15 @@
         m.inv_in[pl.ds(n, 1), :] = inv
         act[:, pl.ds(pl.multiple_of(128 * n, 128), 128)] = (before * sigmoid(before)).astype(BF16)
 
+    for b in range(CH):
+        links.arrive(m.cot_frame.at[b], COT + b)
+    for b in range(CH):
+        for h in range(2):
+            m.cot_full[pl.ds(96 * b, 96), pl.ds(128 * h, 128)] = m.cot_frame[b, h]
+    for copy in projections:
+        copy.wait()
+    m.g[at.slot] = dot(m.w_out[...], m.cot_full[...]).astype(BF16)
+    at.g_first = [links.copy(m.g.at[at.slot], m.g.at[at.slot], to) for to in (at.xs[0], at.xs[2], sibling)]
     here.wait()
     to_sib.wait_recv()
     weights.wait()
@@ -248,15 +269,7 @@
             m.conv_own[f, 1] = lines[2]
         edges.append(links.copy(m.edge_out.at[0, two], m.edge_in.at[0, two], (at.low, c)))
         edges.append(links.copy(m.edge_out.at[1, two], m.edge_in.at[1, two], (at.high, c)))
-    for b in range(CH):
-        links.arrive(m.cot_frame.at[b], COT + b)
-    for b in range(CH):
-        for h in range(2):
-            m.cot_full[pl.ds(96 * b, 96), pl.ds(128 * h, 128)] = m.cot_frame[b, h]
-    for copy in projections:
-        copy.wait()
-    m.g[at.slot] = dot(m.w_out[...], m.cot_full[...]).astype(BF16)
-    at.g_first = [links.copy(m.g.at[at.slot], m.g.at[at.slot], to) for to in (at.xs[0], at.xs[2], sibling)]
+    at.g_on = relay_ring(links, sibling, at.g_first, m.g, at.core * 4, at.x, 192, at.xs, True)
     for p in range(2):
         edges[2 * p].wait_recv()
         edges[2 * p + 1].wait_recv()
@@ -275,18 +288,7 @@
     q, g, k, v, k_t = m.q, m.g, m.k, m.v, m.k_t
     w_qkv = m.w_qkv
 
-    def relay_ring(first, ref, base, i, rows, peers, forward):
-        on = []
-        for side in range(2):
-            first[side].wait_recv()
-            came = base + lax.rem(i + 3 - 2 * side, 4)
-            part = ref.at[came, pl.ds(rows * side, rows)]
-            on.append(links.copy(part, part, peers[2 * side]))
-            if forward:
-                on.append(links.copy(ref.at[came], ref.at[came], sibling))
-        return on
-
-    g_on = relay_ring(at.g_first, g, core * 4, x, 192, at.xs, True)
+    g_on = at.g_on
     gain = gain_columns(m.gain_rows, 1)
     gain = jnp.concatenate([gain, gain], 1)
     for b in range(CH):
@@ -343,8 +345,8 @@
         for n in range(3):
             piece = jnp.concatenate([m.w[9 * t + 3 * h + n] for h in range(3)], 0)
             m.w_t[t, pl.ds(384 * n, 384), :] = piece.T
-    n_on = relay_ring(n_first, m.norm, 0, z, 128, at.zs, False)
-    q_on = relay_ring(q_first, q, core * 4, x, 192, at.xs, True)
+    n_on = relay_ring(links, sibling, n_first, m.norm, 0, z, 128, at.zs, False)
+    q_on = relay_ring(links, sibling, q_first, q, core * 4, x, 192, at.xs, True)
     g_on[0].wait_recv()
     g_on[2].wait_recv()
     g_last = links.copy(g.at[far_x], g.at[far_x], sibling)

time: 120 us -> 124 us (1.033)
  Pallas kernels: 118 us -> 122 us
    pallas_call x1, Pallas kernels: 115 us -> 118 us  [fused(): pl.pallas_call(kernel, out_shape=[jax.ShapeDtypeStruct(s, t) for s, t, _...]
where the time goes in v14:
time: 124 us; the launch traced here: 123 us
  Pallas kernels  122 us (98%)
    pallas_call x1, Pallas kernels, fused(): pl.pallas_call(kernel, out_shape=[jax.ShapeDtypeStruct(s, t) for s, t, _...  118 us
    pallas_call x1, Pallas kernels, on_device(): pl.pallas_call(functools.partial(widen_kernel, cell_scale), out_shape=[ja...  3.24 us

profile of v14, /device:TPU:8, one launch (start us, length us, event | category | flops | bytes accessed | tf_op | source)
XLA Modules:
  0.0 122.6 jit_solution(17670907864998972651)
XLA Ops:
  0.6 118.5 %fused_0.1 = (bf16[4,2,96,128]{3,2,1,0:T(8,128)(2,1)}, bf16[8192,128]{1,0:T(8,128)(2,1)}) custom-call(bf16[4,2,96,128]{3,2,1,0:T(8,128)(2,1)} %refs_0_.1, bf16[4,2,96,128]{3,2,1,0:T(8,128)(2,1)} %refs_1_.1, bf16[27,96,384]{2,1,0:T(8,128)(2,1)} %refs_2_.1, bf16[1,96]{1,0:T(2,128)(2,1)} %bitcast.3, bf16[1,96]{1,0:T(2,128)(2,1)} %bitcast.4, ...), custom_call_target="tpu_custom_call" | custom-call | tf_op jit(solution)/shard_map/fused_0/pallas_call | solution.py:87
  119.1 3.2 %widen.1 = (f32[2592,384]{1,0:T(8,128)}, bf16[4,2,96,128]{3,2,1,0:T(8,128)(2,1)}) custom-call(bf16[8192,128]{1,0:T(8,128)(2,1)} %get-tuple-element.6.flat, bf16[4,2,96,128]{3,2,1,0:T(8,128)(2,1)} %get-tuple-element.7.grad), custom_call_target="tpu_custom_call" | custom-call | tf_op jit(solution)/shard_map/widen/pallas_call | solution.py:781

commit v15 on v13

--- a/solution.py
+++ b/solution.py
@@ -612,14 +612,14 @@
     for n, steps in enumerate(stripes):
         take(steps, 0, first[n])
         second.append(give(steps, 1))
+    for n, steps in enumerate(stripes):
+        take(steps, 1, second[n])
+        third.append(give(steps, 2))
     joined.wait_recv()
     for f in range(4):
         both = part[at.c_near, f].astype(F32) + m.assist[f].astype(F32)
         m.near_part[f] = both.astype(BF16)
     parts.append(links.copy(m.near_part, all_part.at[1], at.near))
-    for n, steps in enumerate(stripes):
-        take(steps, 1, second[n])
-        third.append(give(steps, 2))
     spread, kept = [], []
     for n, steps in enumerate(stripes):
         take(steps, 2, third[n])

time: 120 us -> 119 us (level)
    pallas_call x1, Pallas kernels: 115 us -> 113 us  [fused(): pl.pallas_call(kernel, out_shape=[jax.ShapeDtypeStruct(s, t) for s, t, _...]
where the time goes in v15:
time: 119 us; the launch traced here: 117 us
  Pallas kernels  117 us (98%)
    pallas_call x1, Pallas kernels, fused(): pl.pallas_call(kernel, out_shape=[jax.ShapeDtypeStruct(s, t) for s, t, _...  113 us
    pallas_call x1, Pallas kernels, on_device(): pl.pallas_call(functools.partial(widen_kernel, cell_scale), out_shape=[ja...  3.24 us

profile of v15, /device:TPU:8, one launch (start us, length us, event | category | flops | bytes accessed | tf_op | source)
XLA Modules:
  0.0 117.4 jit_solution(16843888931304760756)
XLA Ops:
  0.6 113.3 %fused_0.1 = (bf16[4,2,96,128]{3,2,1,0:T(8,128)(2,1)}, bf16[8192,128]{1,0:T(8,128)(2,1)}) custom-call(bf16[4,2,96,128]{3,2,1,0:T(8,128)(2,1)} %refs_0_.1, bf16[4,2,96,128]{3,2,1,0:T(8,128)(2,1)} %refs_1_.1, bf16[27,96,384]{2,1,0:T(8,128)(2,1)} %refs_2_.1, bf16[1,96]{1,0:T(2,128)(2,1)} %bitcast.3, bf16[1,96]{1,0:T(2,128)(2,1)} %bitcast.4, ...), custom_call_target="tpu_custom_call" | custom-call | tf_op jit(solution)/shard_map/fused_0/pallas_call | solution.py:87
  114.0 3.2 %widen.1 = (f32[2592,384]{1,0:T(8,128)}, bf16[4,2,96,128]{3,2,1,0:T(8,128)(2,1)}) custom-call(bf16[8192,128]{1,0:T(8,128)(2,1)} %get-tuple-element.6.flat, bf16[4,2,96,128]{3,2,1,0:T(8,128)(2,1)} %get-tuple-element.7.grad), custom_call_target="tpu_custom_call" | custom-call | tf_op jit(solution)/shard_map/widen/pallas_call | solution.py:779
